TPU v7x, 32 devices: a whole 2x2x4 slice. The times are simulated.
32 devices in a mesh: seq: 16 (over z, x, core), chan: 2 (over y).
Axes of the slice: x: 2, y: 2, z: 4, core: 2. Of those that a mesh axis runs over, the one named last changes fastest.
Arguments:
- grad_out: bfloat16 [2048, 4096], P('seq', 'chan'), may hold values from -6 to 6
- out_weight: bfloat16 [4096, 4096], P('seq', 'chan'), may hold values from -0.09375 to 0.09375
- gate_stream: bfloat16 [4096, 2048], P('chan', 'seq'), may hold values from -6 to 6
- conv_output: bfloat16 [4096, 2048], P('chan', 'seq'), may hold values from -6 to 6
- key_stream: bfloat16 [4096, 2048], P('chan', 'seq'), may hold values from -6 to 6
- value_stream: bfloat16 [4096, 2048], P('chan', 'seq'), may hold values from -6 to 6
- long_filter: bfloat16 [4096, 2048], P(('chan', 'seq')), may hold values from 0 to 1
Outputs:
- grad_gate: bfloat16 [4096, 2048], P('chan', 'seq')
- grad_key: bfloat16 [4096, 2048], P('chan', 'seq')
- grad_value: bfloat16 [4096, 2048], P('chan', 'seq')
All inputs are finite; a program needn't handle non-finite values.
Results may differ from a plain program's by a relative error of at most 0.007.
Values may be sent and summed in bfloat16 or wider, within the bound.
No kernel may reach another device: no remote copies, remote signals or barrier semaphores. Data moves between devices by JAX's collectives and lax.ppermute only.
A program may use at most 64 MiB of HBM per device.

v0:
```python
import math

import jax
import jax.numpy as jnp
from jax import lax
from jax.sharding import PartitionSpec as P


def dft_tables(count_outer, count_inner):
    total_len = count_outer * count_inner
    index_outer = jnp.arange(count_outer, dtype=jnp.int32)
    index_inner = jnp.arange(count_inner, dtype=jnp.int32)
    angle_outer = (index_outer[:, None] * index_outer[None, :] % count_outer).astype(
        jnp.float32
    ) * (2.0 * math.pi / count_outer)
    angle_inner = (index_inner[:, None] * index_inner[None, :] % count_inner).astype(
        jnp.float32
    ) * (2.0 * math.pi / count_inner)
    angle_twist = (index_outer[:, None] * index_inner[None, :] % total_len).astype(jnp.float32) * (
        2.0 * math.pi / total_len
    )
    return (
        jnp.cos(angle_outer),
        -jnp.sin(angle_outer),
        jnp.cos(angle_inner),
        -jnp.sin(angle_inner),
        jnp.cos(angle_twist),
        -jnp.sin(angle_twist),
    )


def outer_exact(table, signal):
    table_high = table.astype(jnp.bfloat16)
    table_low = (table - table_high.astype(jnp.float32)).astype(jnp.bfloat16)
    first = jnp.einsum("ab,cbk->cak", table_high, signal, preferred_element_type=jnp.float32)
    return first + jnp.einsum("ab,cbk->cak", table_low, signal, preferred_element_type=jnp.float32)


def outer_wide(table, values):
    return jnp.einsum(
        "ab,cbk->cak",
        table,
        values,
        precision=lax.Precision.HIGH,
        preferred_element_type=jnp.float32,
    )


def inner_wide(values, table):
    return jnp.einsum(
        "cak,kl->cal",
        values,
        table,
        precision=lax.Precision.HIGH,
        preferred_element_type=jnp.float32,
    )


def spectral_forward(signal, tables):
    outer_cos, outer_sin, inner_cos, inner_sin, twist_cos, twist_sin = tables
    part_re = outer_exact(outer_cos, signal)
    part_im = outer_exact(outer_sin, signal)
    turned_re = part_re * twist_cos - part_im * twist_sin
    turned_im = part_re * twist_sin + part_im * twist_cos
    spec_re = inner_wide(turned_re, inner_cos) - inner_wide(turned_im, inner_sin)
    spec_im = inner_wide(turned_re, inner_sin) + inner_wide(turned_im, inner_cos)
    return (spec_re, spec_im)


def spectral_inverse_real(spec_re, spec_im, tables):
    outer_cos, outer_sin, inner_cos, inner_sin, twist_cos, twist_sin = tables
    back_re = inner_wide(spec_re, inner_cos) + inner_wide(spec_im, inner_sin)
    back_im = inner_wide(spec_im, inner_cos) - inner_wide(spec_re, inner_sin)
    turned_re = back_re * twist_cos + back_im * twist_sin
    turned_im = back_im * twist_cos - back_re * twist_sin
    total_len = spec_re.shape[1] * spec_re.shape[2]
    return (outer_wide(outer_cos, turned_re) + outer_wide(outer_sin, turned_im)) / total_len


def correlate(gathered, filters, tables):
    channel_count, seq_len = gathered.shape
    count_outer = tables[0].shape[0]
    count_inner = tables[2].shape[0]
    padding = jnp.zeros((2 * channel_count, seq_len), jnp.bfloat16)
    stacked = jnp.concatenate([gathered, filters], axis=0)
    padded = jnp.concatenate([stacked, padding], axis=1).reshape(
        2 * channel_count, count_outer, count_inner
    )
    both_re, both_im = spectral_forward(padded, tables)
    signal_re, kernel_re = (both_re[:channel_count], both_re[channel_count:])
    signal_im, kernel_im = (both_im[:channel_count], both_im[channel_count:])
    joined_re = kernel_re * signal_re + kernel_im * signal_im
    joined_im = kernel_re * signal_im - kernel_im * signal_re
    result = spectral_inverse_real(joined_re, joined_im, tables)
    return result.reshape(channel_count, -1)[:, :seq_len].astype(jnp.bfloat16)


def per_device(
    grad_out, out_weight, gate_stream, conv_output, key_stream, value_stream, long_filter
):
    seq_count = lax.axis_size("seq")
    token_count = grad_out.shape[0]
    chan_width = out_weight.shape[1]
    group_width = chan_width // seq_count
    full_grad = lax.all_gather(grad_out, "chan", axis=1, tiled=True)
    tables = dft_tables(2 * seq_count, token_count)
    grad_mix = jnp.einsum(
        "nc,tn->ct",
        lax.all_gather(out_weight, "seq", axis=0, tiled=True),
        full_grad,
        preferred_element_type=jnp.float32,
    )
    gated_grad = (grad_mix * gate_stream.astype(jnp.float32)).astype(jnp.bfloat16)
    regrouped = lax.all_to_all(
        gated_grad.reshape(seq_count, group_width, token_count),
        "seq",
        split_axis=0,
        concat_axis=2,
        tiled=True,
    )
    inner_grad = correlate(regrouped[0], long_filter, tables)
    returned = lax.all_to_all(inner_grad[None], "seq", split_axis=2, concat_axis=0, tiled=True)
    grad_inner = returned.reshape(chan_width, token_count)
    grad_gate = (grad_mix * conv_output.astype(jnp.float32)).astype(jnp.bfloat16)
    inner_grad_wide = grad_inner.astype(jnp.float32)
    grad_key = (inner_grad_wide * value_stream.astype(jnp.float32)).astype(jnp.bfloat16)
    grad_value = (inner_grad_wide * key_stream.astype(jnp.float32)).astype(jnp.bfloat16)
    return (grad_gate, grad_key, grad_value)


def solution(mesh):
    in_specs = (
        P("seq", "chan"),
        P("seq", "chan"),
        P("chan", "seq"),
        P("chan", "seq"),
        P("chan", "seq"),
        P("chan", "seq"),
        P(("chan", "seq"), None),
    )
    out_specs = (P("chan", "seq"), P("chan", "seq"), P("chan", "seq"))
    return jax.shard_map(
        per_device, mesh=mesh, in_specs=in_specs, out_specs=out_specs, check_vma=False
    )
```

profile of v0, /device:TPU:0, one launch (start us, length us, event | category | flops | bytes accessed | tf_op | source)
XLA Modules:
  0.0 268.2 jit_solution(14423629071565825038)
XLA Ops:
  8.6 24.9 %all-gather.5.cloned.1.call-done = bf16[128,4096]{1,0:T(8,128)(2,1)} async-done(((bf16[128,2048]{1,0:T(8,128)(2,1)}), bf16[128,4096]{1,0:T(8,128)(2,1)}) %all-gather.5.cloned.1.call-update) | async-done | bytes 1048592 | tf_op jit(solution)/shard_map/all_gather | solution.py:105
  33.6 129.1 %all-gather.3.cloned.1.call-done = bf16[4096,2048]{1,0:T(8,128)(2,1)} async-done(((bf16[256,2048]{1,0:T(8,128)(2,1)}), bf16[4096,2048]{1,0:T(8,128)(2,1)}) %all-gather.3.cloned.1.call-update) | async-done | bytes 16777232 | tf_op jit(solution)/shard_map/all_gather | solution.py:109
  162.7 11.9 %multiply_convert_fusion.1 = (bf16[2048,128]{1,0:T(8,128)(2,1)}, bf16[2048,128]{1,0:T(8,128)(2,1)}) fusion(bf16[2048,128]{1,0:T(8,128)(2,1)} %param.9, bf16[2048,128]{1,0:T(8,128)(2,1)} %param.10, bf16[4096,2048]{1,0:T(8,128)(2,1)} %all-gather.3.cloned.1.call-done, bf16[128,4096]{1,0:T(8,128)(2,1)} %all-gather.5.cloned.1.call-done), kind=kOutput, calls=%fused_computation.39 | convolution fusion | flops 2149056512 | bytes 19922944 | tf_op jit(solution)/shard_map/nc,tn->ct/dot_general | solution.py:107
  174.6 3.9 %all-to-all-start = ((bf16[16,128,128]{2,1,0:T(8,128)(2,1)}), bf16[16,128,128]{2,1,0:T(8,128)(2,1)S(1)}, u32[]{:S(2)}, u32[]{:S(2)}) async-start(bf16[16,128,128]{2,1,0:T(8,128)(2,1)} %bitcast), calls=%async_computation | async-start | bytes 1048576 | tf_op jit(solution)/shard_map/all_to_all | solution.py:114
  178.6 14.2 %all-to-all-done = bf16[16,128,128]{2,1,0:T(8,128)(2,1)S(1)} async-done(((bf16[16,128,128]{2,1,0:T(8,128)(2,1)}), bf16[16,128,128]{2,1,0:T(8,128)(2,1)S(1)}, u32[]{:S(2)}, u32[]{:S(2)}) %all-to-all-start) | async-done | bytes 524320 | tf_op jit(solution)/shard_map/all_to_all | solution.py:114
  194.1 0.8 fusion.75
  194.8 0.8 fusion.69
  195.6 0.8 convolution_add_fusion.1
  196.4 1.5 fusion.2
  197.9 4.2 %fusion.6 = f32[256,32,128]{2,0,1:T(8,128)S(1)} fusion(f32[256,32,128]{2,1,0:T(8,128)S(1)} %get-tuple-element.4), kind=kOutput, calls=%fused_computation.11 | convolution fusion | flops 805552128 | bytes 8388608 | tf_op jit(solution)/shard_map/cak,kl->cal/dot_general | solution.py:50
  202.1 4.4 %fusion.4 = f32[256,32,128]{2,0,1:T(8,128)S(1)} fusion(f32[256,32,128]{2,1,0:T(8,128)S(1)} %get-tuple-element.4), kind=kOutput, calls=%fused_computation.9 | convolution fusion | flops 805535744 | bytes 8388608 | tf_op jit(solution)/shard_map/cak,kl->cal/dot_general | solution.py:50
  206.5 4.2 %fusion.12 = f32[256,32,128]{2,0,1:T(8,128)S(1)} fusion(f32[256,32,128]{2,0,1:T(8,128)S(1)} %fusion.6, f32[256,32,128]{2,1,0:T(8,128)S(1)} %get-tuple-element.3), kind=kOutput, calls=%fused_computation.17 | convolution fusion | flops 806584320 | bytes 12582912 | tf_op jit(solution)/shard_map/cak,kl->cal/dot_general | solution.py:50
  210.7 4.3 %fusion.15 = f32[256,32,128]{2,0,1:T(8,128)S(1)} fusion(f32[256,32,128]{2,0,1:T(8,128)S(1)} %fusion.4, f32[256,32,128]{2,1,0:T(8,128)S(1)} %get-tuple-element.3), kind=kOutput, calls=%fused_computation.18 | convolution fusion | flops 806600704 | bytes 12582912 | tf_op jit(solution)/shard_map/cak,kl->cal/dot_general | solution.py:50
  215.0 0.9 multiply_subtract_fusion.1
  215.9 1.2 fusion.37
  217.1 1.6 fusion.35
  218.8 1.2 convolution_add_fusion.2
  220.0 1.5 multiply_add_fusion
  221.5 2.1 fusion.20
  223.7 2.3 multiply_convert_fusion
  227.8 11.7 %reduce = bf16[2048,128]{1,0:T(8,128)(2,1)S(1)} reduce(bf16[2048,1,128]{2,1,0:T(2,128)(2,1)S(1)} %bitcast.101, bf16[]{:T(256)} %broadcast.144), dimensions={1}, to_apply=%bitcast.77.reduce_sub_computation | reduce | bytes 1048578
  239.6 18.3 %all_to_all.24 = bf16[16,2,8192]{2,1,0:T(2,128)(2,1)S(1)} all-to-all(bf16[16,2,8192]{2,1,0:T(2,128)(2,1)S(1)} %reshape.73), channel_id=1, replica_groups=mesh['seq'=16,'chan'=2] {'seq'}, dimensions={0} | all-to-all | bytes 1048576 | tf_op jit(solution)/shard_map/all_to_all | solution.py:122
  258.5 1.1 bitcast_convert_fusion
  260.0 1.2 fusion.27
  (22 shorter events, 5.6 us)
Async XLA Ops:
  7.2 26.4 %all-gather.5.cloned.1.call-start = ((), (), s32[]{:S(2)}) async-start(), calls=%async_computation.3 | async-start | bytes 1572864 | tf_op jit(solution)/shard_map/all_gather | solution.py:105
  7.9 154.8 %all-gather.3.cloned.1.call-start = ((), (), s32[]{:S(2)}) async-start(), calls=%async_computation.2 | async-start | bytes 17825792 | tf_op jit(solution)/shard_map/all_gather | solution.py:109
  174.6 18.6 %copy-start = (bf16[128,2048]{1,0:T(8,128)(2,1)S(1)}, bf16[128,2048]{1,0:T(8,128)(2,1)}, u32[]{:S(2)}) copy-start(bf16[128,2048]{1,0:T(8,128)(2,1)} %param.13) | copy-start | bytes 1572868
  174.6 18.1 %all-to-all-start = ((bf16[16,128,128]{2,1,0:T(8,128)(2,1)}), bf16[16,128,128]{2,1,0:T(8,128)(2,1)S(1)}, u32[]{:S(2)}, u32[]{:S(2)}) async-start(bf16[16,128,128]{2,1,0:T(8,128)(2,1)} %bitcast), calls=%async_computation | async-start | bytes 1048576 | tf_op jit(solution)/shard_map/all_to_all | solution.py:114
  258.5 1.5 copy-start.1
  258.5 1.5 copy-start.2
Sparse Core Ops, SparseCore 0:
  9.5 23.9 all-gather.4
  35.7 126.8 all-gather.2
where the time goes:
time: 273 us; the launch traced here: 268 us
  waiting for transfers between devices  170 us (62%)
  matrix products  42.9 us (16%)
  blocking collectives  18.3 us (7%)
  other arithmetic  15.3 us (6%)
  between operations  14.5 us (5%)
  starting transfers between devices  3.95 us (1%)
  local copies, waits for them, and re-layouts  3.71 us (1%)
    all_gather x1, waiting for transfers between devices, per_device(): lax.all_gather(out_weight, 'seq', axis=0, tiled=True)  129 us
    all_gather x1, waiting for transfers between devices, per_device(): full_grad = lax.all_gather(grad_out, 'chan', axis=1, tiled=True)  24.9 us
    dot_general x8, matrix products, inner_wide(): jnp.einsum('cak,kl->cal', values, table, precision=lax.Precision.HIGH, pr...  22.7 us
    all_to_all x1, blocking collectives, per_device(): lax.all_to_all(inner_grad[None], 'seq', split_axis=2, concat_axis=0, tile...  18.3 us
    all_to_all x1, waiting for transfers between devices, per_device(): lax.all_to_all(gated_grad.reshape(seq_count, group_width, token_count), '...  14.2 us
    unnamed x2, other arithmetic  12.1 us
    dot_general x1, matrix products, per_device(): jnp.einsum('nc,tn->ct', lax.all_gather(out_weight, 'seq', axis=0, tiled=T...  11.9 us
  transfers between devices with their start and end apart: 3, of which 3 were waited for; matrix products, arithmetic and copies ran while one was open for 0% of the time, Pallas kernels for 0%

commit v1 on v0

--- a/solution.py
+++ b/solution.py
@@ -1,9 +1,244 @@
+import functools
 import math
 
 import jax
 import jax.numpy as jnp
+import numpy as np
 from jax import lax
+from jax.experimental import pallas as pl
+from jax.experimental.pallas import tpu as pltpu
 from jax.sharding import PartitionSpec as P
+
+VMEM_BYTES = 48 * 1024 * 1024
+
+
+def split_table(table):
+    high = table.astype(jnp.bfloat16)
+    low = (table.astype(np.float32) - high.astype(np.float32)).astype(jnp.bfloat16)
+    return high, low
+
+
+def dft_constants(blocks, width):
+    outer = 2 * blocks
+    lines = blocks + 1
+    lane = np.arange(width)
+    twist = 2.0 * np.pi * (np.arange(lines)[:, None] * lane[None, :] % (outer * width)) / (outer * width)
+    inner = 2.0 * np.pi * (lane[:, None] * lane[None, :] % width) / width
+    cos, sin = np.cos(inner), np.sin(inner)
+    forward = np.block([[cos, -sin], [sin, cos]]).astype(np.float32)
+    backward = np.block([[cos, sin], [-sin, cos]]).astype(np.float32)
+    twist = np.stack([np.cos(twist), np.sin(twist)]).astype(np.float32)
+    return twist, split_table(forward), split_table(backward)
+
+
+def scaled_sum(terms):
+    total = None
+    for scale, value in terms:
+        if abs(scale) < 1e-12:
+            continue
+        if abs(scale - 1.0) < 1e-12:
+            term = value
+        elif abs(scale + 1.0) < 1e-12:
+            term = -value
+        else:
+            term = value * np.float32(scale)
+        total = term if total is None else total + term
+    return total
+
+
+def real_lines(parts, period):
+    count = len(parts)
+    half = period // 2
+    if half % 2 or count < 2:
+        cosines, sines = [], []
+        for k in range(half + 1):
+            angle = [2.0 * math.pi * (i * k % period) / period for i in range(count)]
+            cosines.append(scaled_sum([(math.cos(a), p) for a, p in zip(angle, parts)]))
+            sines.append(scaled_sum([(math.sin(a), p) for a, p in zip(angle, parts)]))
+        return cosines, sines
+    even_cos, even_sin = real_lines(parts[0::2], half)
+    quarter = half // 2
+    cosines, sines = [None] * (half + 1), [None] * (half + 1)
+    odd = parts[1::2]
+    for k in range(quarter + 1):
+        angle = [2.0 * math.pi * ((2 * m + 1) * k % period) / period for m in range(len(odd))]
+        odd_cos = scaled_sum([(math.cos(a), p) for a, p in zip(angle, odd)])
+        odd_sin = scaled_sum([(math.sin(a), p) for a, p in zip(angle, odd)])
+        cosines[k] = add(even_cos[k], odd_cos)
+        sines[k] = add(even_sin[k], odd_sin)
+        if k != half - k:
+            cosines[half - k] = subtract(even_cos[k], odd_cos)
+            sines[half - k] = subtract(odd_sin, even_sin[k])
+    return cosines, sines
+
+
+def add(a, b):
+    if a is None or b is None:
+        return b if a is None else a
+    return a + b
+
+
+def subtract(a, b):
+    if b is None:
+        return a
+    return -b if a is None else a - b
+
+
+def real_parts(re, im, period, count):
+    half = period // 2
+    if half % 2 or count < 2:
+        out = []
+        for i in range(count):
+            angle = [2.0 * math.pi * (i * k % period) / period for k in range(half + 1)]
+            terms = [(math.cos(a), r) for a, r in zip(angle, re) if r is not None]
+            terms += [(-math.sin(a), m) for a, m in zip(angle, im) if m is not None]
+            out.append(scaled_sum(terms))
+        return out
+    quarter = half // 2
+    sum_re, sum_im, gap_re, gap_im = [], [], [], []
+    for k in range(quarter + 1):
+        if k == half - k:
+            sum_re.append(re[k]); sum_im.append(None)
+            gap_re.append(None); gap_im.append(im[k])
+        else:
+            sum_re.append(add(re[k], re[half - k])); sum_im.append(subtract(im[k], im[half - k]))
+            gap_re.append(subtract(re[k], re[half - k])); gap_im.append(add(im[k], im[half - k]))
+    out = [None] * count
+    out[0::2] = real_parts(sum_re, sum_im, half, (count + 1) // 2)
+    for i in range(1, count, 2):
+        angle = [2.0 * math.pi * (i * k % period) / period for k in range(quarter + 1)]
+        terms = [(math.cos(a), r) for a, r in zip(angle, gap_re) if r is not None]
+        terms += [(-math.sin(a), m) for a, m in zip(angle, gap_im) if m is not None]
+        out[i] = scaled_sum(terms)
+    return out
+
+
+def put_split(pair_ref, row, rows, re, im):
+    width = re.shape[-1]
+    for at, value in ((0, re), (1, im)):
+        high = value.astype(jnp.bfloat16)
+        low = (value - high.astype(jnp.float32)).astype(jnp.bfloat16)
+        pair_ref[row : row + rows, at * width : (at + 1) * width] = high
+        pair_ref[row : row + rows, (2 + at) * width : (3 + at) * width] = low
+
+
+def wide_dot(pair, high, low):
+    depth = high.shape[0]
+    return (
+        jnp.dot(pair[:, :depth], high, preferred_element_type=jnp.float32)
+        + jnp.dot(pair[:, depth:], high, preferred_element_type=jnp.float32)
+        + jnp.dot(pair[:, :depth], low, preferred_element_type=jnp.float32)
+    )
+
+
+def to_spectrum(read, twist_ref, high_ref, low_ref, pair_ref, out_ref, blocks, channels, rows):
+    width = twist_ref.shape[2]
+    for at in range(0, channels, rows):
+        parts = [read(i, at).astype(jnp.float32) for i in range(blocks)]
+        cosines, sines = real_lines(parts, 2 * blocks)
+        for k in range(blocks + 1):
+            turn_cos, turn_sin = twist_ref[0, k : k + 1, :], twist_ref[1, k : k + 1, :]
+            re, im = cosines[k], sines[k]
+            if im is None:
+                new_re, new_im = re * turn_cos, -(re * turn_sin)
+            else:
+                new_re, new_im = re * turn_cos - im * turn_sin, -(re * turn_sin + im * turn_cos)
+            put_split(pair_ref, k * channels + at, rows, new_re, new_im)
+    out_ref[...] = wide_dot(pair_ref[...], high_ref[...], low_ref[...])
+
+
+def filter_kernel(blocks, rows, taps_ref, twist_ref, high_ref, low_ref, out_ref, pair_ref, spec_ref):
+    channels = taps_ref.shape[0]
+    width = twist_ref.shape[2]
+    to_spectrum(
+        lambda i, at: taps_ref[at : at + rows, i * width : (i + 1) * width],
+        twist_ref, high_ref, low_ref, pair_ref, spec_ref, blocks, channels, rows,
+    )
+    total = 2 * blocks * width
+    for k in range(blocks + 1):
+        scale = (1.0 if k in (0, blocks) else 2.0) / total
+        out_ref[k] = spec_ref[k * channels : (k + 1) * channels, :] * np.float32(scale)
+
+
+def filter_spectrum(taps, blocks, step):
+    channels, length = taps.shape
+    width = length // blocks
+    twist, forward, _ = dft_constants(blocks, width)
+    lines = blocks + 1
+    whole = lambda *shape: pl.BlockSpec(shape, lambda c: (0,) * len(shape))
+    return pl.pallas_call(
+        functools.partial(filter_kernel, blocks, min(16, step)),
+        grid=(channels // step,),
+        in_specs=[
+            pl.BlockSpec((step, length), lambda c: (c, 0)),
+            whole(2, lines, width), whole(2 * width, 2 * width), whole(2 * width, 2 * width),
+        ],
+        out_specs=pl.BlockSpec((lines, step, 2 * width), lambda c: (0, c, 0)),
+        out_shape=jax.ShapeDtypeStruct((lines, channels, 2 * width), jnp.float32),
+        scratch_shapes=[
+            pltpu.VMEM((lines * step, 4 * width), jnp.bfloat16),
+            pltpu.VMEM((lines * step, 2 * width), jnp.float32),
+        ],
+        compiler_params=pltpu.CompilerParams(vmem_limit_bytes=VMEM_BYTES),
+        name="filter_spectrum",
+    )(taps, twist, *forward)
+
+
+def correlate_kernel(
+    blocks, rows, sig_ref, filt_ref, twist_ref, fh_ref, fl_ref, bh_ref, bl_ref, out_ref, pair_ref, spec_ref
+):
+    channels, width = sig_ref.shape[1:]
+    to_spectrum(
+        lambda i, at: sig_ref[i, at : at + rows, :],
+        twist_ref, fh_ref, fl_ref, pair_ref, spec_ref, blocks, channels, rows,
+    )
+    for k in range(blocks + 1):
+        for at in range(0, channels, rows):
+            row = k * channels + at
+            sig_re = spec_ref[row : row + rows, :width]
+            sig_im = spec_ref[row : row + rows, width:]
+            filt_re = filt_ref[k, at : at + rows, :width]
+            filt_im = filt_ref[k, at : at + rows, width:]
+            put_split(
+                pair_ref, row, rows,
+                filt_re * sig_re + filt_im * sig_im, filt_re * sig_im - filt_im * sig_re,
+            )
+    spec_ref[...] = wide_dot(pair_ref[...], bh_ref[...], bl_ref[...])
+    for at in range(0, channels, rows):
+        re_lines, im_lines = [], []
+        for k in range(blocks + 1):
+            turn_cos, turn_sin = twist_ref[0, k : k + 1, :], twist_ref[1, k : k + 1, :]
+            row = k * channels + at
+            re, im = spec_ref[row : row + rows, :width], spec_ref[row : row + rows, width:]
+            re_lines.append(re * turn_cos - im * turn_sin)
+            im_lines.append(re * turn_sin + im * turn_cos)
+        for i, value in enumerate(real_parts(re_lines, im_lines, 2 * blocks, blocks)):
+            out_ref[i, at : at + rows, :] = value.astype(jnp.bfloat16)
+
+
+def correlate(signal, spectrum, step):
+    blocks, channels, width = signal.shape
+    twist, forward, backward = dft_constants(blocks, width)
+    lines = blocks + 1
+    whole = lambda *shape: pl.BlockSpec(shape, lambda c: (0,) * len(shape))
+    table = whole(2 * width, 2 * width)
+    return pl.pallas_call(
+        functools.partial(correlate_kernel, blocks, min(16, step)),
+        grid=(channels // step,),
+        in_specs=[
+            pl.BlockSpec((blocks, step, width), lambda c: (0, c, 0)),
+            pl.BlockSpec((lines, step, 2 * width), lambda c: (0, c, 0)),
+            whole(2, lines, width), table, table, table, table,
+        ],
+        out_specs=pl.BlockSpec((blocks, step, width), lambda c: (0, c, 0)),
+        out_shape=jax.ShapeDtypeStruct((blocks, channels, width), jnp.bfloat16),
+        scratch_shapes=[
+            pltpu.VMEM((lines * step, 4 * width), jnp.bfloat16),
+            pltpu.VMEM((lines * step, 2 * width), jnp.float32),
+        ],
+        compiler_params=pltpu.CompilerParams(vmem_limit_bytes=VMEM_BYTES),
+        name="correlate",
+    )(signal, spectrum, twist, *forward, *backward)
 
 
 def dft_tables(count_outer, count_inner):
@@ -77,7 +312,7 @@
     return (outer_wide(outer_cos, turned_re) + outer_wide(outer_sin, turned_im)) / total_len
 
 
-def correlate(gathered, filters, tables):
+def correlate_plain(gathered, filters, tables):
     channel_count, seq_len = gathered.shape
     count_outer = tables[0].shape[0]
     count_inner = tables[2].shape[0]
@@ -95,7 +330,7 @@
     return result.reshape(channel_count, -1)[:, :seq_len].astype(jnp.bfloat16)
 
 
-def per_device(
+def per_device_gathered(
     grad_out, out_weight, gate_stream, conv_output, key_stream, value_stream, long_filter
 ):
     seq_count = lax.axis_size("seq")
@@ -118,13 +353,105 @@
         concat_axis=2,
         tiled=True,
     )
-    inner_grad = correlate(regrouped[0], long_filter, tables)
+    inner_grad = correlate_plain(regrouped[0], long_filter, tables)
     returned = lax.all_to_all(inner_grad[None], "seq", split_axis=2, concat_axis=0, tiled=True)
     grad_inner = returned.reshape(chan_width, token_count)
     grad_gate = (grad_mix * conv_output.astype(jnp.float32)).astype(jnp.bfloat16)
     inner_grad_wide = grad_inner.astype(jnp.float32)
     grad_key = (inner_grad_wide * value_stream.astype(jnp.float32)).astype(jnp.bfloat16)
     grad_value = (inner_grad_wide * key_stream.astype(jnp.float32)).astype(jnp.bfloat16)
+    return (grad_gate, grad_key, grad_value)
+
+
+def mix_kernel(block_rows, slot_ref, grad_ref, *refs):
+    pieces, (own_ref, other_ref) = refs[:-2], refs[-2:]
+    total = None
+    for distance, piece in enumerate(pieces):
+        at = pl.multiple_of((slot_ref[0] ^ distance) * block_rows, block_rows)
+        term = jnp.dot(grad_ref[:, pl.ds(at, block_rows)], piece[...], preferred_element_type=jnp.float32)
+        total = term if total is None else total + term
+    mixed = total.T
+    tokens = own_ref.shape[1]
+    own_ref[...] = mixed[:, :tokens]
+    other_ref[...] = mixed[:, tokens:].astype(jnp.bfloat16)
+
+
+def partial_mix(slot, grads, pieces, step):
+    rows, channels = pieces[0].shape
+    tokens, depth = grads.shape
+    half = tokens // 2
+    out_spec = pl.BlockSpec((step, half), lambda c: (c, 0))
+    return pl.pallas_call(
+        functools.partial(mix_kernel, rows),
+        grid=(channels // step,),
+        in_specs=[
+            pl.BlockSpec(memory_space=pltpu.SMEM),
+            pl.BlockSpec((tokens, depth), lambda c: (0, 0)),
+        ]
+        + [pl.BlockSpec((rows, step), lambda c: (0, c)) for _ in pieces],
+        out_specs=(out_spec, out_spec),
+        out_shape=(
+            jax.ShapeDtypeStruct((channels, half), jnp.float32),
+            jax.ShapeDtypeStruct((channels, half), jnp.bfloat16),
+        ),
+        compiler_params=pltpu.CompilerParams(vmem_limit_bytes=VMEM_BYTES),
+        cost_estimate=pl.CostEstimate(
+            flops=2 * tokens * depth * channels, bytes_accessed=2 * depth * (channels + tokens), transcendentals=0
+        ),
+        name="partial_mix",
+    )(slot, grads, *pieces)
+
+
+def swap(values, axis, count, mask):
+    return lax.ppermute(values, axis, [(i, i ^ mask) for i in range(count)])
+
+
+def per_device(
+    grad_out, out_weight, gate_stream, conv_output, key_stream, value_stream, long_filter
+):
+    seq_count = lax.axis_size("seq")
+    token_count, shard_features = grad_out.shape
+    weight_rows, chan_width = out_weight.shape
+    group_width = chan_width // seq_count
+    group = seq_count // 2
+    place = lax.axis_index("seq")
+    side = place // group
+    spectrum = filter_spectrum(long_filter, seq_count, min(16, group_width))
+
+    shard = lax.axis_index("chan")
+    peer_grad = swap(grad_out, "chan", 2, 1)
+    mine, theirs = (
+        jnp.where(shard == want, grad_out, peer_grad) for want in (side, 1 - side)
+    )
+    peer_tokens = swap(theirs, "seq", seq_count, group)
+    grads = jnp.concatenate([mine, peer_tokens], axis=0)
+
+    half = chan_width // 2
+    near, far = 2, 4
+    across = swap(out_weight, "seq", seq_count, near)
+    along = swap(out_weight, "seq", seq_count, far)
+    corner_a = swap(across[:, :half], "seq", seq_count, far)
+    corner_b = swap(along[:, half:], "seq", seq_count, near)
+    corner = jnp.concatenate([corner_a, corner_b], axis=1)
+    same = [out_weight, across, along, corner]
+    pieces = []
+    for piece in same:
+        pieces += [piece, swap(piece, "seq", seq_count, 1)]
+    slot = (place % group).reshape(1).astype(jnp.int32)
+    own, other = partial_mix(slot, grads, pieces, min(512, chan_width))
+    received = swap(other, "seq", seq_count, group)
+    grad_mix = own + received.astype(jnp.float32)
+
+    gated_grad = (grad_mix * gate_stream.astype(jnp.float32)).astype(jnp.bfloat16)
+    regrouped = lax.all_to_all(
+        gated_grad.reshape(seq_count, group_width, token_count), "seq", split_axis=0, concat_axis=0, tiled=True
+    )
+    inner_grad = correlate(regrouped, spectrum, min(16, group_width))
+    returned = lax.all_to_all(inner_grad, "seq", split_axis=0, concat_axis=0, tiled=True)
+    grad_inner = returned.reshape(chan_width, token_count).astype(jnp.float32)
+    grad_gate = (grad_mix * conv_output.astype(jnp.float32)).astype(jnp.bfloat16)
+    grad_key = (grad_inner * value_stream.astype(jnp.float32)).astype(jnp.bfloat16)
+    grad_value = (grad_inner * key_stream.astype(jnp.float32)).astype(jnp.bfloat16)
     return (grad_gate, grad_key, grad_value)
 
 
@@ -139,6 +466,8 @@
         P(("chan", "seq"), None),
     )
     out_specs = (P("chan", "seq"), P("chan", "seq"), P("chan", "seq"))
+    square = mesh.shape["chan"] == 2 and mesh.shape["seq"] == 16
     return jax.shard_map(
-        per_device, mesh=mesh, in_specs=in_specs, out_specs=out_specs, check_vma=False
-    )
+        per_device if square else per_device_gathered,
+        mesh=mesh, in_specs=in_specs, out_specs=out_specs, check_vma=False,
+    )

time: 273 us -> 156 us (0.57); the launches traced: 268 us -> 156 us
  waiting for transfers between devices: 170 us -> 90 us
  matrix products: 42.9 us -> 0 us
  Pallas kernels: 0 us -> 15.9 us
  between operations: 14.5 us -> 0.8 us
  starting transfers between devices: 3.95 us -> 17 us
  other arithmetic: 15.3 us -> 5.86 us
  local copies, waits for them, and re-layouts: 3.71 us -> 7.71 us
    all_gather x2 -> x0, waiting for transfers between devices: 154 us -> none  [the longest x1 129 us: per_device(): lax.all_gather(out_weight, 'seq', axis=0, tiled=True)]
    ppermute x0 -> x11, waiting for transfers between devices: none -> 79.4 us  [swap(): return lax.ppermute(values, axis, [(i, i ^ mask) for i in range(count)])]
    dot_general x15 -> x0, matrix products: 42.9 us -> none  [the longest x8 22.7 us: inner_wide(): jnp.einsum('cak,kl->cal', values, table, precision=lax.Precision.HIGH, pr...]
    pallas_call x0 -> x3, Pallas kernels: none -> 15.9 us  [the longest x1 7.2 us: correlate(): pl.pallas_call(functools.partial(correlate_kernel, blocks, min(16, step))...]
    ppermute x0 -> x11, starting transfers between devices: none -> 12.6 us  [swap(): return lax.ppermute(values, axis, [(i, i ^ mask) for i in range(count)])]
    unnamed x2 -> x0, other arithmetic: 12.1 us -> none
    all_to_all x1, waiting for transfers between devices: 14.2 us -> 10.6 us  [per_device(): lax.all_to_all(gated_grad.reshape(seq_count, group_width, token_count), '...]
  transfers between devices with their start and end apart: 3 -> 12, of which waited for: 3 -> 7; matrix products, arithmetic and copies ran while one was open for 0% -> 5% of each run, Pallas kernels for 0% -> 2%
where the time goes in v1:
time: 156 us
  waiting for transfers between devices  90 us (58%)
  blocking collectives  18.4 us (12%)
  starting transfers between devices  17 us (11%)
  Pallas kernels  15.9 us (10%)
  local copies, waits for them, and re-layouts  7.71 us (5%)
  other arithmetic  5.86 us (4%)
    ppermute x11, waiting for transfers between devices, swap(): return lax.ppermute(values, axis, [(i, i ^ mask) for i in range(count)])  79.4 us
    all_to_all x1, blocking collectives, per_device(): lax.all_to_all(inner_grad, 'seq', split_axis=0, concat_axis=0, tiled=True)  18.4 us
    ppermute x11, starting transfers between devices, swap(): return lax.ppermute(values, axis, [(i, i ^ mask) for i in range(count)])  12.6 us
    all_to_all x1, waiting for transfers between devices, per_device(): lax.all_to_all(gated_grad.reshape(seq_count, group_width, token_count), '...  10.6 us
    pallas_call x1, Pallas kernels, correlate(): pl.pallas_call(functools.partial(correlate_kernel, blocks, min(16, step))...  7.2 us
    pallas_call x1, Pallas kernels, partial_mix(): pl.pallas_call(functools.partial(mix_kernel, rows), grid=(channels // ste...  5.58 us
    all_to_all x1, starting transfers between devices, per_device(): lax.all_to_all(gated_grad.reshape(seq_count, group_width, token_count), '...  4.43 us
    unnamed x27, local copies, waits for them, and re-layouts  4.17 us
  transfers between devices with their start and end apart: 12, of which 7 were waited for; matrix products, arithmetic and copies ran while one was open for 5% of the time, Pallas kernels for 2%

profile of v1, /device:TPU:0, one launch (start us, length us, event | category | flops | bytes accessed | tf_op | source)
XLA Modules:
  0.0 155.7 jit_solution(10963242472452815820)
XLA Ops:
  0.6 3.0 %collective-permute-start.3 = (bf16[256,2048]{1,0:T(8,128)(2,1)}, bf16[256,2048]{1,0:T(8,128)(2,1)S(1)}, u32[]{:S(2)}, u32[]{:S(2)}) collective-permute-start(bf16[256,2048]{1,0:T(8,128)(2,1)} %refs_0_.1), channel_id=1, source_target_pairs={{0,4},{2,6},{4,0},{6,2},{8,12},{10,14},{12,8},{14,10},{16,20},{18,... | collective-permute-start | bytes 3145736 | tf_op jit(solution)/shard_map/ppermute | solution.py:406
  3.6 1.6 %collective-permute-start.5 = (bf16[256,2048]{1,0:T(8,128)(2,1)}, bf16[256,2048]{1,0:T(8,128)(2,1)}, u32[]{:S(2)}, u32[]{:S(2)}) collective-permute-start(bf16[256,2048]{1,0:T(8,128)(2,1)} %refs_0_.1), channel_id=1, source_target_pairs={{0,8},{2,10},{4,12},{6,14},{8,0},{10,2},{12,4},{14,6},{16,24},{18,... | collective-permute-start | bytes 3145736 | tf_op jit(solution)/shard_map/ppermute | solution.py:406
  5.2 21.8 %collective-permute-done.3.refs_2_ = bf16[256,2048]{1,0:T(8,128)(2,1)S(1)} collective-permute-done((bf16[256,2048]{1,0:T(8,128)(2,1)}, bf16[256,2048]{1,0:T(8,128)(2,1)S(1)}, u32[]{:S(2)}, u32[]{:S(2)}) %collective-permute-start.3) | collective-permute-done | bytes 1048608 | tf_op jit(solution)/shard_map/ppermute | solution.py:406
  27.8 1.8 %collective-permute-start.7 = (bf16[256,1024]{1,0:T(8,128)(2,1)}, bf16[256,1024]{1,0:T(8,128)(2,1)S(1)}, u32[]{:S(2)}, u32[]{:S(2)}) collective-permute-start(bf16[256,1024]{1,0:T(8,128)(2,1)} %slice.8), channel_id=1, source_target_pairs={{0,8},{2,10},{4,12},{6,14},{8,0},{10,2},{12,4},{14,6},{16,24},{18,... | collective-permute-start | bytes 1572872 | tf_op jit(solution)/shard_map/ppermute | solution.py:406
  29.7 1.9 %slice.9 = bf16[256,1024]{1,0:T(8,128)(2,1)} slice(bf16[256,2048]{1,0:T(8,128)(2,1)} %collective-permute-done.5.refs_4_), slice={[0:256], [1024:2048]} | slice | bytes 1048576 | tf_op jit(solution)/shard_map/slice | solution.py:434
  31.5 1.5 collective-permute-start.8
  33.0 1.5 collective-permute-start
  35.1 6.2 %collective-permute-done.7 = bf16[256,1024]{1,0:T(8,128)(2,1)S(1)} collective-permute-done((bf16[256,1024]{1,0:T(8,128)(2,1)}, bf16[256,1024]{1,0:T(8,128)(2,1)S(1)}, u32[]{:S(2)}, u32[]{:S(2)}) %collective-permute-start.7) | collective-permute-done | bytes 524320 | tf_op jit(solution)/shard_map/ppermute | solution.py:406
  42.1 2.2 %collective-permute-done.8 = bf16[256,1024]{1,0:T(8,128)(2,1)S(1)} collective-permute-done((bf16[256,1024]{1,0:T(8,128)(2,1)}, bf16[256,1024]{1,0:T(8,128)(2,1)S(1)}, u32[]{:S(2)}, u32[]{:S(2)}) %collective-permute-start.8) | collective-permute-done | bytes 524320 | tf_op jit(solution)/shard_map/ppermute | solution.py:406
  45.7 2.1 %broadcast_select_fusion.1 = (bf16[128,2048]{1,0:T(8,128)(2,1)}, bf16[128,2048]{1,0:T(8,128)(2,1)}) fusion(bf16[128,2048]{1,0:T(8,128)(2,1)S(1)} %copy-done.12, bf16[128,2048]{1,0:T(8,128)(2,1)} %collective-permute-done, pred[]{:T(512)S(6)} %eq.8, pred[]{:T(512)S(6)} %eq.9), kind=kLoop, calls=%fused_computation.9 | loop fusion | flops 524288 | bytes 2097154 | tf_op jit(solution)/shard_map/jit(_where)/select_n | solution.py:424
  47.8 2.6 %collective-permute-start.1 = (bf16[128,2048]{1,0:T(8,128)(2,1)}, bf16[128,2048]{1,0:T(8,128)(2,1)}, u32[]{:S(2)}, u32[]{:S(2)}) collective-permute-start(bf16[128,2048]{1,0:T(8,128)(2,1)} %get-tuple-element.10), channel_id=1, source_target_pairs={{0,16},{2,18},{4,20},{6,22},{8,24},{10,26},{12,28},{14,30},{16,0},... | collective-permute-start | bytes 1572872 | tf_op jit(solution)/shard_map/ppermute | solution.py:406
  50.4 23.7 %collective-permute-done.1 = bf16[128,2048]{1,0:T(8,128)(2,1)} collective-permute-done((bf16[128,2048]{1,0:T(8,128)(2,1)}, bf16[128,2048]{1,0:T(8,128)(2,1)}, u32[]{:S(2)}, u32[]{:S(2)}) %collective-permute-start.1) | collective-permute-done | bytes 524320 | tf_op jit(solution)/shard_map/ppermute | solution.py:406
  74.0 1.3 pad_maximum_fusion.grad_ref
  75.4 5.6 %partial_mix.1 = (f32[2048,128]{1,0:T(8,128)S(1)}, bf16[2048,128]{1,0:T(8,128)(2,1)S(1)}) custom-call(s32[1]{0:T(128)} %bitcast.slot_ref, bf16[256,2048]{1,0:T(8,128)(2,1)S(1)} %pad_maximum_fusion.grad_ref, bf16[256,2048]{1,0:T(8,128)(2,1)S(1)} %copy-done, bf16[256,2048]{1,0:T(8,128)(2,1)S(1)} %collective-permute-done.2.refs_1_, ...), custom_call_target="tpu_custom_call" | custom-call | flops 2147483648 | bytes 9437184 | tf_op jit(solution)/shard_map/partial_mix/pallas_call | solution.py:384
  81.1 25.0 %collective-permute-done.10 = bf16[2048,128]{1,0:T(8,128)(2,1)S(1)} collective-permute-done((bf16[2048,128]{1,0:T(8,128)(2,1)S(1)}, bf16[2048,128]{1,0:T(8,128)(2,1)S(1)}, u32[]{:S(2)}, u32[]{:S(2)}) %collective-permute-start.10) | collective-permute-done | bytes 524320 | tf_op jit(solution)/shard_map/ppermute | solution.py:406
  106.1 1.2 multiply_convert_fusion
  107.4 4.4 %all-to-all-start = ((bf16[16,128,128]{2,1,0:T(8,128)(2,1)}), bf16[16,128,128]{2,1,0:T(8,128)(2,1)S(1)}, u32[]{:S(2)}, u32[]{:S(2)}) async-start(bf16[16,128,128]{2,1,0:T(8,128)(2,1)} %bitcast.1), calls=%async_computation | async-start | bytes 1048576 | tf_op jit(solution)/shard_map/all_to_all | solution.py:446
  112.6 3.1 %filter_spectrum.1.filt_ref = f32[17,128,256]{2,1,0:T(8,128)S(1)} custom-call(bf16[128,2048]{1,0:T(8,128)(2,1)S(1)} %copy-done.1, f32[2,17,128]{2,1,0:T(8,128)S(1)} %copy-done.6, bf16[256,256]{1,0:T(8,128)(2,1)S(1)} %copy-done.3, bf16[256,256]{1,0:T(8,128)(2,1)S(1)} %copy-done.2), custom_call_target="tpu_custom_call" | custom-call | tf_op jit(solution)/shard_map/filter_spectrum/pallas_call | solution.py:169
  115.7 10.6 %all-to-all-done.sig_ref = bf16[16,128,128]{2,1,0:T(8,128)(2,1)S(1)} async-done(((bf16[16,128,128]{2,1,0:T(8,128)(2,1)}), bf16[16,128,128]{2,1,0:T(8,128)(2,1)S(1)}, u32[]{:S(2)}, u32[]{:S(2)}) %all-to-all-start) | async-done | bytes 524320 | tf_op jit(solution)/shard_map/all_to_all | solution.py:446
  126.3 0.9 copy-done.4
  127.2 0.9 copy-done.5
  128.9 7.2 %correlate.1 = bf16[16,128,128]{2,1,0:T(8,128)(2,1)S(1)} custom-call(bf16[16,128,128]{2,1,0:T(8,128)(2,1)S(1)} %all-to-all-done.sig_ref, f32[17,128,256]{2,1,0:T(8,128)S(1)} %filter_spectrum.1.filt_ref, f32[2,17,128]{2,1,0:T(8,128)S(1)} %copy-done.7, bf16[256,256]{1,0:T(8,128)(2,1)S(1)} %copy-done.3, bf16[256,256]{1,0:T(8,128)(2,1)S(1)} %copy-done.2, ...), custom_call_target="tpu_custom_call" | custom-call | tf_op jit(solution)/shard_map/correlate/pallas_call | solution.py:225
  136.1 18.4 %all_to_all.10 = bf16[16,128,128]{2,1,0:T(8,128)(2,1)S(1)} all-to-all(bf16[16,128,128]{2,1,0:T(8,128)(2,1)S(1)} %correlate.1), channel_id=1, replica_groups=mesh['seq'=16,'chan'=2] {'seq'}, dimensions={0} | all-to-all | bytes 1048576 | tf_op jit(solution)/shard_map/all_to_all | solution.py:450
  154.4 1.2 fusion.1
  (38 shorter events, 5.1 us)
Async XLA Ops:
  0.6 26.4 %collective-permute-start.3 = (bf16[256,2048]{1,0:T(8,128)(2,1)}, bf16[256,2048]{1,0:T(8,128)(2,1)S(1)}, u32[]{:S(2)}, u32[]{:S(2)}) collective-permute-start(bf16[256,2048]{1,0:T(8,128)(2,1)} %refs_0_.1), channel_id=1, source_target_pairs={{0,4},{2,6},{4,0},{6,2},{8,12},{10,14},{12,8},{14,10},{16,20},{18,... | collective-permute-start | bytes 3145736 | tf_op jit(solution)/shard_map/ppermute | solution.py:406
  3.6 26.0 %collective-permute-start.5 = (bf16[256,2048]{1,0:T(8,128)(2,1)}, bf16[256,2048]{1,0:T(8,128)(2,1)}, u32[]{:S(2)}, u32[]{:S(2)}) collective-permute-start(bf16[256,2048]{1,0:T(8,128)(2,1)} %refs_0_.1), channel_id=1, source_target_pairs={{0,8},{2,10},{4,12},{6,14},{8,0},{10,2},{12,4},{14,6},{16,24},{18,... | collective-permute-start | bytes 3145736 | tf_op jit(solution)/shard_map/ppermute | solution.py:406
  27.8 13.4 %collective-permute-start.7 = (bf16[256,1024]{1,0:T(8,128)(2,1)}, bf16[256,1024]{1,0:T(8,128)(2,1)S(1)}, u32[]{:S(2)}, u32[]{:S(2)}) collective-permute-start(bf16[256,1024]{1,0:T(8,128)(2,1)} %slice.8), channel_id=1, source_target_pairs={{0,8},{2,10},{4,12},{6,14},{8,0},{10,2},{12,4},{14,6},{16,24},{18,... | collective-permute-start | bytes 1572872 | tf_op jit(solution)/shard_map/ppermute | solution.py:406
  31.5 12.8 %collective-permute-start.8 = (bf16[256,1024]{1,0:T(8,128)(2,1)}, bf16[256,1024]{1,0:T(8,128)(2,1)S(1)}, u32[]{:S(2)}, u32[]{:S(2)}) collective-permute-start(bf16[256,1024]{1,0:T(8,128)(2,1)} %slice.9), channel_id=1, source_target_pairs={{0,4},{2,6},{4,0},{6,2},{8,12},{10,14},{12,8},{14,10},{16,20},{18,... | collective-permute-start | bytes 1572872 | tf_op jit(solution)/shard_map/ppermute | solution.py:406
  33.0 12.7 %collective-permute-start = (bf16[128,2048]{1,0:T(8,128)(2,1)}, bf16[128,2048]{1,0:T(8,128)(2,1)}, u32[]{:S(2)}, u32[]{:S(2)}) collective-permute-start(bf16[128,2048]{1,0:T(8,128)(2,1)} %param.15), channel_id=1, source_target_pairs={{0,1},{1,0},{2,3},{3,2},{4,5},{5,4},{6,7},{7,6},{8,9},{9,8},{10,11... | collective-permute-start | bytes 1572872 | tf_op jit(solution)/shard_map/ppermute | solution.py:406
  34.6 40.8 %collective-permute-start.2 = (bf16[256,2048]{1,0:T(8,128)(2,1)}, bf16[256,2048]{1,0:T(8,128)(2,1)S(1)}, u32[]{:S(2)}, u32[]{:S(2)}) collective-permute-start(bf16[256,2048]{1,0:T(8,128)(2,1)} %refs_0_.1), channel_id=1, source_target_pairs={{0,2},{2,0},{4,6},{6,4},{8,10},{10,8},{12,14},{14,12},{16,18},{18,... | collective-permute-start | bytes 3145736 | tf_op jit(solution)/shard_map/ppermute | solution.py:406
  34.6 11.1 %copy-start.12 = (bf16[128,2048]{1,0:T(8,128)(2,1)S(1)}, bf16[128,2048]{1,0:T(8,128)(2,1)}, u32[]{:S(2)}) copy-start(bf16[128,2048]{1,0:T(8,128)(2,1)} %param.15) | copy-start | bytes 1572868
  34.6 40.8 %collective-permute-start.4 = (bf16[256,2048]{1,0:T(8,128)(2,1)S(1)}, bf16[256,2048]{1,0:T(8,128)(2,1)}, u32[]{:S(2)}, u32[]{:S(2)}) collective-permute-start(bf16[256,2048]{1,0:T(8,128)(2,1)S(1)} %collective-permute-done.3.refs_2_), channel_id=1, source_target_pairs={{0,2},{2,0},{4,6},{6,4},{8,10},{10,8},{12,14},{14,12},{16,18},{18,... | collective-permute-start | bytes 3145736 | tf_op jit(solution)/shard_map/ppermute | solution.py:406
  41.3 34.1 %collective-permute-start.6 = (bf16[256,2048]{1,0:T(8,128)(2,1)}, bf16[256,2048]{1,0:T(8,128)(2,1)}, u32[]{:S(2)}, u32[]{:S(2)}) collective-permute-start(bf16[256,2048]{1,0:T(8,128)(2,1)} %collective-permute-done.5.refs_4_), channel_id=1, source_target_pairs={{0,2},{2,0},{4,6},{6,4},{8,10},{10,8},{12,14},{14,12},{16,18},{18,... | collective-permute-start | bytes 3145736 | tf_op jit(solution)/shard_map/ppermute | solution.py:406
  45.2 30.2 %copy-start = (bf16[256,2048]{1,0:T(8,128)(2,1)S(1)}, bf16[256,2048]{1,0:T(8,128)(2,1)}, u32[]{:S(2)}) copy-start(bf16[256,2048]{1,0:T(8,128)(2,1)} %refs_0_.1) | copy-start | bytes 3145732
  45.2 30.2 %collective-permute-start.9 = (bf16[256,2048]{1,0:T(8,128)(2,1)}, bf16[256,2048]{1,0:T(8,128)(2,1)}, u32[]{:S(2)}, u32[]{:S(2)}) collective-permute-start(bf16[256,2048]{1,0:T(8,128)(2,1)} %constant_dynamic-update-slice_fusion.refs_6_), channel_id=1, source_target_pairs={{0,2},{2,0},{4,6},{6,4},{8,10},{10,8},{12,14},{14,12},{16,18},{18,... | collective-permute-start | bytes 3145736 | tf_op jit(solution)/shard_map/ppermute | solution.py:406
  47.8 26.3 %collective-permute-start.1 = (bf16[128,2048]{1,0:T(8,128)(2,1)}, bf16[128,2048]{1,0:T(8,128)(2,1)}, u32[]{:S(2)}, u32[]{:S(2)}) collective-permute-start(bf16[128,2048]{1,0:T(8,128)(2,1)} %get-tuple-element.10), channel_id=1, source_target_pairs={{0,16},{2,18},{4,20},{6,22},{8,24},{10,26},{12,28},{14,30},{16,0},... | collective-permute-start | bytes 1572872 | tf_op jit(solution)/shard_map/ppermute | solution.py:406
  75.4 30.7 %copy-start.8 = (bf16[2048,128]{1,0:T(8,128)(2,1)S(1)}, bf16[2048,128]{1,0:T(8,128)(2,1)}, u32[]{:S(2)}) copy-start(bf16[2048,128]{1,0:T(8,128)(2,1)} %param.17) | copy-start | bytes 1572868
  75.4 30.7 %copy-start.9 = (bf16[2048,128]{1,0:T(8,128)(2,1)S(1)}, bf16[2048,128]{1,0:T(8,128)(2,1)}, u32[]{:S(2)}) copy-start(bf16[2048,128]{1,0:T(8,128)(2,1)} %param.18) | copy-start | bytes 1572868
  81.0 25.1 %collective-permute-start.10 = (bf16[2048,128]{1,0:T(8,128)(2,1)S(1)}, bf16[2048,128]{1,0:T(8,128)(2,1)S(1)}, u32[]{:S(2)}, u32[]{:S(2)}) collective-permute-start(bf16[2048,128]{1,0:T(8,128)(2,1)S(1)} %get-tuple-element.6), channel_id=1, source_target_pairs={{0,16},{2,18},{4,20},{6,22},{8,24},{10,26},{12,28},{14,30},{16,0},... | collective-permute-start | bytes 1572872 | tf_op jit(solution)/shard_map/ppermute | solution.py:406
  106.1 5.7 %copy-start.1 = (bf16[128,2048]{1,0:T(8,128)(2,1)S(1)}, bf16[128,2048]{1,0:T(8,128)(2,1)}, u32[]{:S(2)}) copy-start(bf16[128,2048]{1,0:T(8,128)(2,1)} %taps_ref.1) | copy-start | bytes 1572868
  106.1 5.7 %copy-start.2 = (bf16[256,256]{1,0:T(8,128)(2,1)S(1)}, bf16[256,256]{1,0:T(8,128)(2,1)}, u32[]{:S(2)}) copy-start(bf16[256,256]{1,0:T(8,128)(2,1)} %constant.47.clone.low_ref.fl_ref) | copy-start | bytes 393220
  106.1 5.7 %copy-start.3 = (bf16[256,256]{1,0:T(8,128)(2,1)S(1)}, bf16[256,256]{1,0:T(8,128)(2,1)}, u32[]{:S(2)}) copy-start(bf16[256,256]{1,0:T(8,128)(2,1)} %constant.46.clone.high_ref.fh_ref) | copy-start | bytes 393220
  107.4 18.9 %all-to-all-start = ((bf16[16,128,128]{2,1,0:T(8,128)(2,1)}), bf16[16,128,128]{2,1,0:T(8,128)(2,1)S(1)}, u32[]{:S(2)}, u32[]{:S(2)}) async-start(bf16[16,128,128]{2,1,0:T(8,128)(2,1)} %bitcast.1), calls=%async_computation | async-start | bytes 1048576 | tf_op jit(solution)/shard_map/all_to_all | solution.py:446
  111.9 0.7 copy-start.6
  126.3 0.9 copy-start.4
  127.2 0.9 copy-start.5
  128.8 25.6 %copy-start.10 = (bf16[2048,128]{1,0:T(8,128)(2,1)S(1)}, bf16[2048,128]{1,0:T(8,128)(2,1)}, u32[]{:S(2)}) copy-start(bf16[2048,128]{1,0:T(8,128)(2,1)} %param.19) | copy-start | bytes 1572868
  128.8 25.6 %copy-start.11 = (bf16[2048,128]{1,0:T(8,128)(2,1)S(1)}, bf16[2048,128]{1,0:T(8,128)(2,1)}, u32[]{:S(2)}) copy-start(bf16[2048,128]{1,0:T(8,128)(2,1)} %param.20) | copy-start | bytes 1572868
  (1 other events, 0.7 us)

commit v2 on v1

--- a/solution.py
+++ b/solution.py
@@ -419,17 +419,26 @@
     spectrum = filter_spectrum(long_filter, seq_count, min(16, group_width))
 
     shard = lax.axis_index("chan")
-    peer_grad = swap(grad_out, "chan", 2, 1)
-    mine, theirs = (
-        jnp.where(shard == want, grad_out, peer_grad) for want in (side, 1 - side)
-    )
-    peer_tokens = swap(theirs, "seq", seq_count, group)
-    grads = jnp.concatenate([mine, peer_tokens], axis=0)
-
+    home = shard == side
+    rows = token_count // 2
+    both = ("seq", "chan")
+    at = lambda s, y: s * 2 + y
+    away = [(s, 1 - s // group) for s in range(seq_count)]
+    straight = [(at(s, y), at(s ^ group, y)) for s, y in away]
+    slanted = [(at(s, y), at(s ^ group, 1 - y)) for s, y in away]
+    beside = [(at(s, 1 - y), at(s, y)) for s, y in away]
+    first = lax.ppermute(grad_out[:rows], both, straight)
+    second = lax.ppermute(grad_out[rows:], both, slanted)
+    local = lax.ppermute(grad_out, both, beside)
     half = chan_width // 2
     near, far = 2, 4
     across = swap(out_weight, "seq", seq_count, near)
     along = swap(out_weight, "seq", seq_count, far)
+    across, along, first, second, local = lax.optimization_barrier((across, along, first, second, local))
+    passed = swap(jnp.where(home, first, second), "chan", 2, 1)
+    grads = jnp.concatenate(
+        [jnp.where(home, grad_out, local), jnp.where(home, first, passed), jnp.where(home, passed, second)], axis=0
+    )
     corner_a = swap(across[:, :half], "seq", seq_count, far)
     corner_b = swap(along[:, half:], "seq", seq_count, near)
     corner = jnp.concatenate([corner_a, corner_b], axis=1)

time: 156 us -> 143 us (0.917)
  waiting for transfers between devices: 90 us -> 73.9 us
  starting transfers between devices: 17 us -> 19.1 us
  local copies, waits for them, and re-layouts: 7.71 us -> 9.37 us
    ppermute x11 -> x10, waiting for transfers between devices: 79.4 us -> 49.9 us  [swap(): return lax.ppermute(values, axis, [(i, i ^ mask) for i in range(count)])]
    ppermute x0 -> x3, waiting for transfers between devices: none -> 13.4 us  [the longest x1 12.9 us: per_device(): first = lax.ppermute(grad_out[:rows], both, straight)]
    ppermute x0 -> x3, starting transfers between devices: none -> 5.42 us  [the longest x1 3.45 us: per_device(): local = lax.ppermute(grad_out, both, beside)]
    ppermute x11 -> x10, starting transfers between devices: 12.6 us -> 10.2 us  [swap(): return lax.ppermute(values, axis, [(i, i ^ mask) for i in range(count)])]
    unnamed x27 -> x41, local copies, waits for them, and re-layouts: 4.17 us -> 6.28 us
  transfers between devices with their start and end apart: 12 -> 14, of which waited for: 7 -> 8; matrix products, arithmetic and copies ran while one was open for 5% -> 4% of each run, Pallas kernels for 2% -> 2%
where the time goes in v2:
time: 143 us; the launch traced here: 142 us
  waiting for transfers between devices  73.9 us (52%)
  starting transfers between devices  19.1 us (13%)
  blocking collectives  18.3 us (13%)
  Pallas kernels  15.7 us (11%)
  local copies, waits for them, and re-layouts  9.37 us (7%)
  other arithmetic  4.62 us (3%)
    ppermute x10, waiting for transfers between devices, swap(): return lax.ppermute(values, axis, [(i, i ^ mask) for i in range(count)])  49.9 us
    all_to_all x1, blocking collectives, per_device(): lax.all_to_all(inner_grad, 'seq', split_axis=0, concat_axis=0, tiled=True)  18.3 us
    ppermute x1, waiting for transfers between devices, per_device(): first = lax.ppermute(grad_out[:rows], both, straight)  12.9 us
    all_to_all x1, waiting for transfers between devices, per_device(): lax.all_to_all(gated_grad.reshape(seq_count, group_width, token_count), '...  10.6 us
    ppermute x10, starting transfers between devices, swap(): return lax.ppermute(values, axis, [(i, i ^ mask) for i in range(count)])  10.2 us
    pallas_call x1, Pallas kernels, correlate(): pl.pallas_call(functools.partial(correlate_kernel, blocks, min(16, step))...  7.2 us
    unnamed x41, local copies, waits for them, and re-layouts  6.28 us
    pallas_call x1, Pallas kernels, partial_mix(): pl.pallas_call(functools.partial(mix_kernel, rows), grid=(channels // ste...  5.44 us
  transfers between devices with their start and end apart: 14, of which 8 were waited for; matrix products, arithmetic and copies ran while one was open for 4% of the time, Pallas kernels for 2%

profile of v2, /device:TPU:0, one launch (start us, length us, event | category | flops | bytes accessed | tf_op | source)
XLA Modules:
  0.0 141.9 jit_solution(16951580810649150649)
XLA Ops:
  0.6 3.1 %collective-permute-start.1 = (bf16[256,2048]{1,0:T(8,128)(2,1)}, bf16[256,2048]{1,0:T(8,128)(2,1)S(1)}, u32[]{:S(2)}, u32[]{:S(2)}) collective-permute-start(bf16[256,2048]{1,0:T(8,128)(2,1)} %refs_0_.1), channel_id=1, source_target_pairs={{0,8},{2,10},{4,12},{6,14},{8,0},{10,2},{12,4},{14,6},{16,24},{18,... | collective-permute-start | bytes 3145736 | tf_op jit(solution)/shard_map/ppermute | solution.py:406
  3.7 1.5 %collective-permute-start = (bf16[256,2048]{1,0:T(8,128)(2,1)}, bf16[256,2048]{1,0:T(8,128)(2,1)S(1)}, u32[]{:S(2)}, u32[]{:S(2)}) collective-permute-start(bf16[256,2048]{1,0:T(8,128)(2,1)} %refs_0_.1), channel_id=1, source_target_pairs={{0,4},{2,6},{4,0},{6,2},{8,12},{10,14},{12,8},{14,10},{16,20},{18,... | collective-permute-start | bytes 3145736 | tf_op jit(solution)/shard_map/ppermute | solution.py:406
  5.2 3.4 %collective-permute-start.4 = (bf16[128,2048]{1,0:T(8,128)(2,1)}, bf16[128,2048]{1,0:T(8,128)(2,1)S(1)}, u32[]{:S(2)}, u32[]{:S(2)}) collective-permute-start(bf16[128,2048]{1,0:T(8,128)(2,1)} %param.15), channel_id=1, source_target_pairs={{0,1},{2,3},{4,5},{6,7},{8,9},{10,11},{12,13},{14,15},{17,16},{19,... | collective-permute-start | bytes 1572872 | tf_op jit(solution)/shard_map/ppermute | solution.py:432
  8.7 1.1 fusion.2
  10.4 1.3 collective-permute-start.2
  11.7 12.9 %collective-permute-done.2 = bf16[64,2048]{1,0:T(8,128)(2,1)} collective-permute-done((bf16[64,2048]{1,0:T(8,128)(2,1)S(1)}, bf16[64,2048]{1,0:T(8,128)(2,1)}, u32[]{:S(2)}, u32[]{:S(2)}) %collective-permute-start.2) | collective-permute-done | bytes 262176 | tf_op jit(solution)/shard_map/ppermute | solution.py:430
  25.2 13.2 %collective-permute-done.1.refs_4_ = bf16[256,2048]{1,0:T(8,128)(2,1)S(1)} collective-permute-done((bf16[256,2048]{1,0:T(8,128)(2,1)}, bf16[256,2048]{1,0:T(8,128)(2,1)S(1)}, u32[]{:S(2)}, u32[]{:S(2)}) %collective-permute-start.1) | collective-permute-done | bytes 1048608 | tf_op jit(solution)/shard_map/ppermute | solution.py:406
  39.5 3.0 %collective-permute-start.9 = (bf16[256,1024]{1,0:T(8,128)(2,1)}, bf16[256,1024]{1,0:T(8,128)(2,1)}, u32[]{:S(2)}, u32[]{:S(2)}) collective-permute-start(bf16[256,1024]{1,0:T(8,128)(2,1)} %slice.14), channel_id=1, source_target_pairs={{0,8},{2,10},{4,12},{6,14},{8,0},{10,2},{12,4},{14,6},{16,24},{18,... | collective-permute-start | bytes 1572872 | tf_op jit(solution)/shard_map/ppermute | solution.py:406
  43.0 1.1 slice.15
  44.3 1.5 %collective-permute-start.10 = (bf16[256,1024]{1,0:T(8,128)(2,1)S(1)}, bf16[256,1024]{1,0:T(8,128)(2,1)S(1)}, u32[]{:S(2)}, u32[]{:S(2)}) collective-permute-start(bf16[256,1024]{1,0:T(8,128)(2,1)S(1)} %slice.15), channel_id=1, source_target_pairs={{0,4},{2,6},{4,0},{6,2},{8,12},{10,14},{12,8},{14,10},{16,20},{18,... | collective-permute-start | bytes 1572872 | tf_op jit(solution)/shard_map/ppermute | solution.py:406
  46.8 7.1 %collective-permute-done.9 = bf16[256,1024]{1,0:T(8,128)(2,1)} collective-permute-done((bf16[256,1024]{1,0:T(8,128)(2,1)}, bf16[256,1024]{1,0:T(8,128)(2,1)}, u32[]{:S(2)}, u32[]{:S(2)}) %collective-permute-start.9) | collective-permute-done | bytes 524320 | tf_op jit(solution)/shard_map/ppermute | solution.py:406
  53.9 1.1 constant_dynamic-update-slice_fusion.1
  55.0 3.5 %collective-permute-done.10 = bf16[256,1024]{1,0:T(8,128)(2,1)S(1)} collective-permute-done((bf16[256,1024]{1,0:T(8,128)(2,1)S(1)}, bf16[256,1024]{1,0:T(8,128)(2,1)S(1)}, u32[]{:S(2)}, u32[]{:S(2)}) %collective-permute-start.10) | collective-permute-done | bytes 524320 | tf_op jit(solution)/shard_map/ppermute | solution.py:406
  58.7 1.7 %collective-permute-done.5 = bf16[64,2048]{1,0:T(8,128)(2,1)S(1)} collective-permute-done((bf16[64,2048]{1,0:T(8,128)(2,1)S(1)}, bf16[64,2048]{1,0:T(8,128)(2,1)S(1)}, u32[]{:S(2)}, u32[]{:S(2)}) %collective-permute-start.5) | collective-permute-done | bytes 262176 | tf_op jit(solution)/shard_map/ppermute | solution.py:406
  60.4 1.0 broadcast_select_fusion.2
  63.3 5.4 %partial_mix.1 = (f32[2048,128]{1,0:T(8,128)S(1)}, bf16[2048,128]{1,0:T(8,128)(2,1)S(1)}) custom-call(s32[1]{0:T(128)} %bitcast.slot_ref, bf16[256,2048]{1,0:T(8,128)(2,1)S(1)} %pad_maximum_fusion.grad_ref, bf16[256,2048]{1,0:T(8,128)(2,1)S(1)} %copy-done, bf16[256,2048]{1,0:T(8,128)(2,1)S(1)} %collective-permute-done.6.refs_1_, ...), custom_call_target="tpu_custom_call" | custom-call | flops 2147483648 | bytes 9437184 | tf_op jit(solution)/shard_map/partial_mix/pallas_call | solution.py:384
  68.9 24.4 %collective-permute-done.12 = bf16[2048,128]{1,0:T(8,128)(2,1)S(1)} collective-permute-done((bf16[2048,128]{1,0:T(8,128)(2,1)S(1)}, bf16[2048,128]{1,0:T(8,128)(2,1)S(1)}, u32[]{:S(2)}, u32[]{:S(2)}) %collective-permute-start.12) | collective-permute-done | bytes 524320 | tf_op jit(solution)/shard_map/ppermute | solution.py:406
  93.4 1.2 multiply_convert_fusion
  94.6 3.6 %all-to-all-start = ((bf16[16,128,128]{2,1,0:T(8,128)(2,1)}), bf16[16,128,128]{2,1,0:T(8,128)(2,1)S(1)}, u32[]{:S(2)}, u32[]{:S(2)}) async-start(bf16[16,128,128]{2,1,0:T(8,128)(2,1)} %bitcast.1), calls=%async_computation | async-start | bytes 1048576 | tf_op jit(solution)/shard_map/all_to_all | solution.py:455
  99.0 3.1 %filter_spectrum.1.filt_ref = f32[17,128,256]{2,1,0:T(8,128)S(1)} custom-call(bf16[128,2048]{1,0:T(8,128)(2,1)S(1)} %copy-done.1, f32[2,17,128]{2,1,0:T(8,128)S(1)} %copy-done.6, bf16[256,256]{1,0:T(8,128)(2,1)S(1)} %copy-done.3, bf16[256,256]{1,0:T(8,128)(2,1)S(1)} %copy-done.2), custom_call_target="tpu_custom_call" | custom-call | tf_op jit(solution)/shard_map/filter_spectrum/pallas_call | solution.py:169
  102.1 10.6 %all-to-all-done.sig_ref = bf16[16,128,128]{2,1,0:T(8,128)(2,1)S(1)} async-done(((bf16[16,128,128]{2,1,0:T(8,128)(2,1)}), bf16[16,128,128]{2,1,0:T(8,128)(2,1)S(1)}, u32[]{:S(2)}, u32[]{:S(2)}) %all-to-all-start) | async-done | bytes 524320 | tf_op jit(solution)/shard_map/all_to_all | solution.py:455
  115.2 7.2 %correlate.1 = bf16[16,128,128]{2,1,0:T(8,128)(2,1)S(1)} custom-call(bf16[16,128,128]{2,1,0:T(8,128)(2,1)S(1)} %all-to-all-done.sig_ref, f32[17,128,256]{2,1,0:T(8,128)S(1)} %filter_spectrum.1.filt_ref, f32[2,17,128]{2,1,0:T(8,128)S(1)} %copy-done.7, bf16[256,256]{1,0:T(8,128)(2,1)S(1)} %copy-done.3, bf16[256,256]{1,0:T(8,128)(2,1)S(1)} %copy-done.2, ...), custom_call_target="tpu_custom_call" | custom-call | tf_op jit(solution)/shard_map/correlate/pallas_call | solution.py:225
  122.4 18.3 %all_to_all.10 = bf16[16,128,128]{2,1,0:T(8,128)(2,1)S(1)} all-to-all(bf16[16,128,128]{2,1,0:T(8,128)(2,1)S(1)} %correlate.1), channel_id=1, replica_groups=mesh['seq'=16,'chan'=2] {'seq'}, dimensions={0} | all-to-all | bytes 1048576 | tf_op jit(solution)/shard_map/all_to_all | solution.py:459
  140.7 1.2 fusion.1
  (59 shorter events, 9.5 us)
Async XLA Ops:
  0.6 41.9 %copy-start = (bf16[256,2048]{1,0:T(8,128)(2,1)S(1)}, bf16[256,2048]{1,0:T(8,128)(2,1)}, u32[]{:S(2)}) copy-start(bf16[256,2048]{1,0:T(8,128)(2,1)} %refs_0_.1) | copy-start | bytes 3145732
  0.6 37.7 %collective-permute-start.1 = (bf16[256,2048]{1,0:T(8,128)(2,1)}, bf16[256,2048]{1,0:T(8,128)(2,1)S(1)}, u32[]{:S(2)}, u32[]{:S(2)}) collective-permute-start(bf16[256,2048]{1,0:T(8,128)(2,1)} %refs_0_.1), channel_id=1, source_target_pairs={{0,8},{2,10},{4,12},{6,14},{8,0},{10,2},{12,4},{14,6},{16,24},{18,... | collective-permute-start | bytes 3145736 | tf_op jit(solution)/shard_map/ppermute | solution.py:406
  3.7 34.6 %collective-permute-start = (bf16[256,2048]{1,0:T(8,128)(2,1)}, bf16[256,2048]{1,0:T(8,128)(2,1)S(1)}, u32[]{:S(2)}, u32[]{:S(2)}) collective-permute-start(bf16[256,2048]{1,0:T(8,128)(2,1)} %refs_0_.1), channel_id=1, source_target_pairs={{0,4},{2,6},{4,0},{6,2},{8,12},{10,14},{12,8},{14,10},{16,20},{18,... | collective-permute-start | bytes 3145736 | tf_op jit(solution)/shard_map/ppermute | solution.py:406
  5.2 20.0 %collective-permute-start.4 = (bf16[128,2048]{1,0:T(8,128)(2,1)}, bf16[128,2048]{1,0:T(8,128)(2,1)S(1)}, u32[]{:S(2)}, u32[]{:S(2)}) collective-permute-start(bf16[128,2048]{1,0:T(8,128)(2,1)} %param.15), channel_id=1, source_target_pairs={{0,1},{2,3},{4,5},{6,7},{8,9},{10,11},{12,13},{14,15},{17,16},{19,... | collective-permute-start | bytes 1572872 | tf_op jit(solution)/shard_map/ppermute | solution.py:432
  9.7 2.0 %collective-permute-start.3 = (bf16[64,2048]{1,0:T(8,128)(2,1)S(1)}, bf16[64,2048]{1,0:T(8,128)(2,1)S(1)}, u32[]{:S(2)}, u32[]{:S(2)}) collective-permute-start(bf16[64,2048]{1,0:T(8,128)(2,1)S(1)} %get-tuple-element.21), channel_id=1, source_target_pairs={{1,16},{3,18},{5,20},{7,22},{9,24},{11,26},{13,28},{15,30},{16,1},... | collective-permute-start | bytes 786440 | tf_op jit(solution)/shard_map/ppermute | solution.py:431
  10.4 14.2 %collective-permute-start.2 = (bf16[64,2048]{1,0:T(8,128)(2,1)S(1)}, bf16[64,2048]{1,0:T(8,128)(2,1)}, u32[]{:S(2)}, u32[]{:S(2)}) collective-permute-start(bf16[64,2048]{1,0:T(8,128)(2,1)S(1)} %get-tuple-element.22), channel_id=1, source_target_pairs={{1,17},{3,19},{5,21},{7,23},{9,25},{11,27},{13,29},{15,31},{16,0},... | collective-permute-start | bytes 786440 | tf_op jit(solution)/shard_map/ppermute | solution.py:430
  25.2 14.1 %copy-start.18 = (bf16[128,2048]{1,0:T(8,128)(2,1)}, bf16[128,2048]{1,0:T(8,128)(2,1)S(1)}, u32[]{:S(2)}) copy-start(bf16[128,2048]{1,0:T(8,128)(2,1)S(1)} %collective-permute-done.4) | copy-start | bytes 1572868
  39.5 14.4 %collective-permute-start.9 = (bf16[256,1024]{1,0:T(8,128)(2,1)}, bf16[256,1024]{1,0:T(8,128)(2,1)}, u32[]{:S(2)}, u32[]{:S(2)}) collective-permute-start(bf16[256,1024]{1,0:T(8,128)(2,1)} %slice.14), channel_id=1, source_target_pairs={{0,8},{2,10},{4,12},{6,14},{8,0},{10,2},{12,4},{14,6},{16,24},{18,... | collective-permute-start | bytes 1572872 | tf_op jit(solution)/shard_map/ppermute | solution.py:406
  42.5 19.0 %collective-permute-start.6 = (bf16[256,2048]{1,0:T(8,128)(2,1)S(1)}, bf16[256,2048]{1,0:T(8,128)(2,1)S(1)}, u32[]{:S(2)}, u32[]{:S(2)}) collective-permute-start(bf16[256,2048]{1,0:T(8,128)(2,1)S(1)} %copy-done), channel_id=1, source_target_pairs={{0,2},{2,0},{4,6},{6,4},{8,10},{10,8},{12,14},{14,12},{16,18},{18,... | collective-permute-start | bytes 3145736 | tf_op jit(solution)/shard_map/ppermute | solution.py:406
  42.5 16.1 %copy-start.10 = (bf16[128,2048]{1,0:T(8,128)(2,1)S(1)}, bf16[128,2048]{1,0:T(8,128)(2,1)}, u32[]{:S(2)}) copy-start(bf16[128,2048]{1,0:T(8,128)(2,1)} %param.15) | copy-start | bytes 1572868
  42.5 16.1 %copy-start.19 = (bf16[128,2048]{1,0:T(8,128)(2,1)S(1)}, bf16[128,2048]{1,0:T(8,128)(2,1)}, u32[]{:S(2)}) copy-start(bf16[128,2048]{1,0:T(8,128)(2,1)} %copy-done.18) | copy-start | bytes 1572868
  42.5 19.0 %collective-permute-start.7 = (bf16[256,2048]{1,0:T(8,128)(2,1)S(1)}, bf16[256,2048]{1,0:T(8,128)(2,1)S(1)}, u32[]{:S(2)}, u32[]{:S(2)}) collective-permute-start(bf16[256,2048]{1,0:T(8,128)(2,1)S(1)} %collective-permute-done.refs_2_), channel_id=1, source_target_pairs={{0,2},{2,0},{4,6},{6,4},{8,10},{10,8},{12,14},{14,12},{16,18},{18,... | collective-permute-start | bytes 3145736 | tf_op jit(solution)/shard_map/ppermute | solution.py:406
  44.1 17.5 %collective-permute-start.8 = (bf16[256,2048]{1,0:T(8,128)(2,1)}, bf16[256,2048]{1,0:T(8,128)(2,1)S(1)}, u32[]{:S(2)}, u32[]{:S(2)}) collective-permute-start(bf16[256,2048]{1,0:T(8,128)(2,1)} %copy-done.8), channel_id=1, source_target_pairs={{0,2},{2,0},{4,6},{6,4},{8,10},{10,8},{12,14},{14,12},{16,18},{18,... | collective-permute-start | bytes 3145736 | tf_op jit(solution)/shard_map/ppermute | solution.py:406
  44.3 14.2 %collective-permute-start.10 = (bf16[256,1024]{1,0:T(8,128)(2,1)S(1)}, bf16[256,1024]{1,0:T(8,128)(2,1)S(1)}, u32[]{:S(2)}, u32[]{:S(2)}) collective-permute-start(bf16[256,1024]{1,0:T(8,128)(2,1)S(1)} %slice.15), channel_id=1, source_target_pairs={{0,4},{2,6},{4,0},{6,2},{8,12},{10,14},{12,8},{14,10},{16,20},{18,... | collective-permute-start | bytes 1572872 | tf_op jit(solution)/shard_map/ppermute | solution.py:406
  53.9 6.5 %collective-permute-start.5 = (bf16[64,2048]{1,0:T(8,128)(2,1)S(1)}, bf16[64,2048]{1,0:T(8,128)(2,1)S(1)}, u32[]{:S(2)}, u32[]{:S(2)}) collective-permute-start(bf16[64,2048]{1,0:T(8,128)(2,1)S(1)} %broadcast_select_fusion.3), channel_id=1, source_target_pairs={{0,1},{1,0},{2,3},{3,2},{4,5},{5,4},{6,7},{7,6},{8,9},{9,8},{10,11... | collective-permute-start | bytes 786440 | tf_op jit(solution)/shard_map/ppermute | solution.py:406
  58.6 3.0 %collective-permute-start.11 = (bf16[256,2048]{1,0:T(8,128)(2,1)S(1)}, bf16[256,2048]{1,0:T(8,128)(2,1)S(1)}, u32[]{:S(2)}, u32[]{:S(2)}) collective-permute-start(bf16[256,2048]{1,0:T(8,128)(2,1)S(1)} %constant_dynamic-update-slice_fusion.refs_6_), channel_id=1, source_target_pairs={{0,2},{2,0},{4,6},{6,4},{8,10},{10,8},{12,14},{14,12},{16,18},{18,... | collective-permute-start | bytes 3145736 | tf_op jit(solution)/shard_map/ppermute | solution.py:406
  63.3 30.1 %copy-start.14 = (bf16[2048,128]{1,0:T(8,128)(2,1)S(1)}, bf16[2048,128]{1,0:T(8,128)(2,1)}, u32[]{:S(2)}) copy-start(bf16[2048,128]{1,0:T(8,128)(2,1)} %param.17) | copy-start | bytes 1572868
  63.3 30.1 %copy-start.15 = (bf16[2048,128]{1,0:T(8,128)(2,1)S(1)}, bf16[2048,128]{1,0:T(8,128)(2,1)}, u32[]{:S(2)}) copy-start(bf16[2048,128]{1,0:T(8,128)(2,1)} %param.18) | copy-start | bytes 1572868
  68.7 24.7 %collective-permute-start.12 = (bf16[2048,128]{1,0:T(8,128)(2,1)S(1)}, bf16[2048,128]{1,0:T(8,128)(2,1)S(1)}, u32[]{:S(2)}, u32[]{:S(2)}) collective-permute-start(bf16[2048,128]{1,0:T(8,128)(2,1)S(1)} %get-tuple-element.16), channel_id=1, source_target_pairs={{0,16},{2,18},{4,20},{6,22},{8,24},{10,26},{12,28},{14,30},{16,0},... | collective-permute-start | bytes 1572872 | tf_op jit(solution)/shard_map/ppermute | solution.py:406
  93.4 4.9 %copy-start.2 = (bf16[256,256]{1,0:T(8,128)(2,1)S(1)}, bf16[256,256]{1,0:T(8,128)(2,1)}, u32[]{:S(2)}) copy-start(bf16[256,256]{1,0:T(8,128)(2,1)} %constant.46.clone.low_ref.fl_ref) | copy-start | bytes 393220
  93.4 4.9 %copy-start.3 = (bf16[256,256]{1,0:T(8,128)(2,1)S(1)}, bf16[256,256]{1,0:T(8,128)(2,1)}, u32[]{:S(2)}) copy-start(bf16[256,256]{1,0:T(8,128)(2,1)} %constant.45.clone.high_ref.fh_ref) | copy-start | bytes 393220
  94.6 18.0 %all-to-all-start = ((bf16[16,128,128]{2,1,0:T(8,128)(2,1)}), bf16[16,128,128]{2,1,0:T(8,128)(2,1)S(1)}, u32[]{:S(2)}, u32[]{:S(2)}) async-start(bf16[16,128,128]{2,1,0:T(8,128)(2,1)} %bitcast.1), calls=%async_computation | async-start | bytes 1048576 | tf_op jit(solution)/shard_map/all_to_all | solution.py:455
  115.2 25.5 %copy-start.16 = (bf16[2048,128]{1,0:T(8,128)(2,1)S(1)}, bf16[2048,128]{1,0:T(8,128)(2,1)}, u32[]{:S(2)}) copy-start(bf16[2048,128]{1,0:T(8,128)(2,1)} %param.19) | copy-start | bytes 1572868
  115.2 25.5 %copy-start.17 = (bf16[2048,128]{1,0:T(8,128)(2,1)S(1)}, bf16[2048,128]{1,0:T(8,128)(2,1)}, u32[]{:S(2)}) copy-start(bf16[2048,128]{1,0:T(8,128)(2,1)} %param.20) | copy-start | bytes 1572868
  (10 other events, 16.2 us)

commit v3 on v1

--- a/solution.py
+++ b/solution.py
@@ -9,7 +9,7 @@
 from jax.experimental.pallas import tpu as pltpu
 from jax.sharding import PartitionSpec as P
 
-VMEM_BYTES = 48 * 1024 * 1024
+VMEM_BYTES = 16 * 1024 * 1024
 
 
 def split_table(table):
@@ -131,8 +131,7 @@
     )
 
 
-def to_spectrum(read, twist_ref, high_ref, low_ref, pair_ref, out_ref, blocks, channels, rows):
-    width = twist_ref.shape[2]
+def to_spectrum(read, twist_ref, high_ref, low_ref, pair_ref, spec_ref, blocks, channels, rows):
     for at in range(0, channels, rows):
         parts = [read(i, at).astype(jnp.float32) for i in range(blocks)]
         cosines, sines = real_lines(parts, 2 * blocks)
@@ -144,101 +143,122 @@
             else:
                 new_re, new_im = re * turn_cos - im * turn_sin, -(re * turn_sin + im * turn_cos)
             put_split(pair_ref, k * channels + at, rows, new_re, new_im)
-    out_ref[...] = wide_dot(pair_ref[...], high_ref[...], low_ref[...])
-
-
-def filter_kernel(blocks, rows, taps_ref, twist_ref, high_ref, low_ref, out_ref, pair_ref, spec_ref):
-    channels = taps_ref.shape[0]
-    width = twist_ref.shape[2]
-    to_spectrum(
-        lambda i, at: taps_ref[at : at + rows, i * width : (i + 1) * width],
-        twist_ref, high_ref, low_ref, pair_ref, spec_ref, blocks, channels, rows,
-    )
+    spec_ref[...] = wide_dot(pair_ref[...], high_ref[...], low_ref[...])
+
+
+def each_step(channels, step, body):
+    pl.loop(0, channels // step)(lambda c: body(pl.multiple_of(c * step, step)))
+
+
+def table_fetch(hbm_refs, vmem_refs, sems):
+    copies = [pltpu.make_async_copy(src, dst, sems.at[i]) for i, (src, dst) in enumerate(zip(hbm_refs, vmem_refs))]
+    for copy in copies:
+        copy.start()
+    side = vmem_refs[1].shape[1]
+    return copies, [vmem_refs[1].at[pl.ds(i * side, side)] for i in range(vmem_refs[1].shape[0] // side)]
+
+
+def filter_kernel(blocks, step, rows, taps_ref, twist_hbm, packed_hbm, out_ref, pair_ref, spec_ref, twist_ref, packed_ref, sems):
+    copies, (high_ref, low_ref) = table_fetch((twist_hbm, packed_hbm), (twist_ref, packed_ref), sems)
+    channels, length = taps_ref.shape
+    width = length // blocks
     total = 2 * blocks * width
-    for k in range(blocks + 1):
-        scale = (1.0 if k in (0, blocks) else 2.0) / total
-        out_ref[k] = spec_ref[k * channels : (k + 1) * channels, :] * np.float32(scale)
+    for copy in copies:
+        copy.wait()
+
+    def body(start):
+        to_spectrum(
+            lambda i, at: taps_ref[pl.ds(start + at, rows), i * width : (i + 1) * width],
+            twist_ref, high_ref, low_ref, pair_ref, spec_ref, blocks, step, rows,
+        )
+        for k in range(blocks + 1):
+            scale = (1.0 if k in (0, blocks) else 2.0) / total
+            out_ref[k, pl.ds(start, step)] = spec_ref[k * step : (k + 1) * step, :] * np.float32(scale)
+
+    each_step(channels, step, body)
+
+
+def transform_scratch(blocks, width, step, tables):
+    lines = blocks + 1
+    return [
+        pltpu.VMEM((lines * step, 4 * width), jnp.bfloat16),
+        pltpu.VMEM((lines * step, 2 * width), jnp.float32),
+        pltpu.VMEM((2, lines, width), jnp.float32),
+        pltpu.VMEM((tables * 2 * width, 2 * width), jnp.bfloat16),
+        pltpu.SemaphoreType.DMA((2,)),
+    ]
 
 
 def filter_spectrum(taps, blocks, step):
     channels, length = taps.shape
     width = length // blocks
     twist, forward, _ = dft_constants(blocks, width)
-    lines = blocks + 1
-    whole = lambda *shape: pl.BlockSpec(shape, lambda c: (0,) * len(shape))
+    in_hbm = pl.BlockSpec(memory_space=pltpu.HBM)
+    in_vmem = pl.BlockSpec(memory_space=pltpu.VMEM)
     return pl.pallas_call(
-        functools.partial(filter_kernel, blocks, min(16, step)),
-        grid=(channels // step,),
-        in_specs=[
-            pl.BlockSpec((step, length), lambda c: (c, 0)),
-            whole(2, lines, width), whole(2 * width, 2 * width), whole(2 * width, 2 * width),
-        ],
-        out_specs=pl.BlockSpec((lines, step, 2 * width), lambda c: (0, c, 0)),
-        out_shape=jax.ShapeDtypeStruct((lines, channels, 2 * width), jnp.float32),
-        scratch_shapes=[
-            pltpu.VMEM((lines * step, 4 * width), jnp.bfloat16),
-            pltpu.VMEM((lines * step, 2 * width), jnp.float32),
-        ],
+        functools.partial(filter_kernel, blocks, step, min(16, step)),
+        in_specs=[in_vmem, in_hbm, in_hbm],
+        out_specs=in_vmem,
+        out_shape=jax.ShapeDtypeStruct((blocks + 1, channels, 2 * width), jnp.float32),
+        scratch_shapes=transform_scratch(blocks, width, step, 2),
         compiler_params=pltpu.CompilerParams(vmem_limit_bytes=VMEM_BYTES),
         name="filter_spectrum",
-    )(taps, twist, *forward)
+    )(taps, twist, np.concatenate(forward))
 
 
 def correlate_kernel(
-    blocks, rows, sig_ref, filt_ref, twist_ref, fh_ref, fl_ref, bh_ref, bl_ref, out_ref, pair_ref, spec_ref
+    blocks, step, rows, sig_ref, filt_ref, twist_hbm, packed_hbm, out_ref, pair_ref, spec_ref, twist_ref, packed_ref, sems
 ):
+    copies, (fh_ref, fl_ref, bh_ref, bl_ref) = table_fetch((twist_hbm, packed_hbm), (twist_ref, packed_ref), sems)
     channels, width = sig_ref.shape[1:]
-    to_spectrum(
-        lambda i, at: sig_ref[i, at : at + rows, :],
-        twist_ref, fh_ref, fl_ref, pair_ref, spec_ref, blocks, channels, rows,
-    )
-    for k in range(blocks + 1):
-        for at in range(0, channels, rows):
-            row = k * channels + at
-            sig_re = spec_ref[row : row + rows, :width]
-            sig_im = spec_ref[row : row + rows, width:]
-            filt_re = filt_ref[k, at : at + rows, :width]
-            filt_im = filt_ref[k, at : at + rows, width:]
-            put_split(
-                pair_ref, row, rows,
-                filt_re * sig_re + filt_im * sig_im, filt_re * sig_im - filt_im * sig_re,
-            )
-    spec_ref[...] = wide_dot(pair_ref[...], bh_ref[...], bl_ref[...])
-    for at in range(0, channels, rows):
-        re_lines, im_lines = [], []
+    for copy in copies:
+        copy.wait()
+
+    def body(start):
+        to_spectrum(
+            lambda i, at: sig_ref[i, pl.ds(start + at, rows), :],
+            twist_ref, fh_ref, fl_ref, pair_ref, spec_ref, blocks, step, rows,
+        )
         for k in range(blocks + 1):
-            turn_cos, turn_sin = twist_ref[0, k : k + 1, :], twist_ref[1, k : k + 1, :]
-            row = k * channels + at
-            re, im = spec_ref[row : row + rows, :width], spec_ref[row : row + rows, width:]
-            re_lines.append(re * turn_cos - im * turn_sin)
-            im_lines.append(re * turn_sin + im * turn_cos)
-        for i, value in enumerate(real_parts(re_lines, im_lines, 2 * blocks, blocks)):
-            out_ref[i, at : at + rows, :] = value.astype(jnp.bfloat16)
+            for at in range(0, step, rows):
+                row = k * step + at
+                sig_re = spec_ref[row : row + rows, :width]
+                sig_im = spec_ref[row : row + rows, width:]
+                filt_re = filt_ref[k, pl.ds(start + at, rows), :width]
+                filt_im = filt_ref[k, pl.ds(start + at, rows), width:]
+                put_split(
+                    pair_ref, row, rows,
+                    filt_re * sig_re + filt_im * sig_im, filt_re * sig_im - filt_im * sig_re,
+                )
+        spec_ref[...] = wide_dot(pair_ref[...], bh_ref[...], bl_ref[...])
+        for at in range(0, step, rows):
+            re_lines, im_lines = [], []
+            for k in range(blocks + 1):
+                turn_cos, turn_sin = twist_ref[0, k : k + 1, :], twist_ref[1, k : k + 1, :]
+                row = k * step + at
+                re, im = spec_ref[row : row + rows, :width], spec_ref[row : row + rows, width:]
+                re_lines.append(re * turn_cos - im * turn_sin)
+                im_lines.append(re * turn_sin + im * turn_cos)
+            for i, value in enumerate(real_parts(re_lines, im_lines, 2 * blocks, blocks)):
+                out_ref[i, pl.ds(start + at, rows), :] = value.astype(jnp.bfloat16)
+
+    each_step(channels, step, body)
 
 
 def correlate(signal, spectrum, step):
     blocks, channels, width = signal.shape
     twist, forward, backward = dft_constants(blocks, width)
-    lines = blocks + 1
-    whole = lambda *shape: pl.BlockSpec(shape, lambda c: (0,) * len(shape))
-    table = whole(2 * width, 2 * width)
+    in_hbm = pl.BlockSpec(memory_space=pltpu.HBM)
+    in_vmem = pl.BlockSpec(memory_space=pltpu.VMEM)
     return pl.pallas_call(
-        functools.partial(correlate_kernel, blocks, min(16, step)),
-        grid=(channels // step,),
-        in_specs=[
-            pl.BlockSpec((blocks, step, width), lambda c: (0, c, 0)),
-            pl.BlockSpec((lines, step, 2 * width), lambda c: (0, c, 0)),
-            whole(2, lines, width), table, table, table, table,
-        ],
-        out_specs=pl.BlockSpec((blocks, step, width), lambda c: (0, c, 0)),
+        functools.partial(correlate_kernel, blocks, step, min(16, step)),
+        in_specs=[in_vmem, in_vmem, in_hbm, in_hbm],
+        out_specs=in_vmem,
         out_shape=jax.ShapeDtypeStruct((blocks, channels, width), jnp.bfloat16),
-        scratch_shapes=[
-            pltpu.VMEM((lines * step, 4 * width), jnp.bfloat16),
-            pltpu.VMEM((lines * step, 2 * width), jnp.float32),
-        ],
+        scratch_shapes=transform_scratch(blocks, width, step, 4),
         compiler_params=pltpu.CompilerParams(vmem_limit_bytes=VMEM_BYTES),
         name="correlate",
-    )(signal, spectrum, twist, *forward, *backward)
+    )(signal, spectrum, twist, np.concatenate(forward + backward))
 
 
 def dft_tables(count_outer, count_inner):
@@ -363,43 +383,139 @@
     return (grad_gate, grad_key, grad_value)
 
 
-def mix_kernel(block_rows, slot_ref, grad_ref, *refs):
-    pieces, (own_ref, other_ref) = refs[:-2], refs[-2:]
-    total = None
-    for distance, piece in enumerate(pieces):
-        at = pl.multiple_of((slot_ref[0] ^ distance) * block_rows, block_rows)
-        term = jnp.dot(grad_ref[:, pl.ds(at, block_rows)], piece[...], preferred_element_type=jnp.float32)
-        total = term if total is None else total + term
-    mixed = total.T
-    tokens = own_ref.shape[1]
-    own_ref[...] = mixed[:, :tokens]
-    other_ref[...] = mixed[:, tokens:].astype(jnp.bfloat16)
-
-
-def partial_mix(slot, grads, pieces, step):
-    rows, channels = pieces[0].shape
-    tokens, depth = grads.shape
-    half = tokens // 2
-    out_spec = pl.BlockSpec((step, half), lambda c: (c, 0))
+def share_kernel(rows, flags_ref, own_ref, local_ref, first_ref, second_ref, mine_ref, mine_far_ref, theirs_ref, theirs_far_ref):
+    home, core = flags_ref[0] == 1, flags_ref[1]
+    tokens = own_ref.shape[0]
+
+    def place(near, far):
+        for block in range(own_ref.shape[1] // (2 * rows)):
+            lanes = pl.ds(block * rows, rows)
+            mine = pl.ds(pl.multiple_of((2 * block + core) * rows, rows), rows)
+            theirs = pl.ds(pl.multiple_of((2 * block + 1 - core) * rows, rows), rows)
+            mine_ref[:, lanes] = near[:, mine]
+            mine_far_ref[:, lanes] = far[:, mine]
+            theirs_ref[:tokens, lanes] = near[:, theirs]
+            theirs_ref[tokens:, lanes] = far[:, theirs]
+            theirs_far_ref[:, lanes] = far[:, theirs]
+
+    pl.when(home)(lambda: place(own_ref, first_ref))
+    pl.when(jnp.logical_not(home))(lambda: place(local_ref, second_ref))
+
+
+def share_blocks(flags, rows, own, local, first, second):
+    tokens, features = own.shape
+    part = first.shape[0]
+    whole = lambda a: pl.BlockSpec(a.shape, lambda: (0, 0))
+    shapes = [
+        jax.ShapeDtypeStruct((t, features // 2), own.dtype) for t in (tokens, part, tokens + part, part)
+    ]
     return pl.pallas_call(
-        functools.partial(mix_kernel, rows),
-        grid=(channels // step,),
-        in_specs=[
-            pl.BlockSpec(memory_space=pltpu.SMEM),
-            pl.BlockSpec((tokens, depth), lambda c: (0, 0)),
-        ]
-        + [pl.BlockSpec((rows, step), lambda c: (0, c)) for _ in pieces],
-        out_specs=(out_spec, out_spec),
+        functools.partial(share_kernel, rows),
+        in_specs=[pl.BlockSpec(memory_space=pltpu.SMEM)] + [whole(a) for a in (own, local, first, second)],
+        out_shape=shapes,
+        compiler_params=pltpu.CompilerParams(vmem_limit_bytes=VMEM_BYTES),
+        name="share_blocks",
+    )(flags, own, local, first, second)
+
+
+def mix_kernel(rows, step, flags_ref, mine_ref, mine_far_ref, beside_ref, across_ref, slant_ref, *refs):
+    own_ref, near_ref, far_edge_ref, corner_edge_ref, far_ref, corner_ref, keep_ref, send_ref, grad_ref = refs
+    tokens, part = mine_ref.shape[0], mine_far_ref.shape[0]
+
+    def place(first, second):
+        for distance in range(mine_ref.shape[1] // rows):
+            at = pl.ds(pl.multiple_of((flags_ref[2] ^ distance) * rows, rows), rows)
+            lanes = slice(distance * rows, (distance + 1) * rows)
+            grad_ref[:tokens, lanes] = mine_ref[:, at]
+            grad_ref[tokens + first : tokens + first + part, lanes] = mine_far_ref[:, at]
+            grad_ref[tokens + second : tokens + second + part, lanes] = beside_ref[:, at]
+            grad_ref[2 * tokens : 3 * tokens, lanes] = across_ref[:tokens, at]
+            grad_ref[3 * tokens + first : 3 * tokens + first + part, lanes] = across_ref[tokens:, at]
+            grad_ref[3 * tokens + second : 3 * tokens + second + part, lanes] = slant_ref[:, at]
+
+    pl.when(flags_ref[0] == 1)(lambda: place(0, part))
+    pl.when(flags_ref[0] != 1)(lambda: place(part, 0))
+
+    edge = far_edge_ref.shape[1]
+    for start in range(0, own_ref.shape[1], step):
+        lanes = slice(start, start + step)
+        if start < edge:
+            others = (far_edge_ref[:, lanes], corner_edge_ref[:, lanes])
+        else:
+            others = (far_ref[:, start - edge : start - edge + step], corner_ref[:, start - edge : start - edge + step])
+        weight = jnp.concatenate([own_ref[:, lanes], near_ref[:, lanes], *others], axis=0)
+        total = jnp.dot(grad_ref[...], weight, preferred_element_type=jnp.float32)
+        keep_ref[:, lanes] = total[: 2 * tokens]
+        send_ref[:, lanes] = total[2 * tokens :].astype(jnp.bfloat16)
+
+
+def partial_mix(flags, grads, own, near, far_parts, corner_parts, step):
+    rows, channels = own.shape
+    tokens, depth = grads[0].shape
+    arrays = (*grads, own, near, far_parts[0], corner_parts[0], far_parts[1], corner_parts[1])
+    return pl.pallas_call(
+        functools.partial(mix_kernel, rows, step),
+        in_specs=[pl.BlockSpec(memory_space=pltpu.SMEM)] + [pl.BlockSpec(memory_space=pltpu.VMEM) for _ in arrays],
+        out_specs=(pl.BlockSpec(memory_space=pltpu.VMEM), pl.BlockSpec(memory_space=pltpu.VMEM)),
         out_shape=(
-            jax.ShapeDtypeStruct((channels, half), jnp.float32),
-            jax.ShapeDtypeStruct((channels, half), jnp.bfloat16),
+            jax.ShapeDtypeStruct((2 * tokens, channels), jnp.float32),
+            jax.ShapeDtypeStruct((2 * tokens, channels), jnp.bfloat16),
         ),
+        scratch_shapes=[pltpu.VMEM((4 * tokens, depth), jnp.bfloat16)],
         compiler_params=pltpu.CompilerParams(vmem_limit_bytes=VMEM_BYTES),
         cost_estimate=pl.CostEstimate(
-            flops=2 * tokens * depth * channels, bytes_accessed=2 * depth * (channels + tokens), transcendentals=0
+            flops=8 * tokens * depth * channels, bytes_accessed=2 * depth * (channels + tokens), transcendentals=0
         ),
         name="partial_mix",
-    )(slot, grads, *pieces)
+    )(flags, *arrays)
+
+
+def gate_kernel(step, keep_ref, near_ref, far_ref, gate_ref, conv_ref, gated_ref, out_ref):
+    tokens = far_ref.shape[0]
+    for start in range(0, gate_ref.shape[0], step):
+        at = slice(start, start + step)
+        near = near_ref[:tokens, at].astype(jnp.float32)
+        far = far_ref[:, at].astype(jnp.float32)
+        mix = (keep_ref[:tokens, at] + near + far).T
+        gated_ref[at] = (mix * gate_ref[at].astype(jnp.float32)).astype(jnp.bfloat16)
+        out_ref[at] = (mix * conv_ref[at].astype(jnp.float32)).astype(jnp.bfloat16)
+
+
+def gate_mix(keep, near, far, gate, conv, step):
+    channels, tokens = gate.shape
+    whole = pl.BlockSpec(memory_space=pltpu.VMEM)
+    shape = jax.ShapeDtypeStruct((channels, tokens), jnp.bfloat16)
+    return pl.pallas_call(
+        functools.partial(gate_kernel, step),
+        in_specs=[whole] * 5,
+        out_specs=(whole, whole),
+        out_shape=(shape, shape),
+        compiler_params=pltpu.CompilerParams(vmem_limit_bytes=VMEM_BYTES),
+        cost_estimate=pl.CostEstimate(flops=0, bytes_accessed=16 * channels * tokens, transcendentals=0),
+        name="gate_mix",
+    )(keep, near, far, gate, conv)
+
+
+def output_kernel(inner_ref, value_ref, key_ref, grad_key_ref, grad_value_ref):
+    inner = inner_ref[...].astype(jnp.float32)
+    grad_key_ref[...] = (inner * value_ref[...].astype(jnp.float32)).astype(jnp.bfloat16)
+    grad_value_ref[...] = (inner * key_ref[...].astype(jnp.float32)).astype(jnp.bfloat16)
+
+
+def output_products(inner, value, key):
+    channels, tokens = value.shape
+    steps = 2
+    block = pl.BlockSpec((channels // steps, tokens), lambda g: (g, 0))
+    shape = jax.ShapeDtypeStruct(value.shape, jnp.bfloat16)
+    return pl.pallas_call(
+        output_kernel,
+        grid=(steps,),
+        in_specs=[block, block, block],
+        out_specs=(block, block),
+        out_shape=(shape, shape),
+        compiler_params=pltpu.CompilerParams(vmem_limit_bytes=VMEM_BYTES),
+        name="output_products",
+    )(inner, value, key)
 
 
 def swap(values, axis, count, mask):
@@ -416,42 +532,47 @@
     group = seq_count // 2
     place = lax.axis_index("seq")
     side = place // group
-    spectrum = filter_spectrum(long_filter, seq_count, min(16, group_width))
+    core = place % 2
+    near, far = 2, 4
+    hop = lambda values, mask: swap(values, "seq", seq_count, mask)
+
+    spectrum = filter_spectrum(long_filter, seq_count, min(32, group_width))
 
     shard = lax.axis_index("chan")
-    peer_grad = swap(grad_out, "chan", 2, 1)
-    mine, theirs = (
-        jnp.where(shard == want, grad_out, peer_grad) for want in (side, 1 - side)
-    )
-    peer_tokens = swap(theirs, "seq", seq_count, group)
-    grads = jnp.concatenate([mine, peer_tokens], axis=0)
-
-    half = chan_width // 2
-    near, far = 2, 4
-    across = swap(out_weight, "seq", seq_count, near)
-    along = swap(out_weight, "seq", seq_count, far)
-    corner_a = swap(across[:, :half], "seq", seq_count, far)
-    corner_b = swap(along[:, half:], "seq", seq_count, near)
-    corner = jnp.concatenate([corner_a, corner_b], axis=1)
-    same = [out_weight, across, along, corner]
-    pieces = []
-    for piece in same:
-        pieces += [piece, swap(piece, "seq", seq_count, 1)]
-    slot = (place % group).reshape(1).astype(jnp.int32)
-    own, other = partial_mix(slot, grads, pieces, min(512, chan_width))
-    received = swap(other, "seq", seq_count, group)
-    grad_mix = own + received.astype(jnp.float32)
-
-    gated_grad = (grad_mix * gate_stream.astype(jnp.float32)).astype(jnp.bfloat16)
+    home = shard == side
+    flags = jnp.stack([home.astype(jnp.int32), core.astype(jnp.int32), (place % group // 2).astype(jnp.int32)])
+    part = token_count // 2
+    both = ("seq", "chan")
+    at = lambda s, y: s * 2 + y
+    away = [(s, 1 - s // group) for s in range(seq_count)]
+    first = lax.ppermute(grad_out[:part], both, [(at(s, y), at(s ^ group, y)) for s, y in away])
+    second = lax.ppermute(grad_out[part:], both, [(at(s, y), at(s ^ group, 1 - y)) for s, y in away])
+    local = lax.ppermute(grad_out, both, [(at(s, 1 - y), at(s, y)) for s, y in away])
+
+    lead = chan_width // 8 * 3
+    edge, rest = out_weight[:, :lead], out_weight[:, lead:]
+    near_all, far_rest = hop(out_weight, near), hop(rest, far)
+    far_edge, corner_edge, corner_rest = hop(edge, far), hop(near_all[:, :lead], far), hop(far_rest, near)
+
+    mine, mine_far, theirs, theirs_far = share_blocks(flags, weight_rows, grad_out, local, first, second)
+    beside = swap(mine_far, "chan", 2, 1)
+    across = hop(theirs, 1)
+    slant = lax.ppermute(
+        theirs_far, both, [(at(s, y), at(s ^ 1, 1 - y)) for s in range(seq_count) for y in range(2)]
+    )
+    keep, send = partial_mix(
+        flags, (mine, mine_far, beside, across, slant),
+        out_weight, near_all, (far_edge, far_rest), (corner_edge, corner_rest), chan_width // 8,
+    )
+    given = hop(send, 1)
+    over = hop((keep[token_count:] + given[token_count:].astype(jnp.float32)).astype(jnp.bfloat16), group)
+    gated, grad_gate = gate_mix(keep, given, over, gate_stream, conv_output, chan_width // 4)
     regrouped = lax.all_to_all(
-        gated_grad.reshape(seq_count, group_width, token_count), "seq", split_axis=0, concat_axis=0, tiled=True
-    )
-    inner_grad = correlate(regrouped, spectrum, min(16, group_width))
-    returned = lax.all_to_all(inner_grad, "seq", split_axis=0, concat_axis=0, tiled=True)
-    grad_inner = returned.reshape(chan_width, token_count).astype(jnp.float32)
-    grad_gate = (grad_mix * conv_output.astype(jnp.float32)).astype(jnp.bfloat16)
-    grad_key = (grad_inner * value_stream.astype(jnp.float32)).astype(jnp.bfloat16)
-    grad_value = (grad_inner * key_stream.astype(jnp.float32)).astype(jnp.bfloat16)
+        gated.reshape(seq_count, group_width, token_count), "seq", split_axis=0, concat_axis=0, tiled=True
+    )
+    inner = correlate(regrouped, spectrum, min(32, group_width))
+    returned = lax.all_to_all(inner, "seq", split_axis=0, concat_axis=0, tiled=True)
+    grad_key, grad_value = output_products(returned.reshape(chan_width, token_count), value_stream, key_stream)
     return (grad_gate, grad_key, grad_value)
 
 

time: 156 us -> 131 us (0.84)
  waiting for transfers between devices: 90 us -> 74.6 us
  other arithmetic: 5.86 us -> 0.2 us
  starting transfers between devices: 17 us -> 14.5 us
    ppermute x11 -> x9, waiting for transfers between devices: 79.4 us -> 57.5 us  [swap(): return lax.ppermute(values, axis, [(i, i ^ mask) for i in range(count)])]
    ppermute x11 -> x9, starting transfers between devices: 12.6 us -> 5.4 us  [swap(): return lax.ppermute(values, axis, [(i, i ^ mask) for i in range(count)])]
    ppermute x0 -> x4, waiting for transfers between devices: none -> 5.93 us  [the longest x1 5.92 us: per_device(): lax.ppermute(grad_out[:part], both, [(at(s, y), at(s ^ group, y)) for s,...]
    ppermute x0 -> x4, starting transfers between devices: none -> 5.49 us  [the longest x1 3.45 us: per_device(): lax.ppermute(grad_out, both, [(at(s, 1 - y), at(s, y)) for s, y in away])]
    convert_element_type x2 -> x1, other arithmetic: 2.48 us -> 0.12 us  [per_device(): (keep[token_count:] + given[token_count:].astype(jnp.float32)).astype(jnp...]
    select_n x1 -> x0, other arithmetic: 2.08 us -> none  [per_device(): jnp.where(shard == want, grad_out, peer_grad)]
    unnamed x27 -> x22, local copies, waits for them, and re-layouts: 4.17 us -> 2.56 us
    slice x2 -> x4, local copies, waits for them, and re-layouts: 2.71 us -> 4.04 us  [the longest x2 1.95 us: per_device(): edge, rest = (out_weight[:, :lead], out_weight[:, lead:])]
  transfers between devices with their start and end apart: 12 -> 14, of which waited for: 7 -> 8; matrix products, arithmetic and copies ran while one was open for 5% -> 3% of each run, Pallas kernels for 2% -> 2%
where the time goes in v3:
time: 131 us
  waiting for transfers between devices  74.6 us (57%)
  blocking collectives  18.3 us (14%)
  Pallas kernels  15.5 us (12%)
  starting transfers between devices  14.5 us (11%)
  local copies, waits for them, and re-layouts  6.6 us (5%)
    ppermute x9, waiting for transfers between devices, swap(): return lax.ppermute(values, axis, [(i, i ^ mask) for i in range(count)])  57.5 us
    all_to_all x1, blocking collectives, per_device(): lax.all_to_all(inner, 'seq', split_axis=0, concat_axis=0, tiled=True)  18.3 us
    all_to_all x1, waiting for transfers between devices, per_device(): lax.all_to_all(gated.reshape(seq_count, group_width, token_count), 'seq',...  11.1 us
    ppermute x1, waiting for transfers between devices, per_device(): lax.ppermute(grad_out[:part], both, [(at(s, y), at(s ^ group, y)) for s,...  5.92 us
    pallas_call x1, Pallas kernels, correlate(): pl.pallas_call(functools.partial(correlate_kernel, blocks, step, min(16,...  5.91 us
    ppermute x9, starting transfers between devices, swap(): return lax.ppermute(values, axis, [(i, i ^ mask) for i in range(count)])  5.4 us
    pallas_call x1, Pallas kernels, partial_mix(): pl.pallas_call(functools.partial(mix_kernel, rows, step), in_specs=[pl.Bl...  4.02 us
    all_to_all x1, starting transfers between devices, per_device(): lax.all_to_all(gated.reshape(seq_count, group_width, token_count), 'seq',...  3.57 us
  transfers between devices with their start and end apart: 14, of which 8 were waited for; matrix products, arithmetic and copies ran while one was open for 3% of the time, Pallas kernels for 2%

profile of v3, /device:TPU:0, one launch (start us, length us, event | category | flops | bytes accessed | tf_op | source)
XLA Modules:
  0.0 130.5 jit_solution(2849590675772888720)
XLA Ops:
  0.7 3.0 %collective-permute-start.6 = (bf16[256,2048]{1,0:T(8,128)(2,1)}, bf16[256,2048]{1,0:T(8,128)(2,1)}, u32[]{:S(2)}, u32[]{:S(2)}) collective-permute-start(bf16[256,2048]{1,0:T(8,128)(2,1)} %refs_0_.1), channel_id=1, source_target_pairs={{0,4},{2,6},{4,0},{6,2},{8,12},{10,14},{12,8},{14,10},{16,20},{18,... | collective-permute-start | bytes 3145736 | tf_op jit(solution)/shard_map/ppermute | solution.py:522
  3.7 1.2 slice.25
  4.8 1.6 %collective-permute-start.9 = (bf16[256,1280]{1,0:T(8,128)(2,1)S(1)}, bf16[256,1280]{1,0:T(8,128)(2,1)S(1)}, u32[]{:S(2)}, u32[]{:S(2)}) collective-permute-start(bf16[256,1280]{1,0:T(8,128)(2,1)S(1)} %slice.25), channel_id=1, source_target_pairs={{0,8},{2,10},{4,12},{6,14},{8,0},{10,2},{12,4},{14,6},{16,24},{18,... | collective-permute-start | bytes 1966088 | tf_op jit(solution)/shard_map/ppermute | solution.py:522
  6.5 3.4 %collective-permute-start = (bf16[128,2048]{1,0:T(8,128)(2,1)}, bf16[128,2048]{1,0:T(8,128)(2,1)S(1)}, u32[]{:S(2)}, u32[]{:S(2)}) collective-permute-start(bf16[128,2048]{1,0:T(8,128)(2,1)} %own_ref.1), channel_id=1, source_target_pairs={{0,1},{2,3},{4,5},{6,7},{8,9},{10,11},{12,13},{14,15},{17,16},{19,... | collective-permute-start | bytes 1572872 | tf_op jit(solution)/shard_map/ppermute | solution.py:550
  9.9 1.1 fusion
  11.7 1.3 collective-permute-start.1
  13.0 16.8 %collective-permute-done.9.refs_4_ = bf16[256,1280]{1,0:T(8,128)(2,1)S(1)} collective-permute-done((bf16[256,1280]{1,0:T(8,128)(2,1)S(1)}, bf16[256,1280]{1,0:T(8,128)(2,1)S(1)}, u32[]{:S(2)}, u32[]{:S(2)}) %collective-permute-start.9) | collective-permute-done | bytes 655392 | tf_op jit(solution)/shard_map/ppermute | solution.py:522
  30.3 0.8 slice.23
  31.1 5.9 %collective-permute-done.1.first_ref = bf16[64,2048]{1,0:T(8,128)(2,1)S(1)} collective-permute-done((bf16[64,2048]{1,0:T(8,128)(2,1)S(1)}, bf16[64,2048]{1,0:T(8,128)(2,1)S(1)}, u32[]{:S(2)}, u32[]{:S(2)}) %collective-permute-start.1) | collective-permute-done | bytes 262176 | tf_op jit(solution)/shard_map/ppermute | solution.py:548
  37.8 1.0 slice.28
  39.0 6.0 %collective-permute-done.7.refs_2_ = bf16[256,768]{1,0:T(8,128)(2,1)} collective-permute-done((bf16[256,768]{1,0:T(8,128)(2,1)}, bf16[256,768]{1,0:T(8,128)(2,1)}, u32[]{:S(2)}, u32[]{:S(2)}) %collective-permute-start.7) | collective-permute-done | bytes 393248 | tf_op jit(solution)/shard_map/ppermute | solution.py:522
  45.0 5.0 %collective-permute-done.3.beside_ref = bf16[64,1024]{1,0:T(8,128)(2,1)S(1)} collective-permute-done((bf16[64,1024]{1,0:T(8,128)(2,1)S(1)}, bf16[64,1024]{1,0:T(8,128)(2,1)S(1)}, u32[]{:S(2)}, u32[]{:S(2)}) %collective-permute-start.3) | collective-permute-done | bytes 131104 | tf_op jit(solution)/shard_map/ppermute | solution.py:522
  50.0 2.0 %collective-permute-done.8.refs_3_ = bf16[256,768]{1,0:T(8,128)(2,1)S(1)} collective-permute-done((bf16[256,768]{1,0:T(8,128)(2,1)S(1)}, bf16[256,768]{1,0:T(8,128)(2,1)S(1)}, u32[]{:S(2)}, u32[]{:S(2)}) %collective-permute-start.8) | collective-permute-done | bytes 393248 | tf_op jit(solution)/shard_map/ppermute | solution.py:522
  52.0 4.0 %partial_mix.1 = (f32[256,2048]{1,0:T(8,128)S(1)}, bf16[256,2048]{1,0:T(8,128)(2,1)S(1)}) custom-call(s32[3]{0:T(128)S(1)} %pad_add_fusion.flags_ref, bf16[128,1024]{1,0:T(8,128)(2,1)S(1)} %get-tuple-element.13.mine_ref, bf16[64,1024]{1,0:T(8,128)(2,1)S(1)} %get-tuple-element.14.mine_far_ref, bf16[64,1024]{1,0:T(8,128)(2,1)S(1)} %collective-permute-done.3.beside_ref, ...), custom_call_target="tpu_custom_call" | custom-call | flops 2147483648 | bytes 4456448 | tf_op jit(solution)/shard_map/partial_mix/pallas_call | solution.py:456
  56.1 2.6 %collective-permute-done.11.near_ref = bf16[256,2048]{1,0:T(8,128)(2,1)S(1)} collective-permute-done((bf16[256,2048]{1,0:T(8,128)(2,1)S(1)}, bf16[256,2048]{1,0:T(8,128)(2,1)S(1)}, u32[]{:S(2)}, u32[]{:S(2)}) %collective-permute-start.11) | collective-permute-done | bytes 1048608 | tf_op jit(solution)/shard_map/ppermute | solution.py:522
  59.0 25.1 %collective-permute-done.12.far_ref = bf16[128,2048]{1,0:T(8,128)(2,1)S(1)} collective-permute-done((bf16[128,2048]{1,0:T(8,128)(2,1)S(1)}, bf16[128,2048]{1,0:T(8,128)(2,1)S(1)}, u32[]{:S(2)}, u32[]{:S(2)}) %collective-permute-start.12) | collective-permute-done | bytes 524320 | tf_op jit(solution)/shard_map/ppermute | solution.py:522
  84.1 1.4 %gate_mix.1 = (bf16[2048,128]{1,0:T(8,128)(2,1)}, bf16[2048,128]{1,0:T(8,128)(2,1)}) custom-call(f32[256,2048]{1,0:T(8,128)S(1)} %get-tuple-element.17.keep_ref, bf16[256,2048]{1,0:T(8,128)(2,1)S(1)} %collective-permute-done.11.near_ref, bf16[128,2048]{1,0:T(8,128)(2,1)S(1)} %collective-permute-done.12.far_ref, bf16[2048,128]{1,0:T(8,128)(2,1)S(1)} %copy-done.2, ...), custom_call_target="tpu_custom_call" | custom-call | bytes 4194304 | tf_op jit(solution)/shard_map/gate_mix/pallas_call | solution.py:488
  85.5 3.6 %all-to-all-start = ((bf16[16,128,128]{2,1,0:T(8,128)(2,1)}), bf16[16,128,128]{2,1,0:T(8,128)(2,1)S(1)}, u32[]{:S(2)}, u32[]{:S(2)}) async-start(bf16[16,128,128]{2,1,0:T(8,128)(2,1)} %bitcast.3), calls=%async_computation | async-start | bytes 1048576 | tf_op jit(solution)/shard_map/all_to_all | solution.py:570
  89.8 2.5 %filter_spectrum.1.filt_ref = f32[17,128,256]{2,1,0:T(8,128)S(1)} custom-call(bf16[128,2048]{1,0:T(8,128)(2,1)S(1)} %copy-done.6, f32[2,17,128]{2,1,0:T(8,128)S(1)} %copy-done.9, bf16[512,256]{1,0:T(8,128)(2,1)S(1)} %copy-done.8), custom_call_target="tpu_custom_call" | custom-call | tf_op jit(solution)/shard_map/filter_spectrum/pallas_call | solution.py:198
  92.3 11.1 %all-to-all-done.sig_ref = bf16[16,128,128]{2,1,0:T(8,128)(2,1)S(1)} async-done(((bf16[16,128,128]{2,1,0:T(8,128)(2,1)}), bf16[16,128,128]{2,1,0:T(8,128)(2,1)S(1)}, u32[]{:S(2)}, u32[]{:S(2)}) %all-to-all-start) | async-done | bytes 524320 | tf_op jit(solution)/shard_map/all_to_all | solution.py:570
  103.5 1.0 copy-done.7
  105.2 5.9 %correlate.1 = bf16[16,128,128]{2,1,0:T(8,128)(2,1)S(1)} custom-call(bf16[16,128,128]{2,1,0:T(8,128)(2,1)S(1)} %all-to-all-done.sig_ref, f32[17,128,256]{2,1,0:T(8,128)S(1)} %filter_spectrum.1.filt_ref, f32[2,17,128]{2,1,0:T(8,128)S(1)} %copy-done.10, bf16[1024,256]{1,0:T(8,128)(2,1)S(1)} %copy-done.7), custom_call_target="tpu_custom_call" | custom-call | tf_op jit(solution)/shard_map/correlate/pallas_call | solution.py:253
  111.2 18.3 %all_to_all.10 = bf16[16,128,128]{2,1,0:T(8,128)(2,1)S(1)} all-to-all(bf16[16,128,128]{2,1,0:T(8,128)(2,1)S(1)} %correlate.1), channel_id=1, replica_groups=mesh['seq'=16,'chan'=2] {'seq'}, dimensions={0} | all-to-all | bytes 1048576 | tf_op jit(solution)/shard_map/all_to_all | solution.py:574
  129.5 1.0 output_products.1
  (39 shorter events, 3.9 us)
Async XLA Ops:
  0.6 29.6 %copy-start.1 = (bf16[256,2048]{1,0:T(8,128)(2,1)S(1)}, bf16[256,2048]{1,0:T(8,128)(2,1)}, u32[]{:S(2)}) copy-start(bf16[256,2048]{1,0:T(8,128)(2,1)} %refs_0_.1) | copy-start | bytes 3145732
  0.6 36.4 %copy-start = (bf16[128,2048]{1,0:T(8,128)(2,1)S(1)}, bf16[128,2048]{1,0:T(8,128)(2,1)}, u32[]{:S(2)}) copy-start(bf16[128,2048]{1,0:T(8,128)(2,1)} %own_ref.1) | copy-start | bytes 1572868
  0.7 37.2 %collective-permute-start.6 = (bf16[256,2048]{1,0:T(8,128)(2,1)}, bf16[256,2048]{1,0:T(8,128)(2,1)}, u32[]{:S(2)}, u32[]{:S(2)}) collective-permute-start(bf16[256,2048]{1,0:T(8,128)(2,1)} %refs_0_.1), channel_id=1, source_target_pairs={{0,4},{2,6},{4,0},{6,2},{8,12},{10,14},{12,8},{14,10},{16,20},{18,... | collective-permute-start | bytes 3145736 | tf_op jit(solution)/shard_map/ppermute | solution.py:522
  4.8 25.0 %collective-permute-start.9 = (bf16[256,1280]{1,0:T(8,128)(2,1)S(1)}, bf16[256,1280]{1,0:T(8,128)(2,1)S(1)}, u32[]{:S(2)}, u32[]{:S(2)}) collective-permute-start(bf16[256,1280]{1,0:T(8,128)(2,1)S(1)} %slice.25), channel_id=1, source_target_pairs={{0,8},{2,10},{4,12},{6,14},{8,0},{10,2},{12,4},{14,6},{16,24},{18,... | collective-permute-start | bytes 1966088 | tf_op jit(solution)/shard_map/ppermute | solution.py:522
  6.5 30.6 %collective-permute-start = (bf16[128,2048]{1,0:T(8,128)(2,1)}, bf16[128,2048]{1,0:T(8,128)(2,1)S(1)}, u32[]{:S(2)}, u32[]{:S(2)}) collective-permute-start(bf16[128,2048]{1,0:T(8,128)(2,1)} %own_ref.1), channel_id=1, source_target_pairs={{0,1},{2,3},{4,5},{6,7},{8,9},{10,11},{12,13},{14,15},{17,16},{19,... | collective-permute-start | bytes 1572872 | tf_op jit(solution)/shard_map/ppermute | solution.py:550
  11.0 20.1 %collective-permute-start.2 = (bf16[64,2048]{1,0:T(8,128)(2,1)S(1)}, bf16[64,2048]{1,0:T(8,128)(2,1)S(1)}, u32[]{:S(2)}, u32[]{:S(2)}) collective-permute-start(bf16[64,2048]{1,0:T(8,128)(2,1)S(1)} %get-tuple-element.23), channel_id=1, source_target_pairs={{1,16},{3,18},{5,20},{7,22},{9,24},{11,26},{13,28},{15,30},{16,1},... | collective-permute-start | bytes 786440 | tf_op jit(solution)/shard_map/ppermute | solution.py:549
  11.7 25.4 %collective-permute-start.1 = (bf16[64,2048]{1,0:T(8,128)(2,1)S(1)}, bf16[64,2048]{1,0:T(8,128)(2,1)S(1)}, u32[]{:S(2)}, u32[]{:S(2)}) collective-permute-start(bf16[64,2048]{1,0:T(8,128)(2,1)S(1)} %get-tuple-element.24), channel_id=1, source_target_pairs={{1,17},{3,19},{5,21},{7,23},{9,25},{11,27},{13,29},{15,31},{16,0},... | collective-permute-start | bytes 786440 | tf_op jit(solution)/shard_map/ppermute | solution.py:548
  29.8 20.2 %collective-permute-start.10 = (bf16[256,1280]{1,0:T(8,128)(2,1)S(1)}, bf16[256,1280]{1,0:T(8,128)(2,1)}, u32[]{:S(2)}, u32[]{:S(2)}) collective-permute-start(bf16[256,1280]{1,0:T(8,128)(2,1)S(1)} %collective-permute-done.9.refs_4_), channel_id=1, source_target_pairs={{0,4},{2,6},{4,0},{6,2},{8,12},{10,14},{12,8},{14,10},{16,20},{18,... | collective-permute-start | bytes 1966088 | tf_op jit(solution)/shard_map/ppermute | solution.py:522
  31.1 14.0 %collective-permute-start.7 = (bf16[256,768]{1,0:T(8,128)(2,1)}, bf16[256,768]{1,0:T(8,128)(2,1)}, u32[]{:S(2)}, u32[]{:S(2)}) collective-permute-start(bf16[256,768]{1,0:T(8,128)(2,1)} %slice.23), channel_id=1, source_target_pairs={{0,8},{2,10},{4,12},{6,14},{8,0},{10,2},{12,4},{14,6},{16,24},{18,... | collective-permute-start | bytes 1179656 | tf_op jit(solution)/shard_map/ppermute | solution.py:522
  37.7 12.3 %collective-permute-start.4 = (bf16[192,1024]{1,0:T(8,128)(2,1)S(1)}, bf16[192,1024]{1,0:T(8,128)(2,1)S(1)}, u32[]{:S(2)}, u32[]{:S(2)}) collective-permute-start(bf16[192,1024]{1,0:T(8,128)(2,1)S(1)} %get-tuple-element.15), channel_id=1, source_target_pairs={{0,2},{2,0},{4,6},{6,4},{8,10},{10,8},{12,14},{14,12},{16,18},{18,... | collective-permute-start | bytes 1179656 | tf_op jit(solution)/shard_map/ppermute | solution.py:522
  38.9 13.2 %collective-permute-start.8 = (bf16[256,768]{1,0:T(8,128)(2,1)S(1)}, bf16[256,768]{1,0:T(8,128)(2,1)S(1)}, u32[]{:S(2)}, u32[]{:S(2)}) collective-permute-start(bf16[256,768]{1,0:T(8,128)(2,1)S(1)} %slice.28), channel_id=1, source_target_pairs={{0,8},{2,10},{4,12},{6,14},{8,0},{10,2},{12,4},{14,6},{16,24},{18,... | collective-permute-start | bytes 1179656 | tf_op jit(solution)/shard_map/ppermute | solution.py:522
  38.9 6.1 %collective-permute-start.5 = (bf16[64,1024]{1,0:T(8,128)(2,1)S(1)}, bf16[64,1024]{1,0:T(8,128)(2,1)S(1)}, u32[]{:S(2)}, u32[]{:S(2)}) collective-permute-start(bf16[64,1024]{1,0:T(8,128)(2,1)S(1)} %get-tuple-element.16), channel_id=1, source_target_pairs={{0,3},{1,2},{2,1},{3,0},{4,7},{5,6},{6,5},{7,4},{8,11},{9,10},{10,... | collective-permute-start | bytes 393224 | tf_op jit(solution)/shard_map/ppermute | solution.py:560
  45.0 5.0 %collective-permute-start.3 = (bf16[64,1024]{1,0:T(8,128)(2,1)S(1)}, bf16[64,1024]{1,0:T(8,128)(2,1)S(1)}, u32[]{:S(2)}, u32[]{:S(2)}) collective-permute-start(bf16[64,1024]{1,0:T(8,128)(2,1)S(1)} %get-tuple-element.14.mine_far_ref), channel_id=1, source_target_pairs={{0,1},{1,0},{2,3},{3,2},{4,5},{5,4},{6,7},{7,6},{8,9},{9,8},{10,11... | collective-permute-start | bytes 393224 | tf_op jit(solution)/shard_map/ppermute | solution.py:522
  56.0 28.1 %copy-start.2 = (bf16[2048,128]{1,0:T(8,128)(2,1)S(1)}, bf16[2048,128]{1,0:T(8,128)(2,1)}, u32[]{:S(2)}) copy-start(bf16[2048,128]{1,0:T(8,128)(2,1)} %gate_ref.1) | copy-start | bytes 1572868
  56.1 28.0 %copy-start.3 = (bf16[2048,128]{1,0:T(8,128)(2,1)S(1)}, bf16[2048,128]{1,0:T(8,128)(2,1)}, u32[]{:S(2)}) copy-start(bf16[2048,128]{1,0:T(8,128)(2,1)} %conv_ref.1) | copy-start | bytes 1572868
  56.1 2.7 %collective-permute-start.11 = (bf16[256,2048]{1,0:T(8,128)(2,1)S(1)}, bf16[256,2048]{1,0:T(8,128)(2,1)S(1)}, u32[]{:S(2)}, u32[]{:S(2)}) collective-permute-start(bf16[256,2048]{1,0:T(8,128)(2,1)S(1)} %get-tuple-element.18), channel_id=1, source_target_pairs={{0,2},{2,0},{4,6},{6,4},{8,10},{10,8},{12,14},{14,12},{16,18},{18,... | collective-permute-start | bytes 3145736 | tf_op jit(solution)/shard_map/ppermute | solution.py:522
  58.9 30.1 %copy-start.6 = (bf16[128,2048]{1,0:T(8,128)(2,1)S(1)}, bf16[128,2048]{1,0:T(8,128)(2,1)}, u32[]{:S(2)}) copy-start(bf16[128,2048]{1,0:T(8,128)(2,1)} %taps_ref.1) | copy-start | bytes 1572868
  58.9 30.1 %copy-start.8 = (bf16[512,256]{1,0:T(8,128)(2,1)S(1)}, bf16[512,256]{1,0:T(8,128)(2,1)}, u32[]{:S(2)}) copy-start(bf16[512,256]{1,0:T(8,128)(2,1)} %constant.58.clone.packed_hbm) | copy-start | bytes 786436
  58.9 25.1 %collective-permute-start.12 = (bf16[128,2048]{1,0:T(8,128)(2,1)S(1)}, bf16[128,2048]{1,0:T(8,128)(2,1)S(1)}, u32[]{:S(2)}, u32[]{:S(2)}) collective-permute-start(bf16[128,2048]{1,0:T(8,128)(2,1)S(1)} %add_convert_fusion), channel_id=1, source_target_pairs={{0,16},{2,18},{4,20},{6,22},{8,24},{10,26},{12,28},{14,30},{16,0},... | collective-permute-start | bytes 1572872 | tf_op jit(solution)/shard_map/ppermute | solution.py:522
  85.5 18.0 %all-to-all-start = ((bf16[16,128,128]{2,1,0:T(8,128)(2,1)}), bf16[16,128,128]{2,1,0:T(8,128)(2,1)S(1)}, u32[]{:S(2)}, u32[]{:S(2)}) async-start(bf16[16,128,128]{2,1,0:T(8,128)(2,1)} %bitcast.3), calls=%async_computation | async-start | bytes 1048576 | tf_op jit(solution)/shard_map/all_to_all | solution.py:570
  89.1 0.7 copy-start.9
  92.3 37.1 %copy-start.4 = (bf16[2048,128]{1,0:T(8,128)(2,1)S(1)}, bf16[2048,128]{1,0:T(8,128)(2,1)}, u32[]{:S(2)}) copy-start(bf16[2048,128]{1,0:T(8,128)(2,1)} %value_ref.1) | copy-start | bytes 1572868
  103.5 1.0 copy-start.7
  105.2 24.2 %copy-start.5 = (bf16[2048,128]{1,0:T(8,128)(2,1)S(1)}, bf16[2048,128]{1,0:T(8,128)(2,1)}, u32[]{:S(2)}) copy-start(bf16[2048,128]{1,0:T(8,128)(2,1)} %key_ref.1) | copy-start | bytes 1572868
  (1 other events, 0.7 us)

commit v4 on v3

--- a/solution.py
+++ b/solution.py
@@ -1,4 +1,5 @@
 import functools
+import itertools
 import math
 
 import jax
@@ -10,12 +11,6 @@
 from jax.sharding import PartitionSpec as P
 
 VMEM_BYTES = 16 * 1024 * 1024
-
-
-def split_table(table):
-    high = table.astype(jnp.bfloat16)
-    low = (table.astype(np.float32) - high.astype(np.float32)).astype(jnp.bfloat16)
-    return high, low
 
 
 def dft_constants(blocks, width):
@@ -28,7 +23,7 @@
     forward = np.block([[cos, -sin], [sin, cos]]).astype(np.float32)
     backward = np.block([[cos, sin], [-sin, cos]]).astype(np.float32)
     twist = np.stack([np.cos(twist), np.sin(twist)]).astype(np.float32)
-    return twist, split_table(forward), split_table(backward)
+    return twist, forward, backward
 
 
 def scaled_sum(terms):
@@ -136,7 +131,8 @@
         parts = [read(i, at).astype(jnp.float32) for i in range(blocks)]
         cosines, sines = real_lines(parts, 2 * blocks)
         for k in range(blocks + 1):
-            turn_cos, turn_sin = twist_ref[0, k : k + 1, :], twist_ref[1, k : k + 1, :]
+            width = cosines[k].shape[1]
+            turn_cos, turn_sin = twist_ref[k : k + 1, :width], twist_ref[k : k + 1, width:]
             re, im = cosines[k], sines[k]
             if im is None:
                 new_re, new_im = re * turn_cos, -(re * turn_sin)
@@ -150,21 +146,28 @@
     pl.loop(0, channels // step)(lambda c: body(pl.multiple_of(c * step, step)))
 
 
-def table_fetch(hbm_refs, vmem_refs, sems):
-    copies = [pltpu.make_async_copy(src, dst, sems.at[i]) for i, (src, dst) in enumerate(zip(hbm_refs, vmem_refs))]
-    for copy in copies:
-        copy.start()
-    side = vmem_refs[1].shape[1]
-    return copies, [vmem_refs[1].at[pl.ds(i * side, side)] for i in range(vmem_refs[1].shape[0] // side)]
-
-
-def filter_kernel(blocks, step, rows, taps_ref, twist_hbm, packed_hbm, out_ref, pair_ref, spec_ref, twist_ref, packed_ref, sems):
-    copies, (high_ref, low_ref) = table_fetch((twist_hbm, packed_hbm), (twist_ref, packed_ref), sems)
+def table_rows(blocks, width):
+    twist, forward, backward = dft_constants(blocks, width)
+    lines = np.zeros((-(-(blocks + 1) // 8) * 8, 2 * width), np.float32)
+    lines[: blocks + 1, :width], lines[: blocks + 1, width:] = twist
+    return np.concatenate([lines, forward, backward])
+
+
+def split_into(high_ref, low_ref, table):
+    high = table.astype(jnp.bfloat16)
+    high_ref[...] = high
+    low_ref[...] = (table - high.astype(jnp.float32)).astype(jnp.bfloat16)
+
+
+def filter_kernel(blocks, step, rows, taps_ref, table_ref, out_ref, pair_ref, spec_ref, high_ref, low_ref):
     channels, length = taps_ref.shape
     width = length // blocks
     total = 2 * blocks * width
-    for copy in copies:
-        copy.wait()
+    spectra = (blocks + 1) * channels
+    tail = table_ref.shape[0] - 4 * width
+    out_ref[spectra:] = table_ref[...]
+    twist_ref = table_ref.at[:tail]
+    split_into(high_ref, low_ref, table_ref[tail : tail + 2 * width])
 
     def body(start):
         to_spectrum(
@@ -173,7 +176,7 @@
         )
         for k in range(blocks + 1):
             scale = (1.0 if k in (0, blocks) else 2.0) / total
-            out_ref[k, pl.ds(start, step)] = spec_ref[k * step : (k + 1) * step, :] * np.float32(scale)
+            out_ref[pl.ds(k * channels + start, step)] = spec_ref[k * step : (k + 1) * step, :] * np.float32(scale)
 
     each_step(channels, step, body)
 
@@ -183,36 +186,34 @@
     return [
         pltpu.VMEM((lines * step, 4 * width), jnp.bfloat16),
         pltpu.VMEM((lines * step, 2 * width), jnp.float32),
-        pltpu.VMEM((2, lines, width), jnp.float32),
-        pltpu.VMEM((tables * 2 * width, 2 * width), jnp.bfloat16),
-        pltpu.SemaphoreType.DMA((2,)),
-    ]
+    ] + [pltpu.VMEM((2 * width, 2 * width), jnp.bfloat16) for _ in range(2 * tables)]
 
 
 def filter_spectrum(taps, blocks, step):
     channels, length = taps.shape
     width = length // blocks
-    twist, forward, _ = dft_constants(blocks, width)
-    in_hbm = pl.BlockSpec(memory_space=pltpu.HBM)
+    table = table_rows(blocks, width)
     in_vmem = pl.BlockSpec(memory_space=pltpu.VMEM)
     return pl.pallas_call(
         functools.partial(filter_kernel, blocks, step, min(16, step)),
-        in_specs=[in_vmem, in_hbm, in_hbm],
+        in_specs=[in_vmem, in_vmem],
         out_specs=in_vmem,
-        out_shape=jax.ShapeDtypeStruct((blocks + 1, channels, 2 * width), jnp.float32),
-        scratch_shapes=transform_scratch(blocks, width, step, 2),
+        out_shape=jax.ShapeDtypeStruct(((blocks + 1) * channels + table.shape[0], 2 * width), jnp.float32),
+        scratch_shapes=transform_scratch(blocks, width, step, 1),
         compiler_params=pltpu.CompilerParams(vmem_limit_bytes=VMEM_BYTES),
         name="filter_spectrum",
-    )(taps, twist, np.concatenate(forward))
+    )(taps, table)
 
 
 def correlate_kernel(
-    blocks, step, rows, sig_ref, filt_ref, twist_hbm, packed_hbm, out_ref, pair_ref, spec_ref, twist_ref, packed_ref, sems
+    blocks, step, rows, sig_ref, filt_ref, out_ref, pair_ref, spec_ref, fh_ref, fl_ref, bh_ref, bl_ref
 ):
-    copies, (fh_ref, fl_ref, bh_ref, bl_ref) = table_fetch((twist_hbm, packed_hbm), (twist_ref, packed_ref), sems)
     channels, width = sig_ref.shape[1:]
-    for copy in copies:
-        copy.wait()
+    spectra = (blocks + 1) * channels
+    tail = filt_ref.shape[0] - 4 * width
+    twist_ref = filt_ref.at[spectra:tail]
+    split_into(fh_ref, fl_ref, filt_ref[tail : tail + 2 * width])
+    split_into(bh_ref, bl_ref, filt_ref[tail + 2 * width :])
 
     def body(start):
         to_spectrum(
@@ -224,8 +225,8 @@
                 row = k * step + at
                 sig_re = spec_ref[row : row + rows, :width]
                 sig_im = spec_ref[row : row + rows, width:]
-                filt_re = filt_ref[k, pl.ds(start + at, rows), :width]
-                filt_im = filt_ref[k, pl.ds(start + at, rows), width:]
+                filt_re = filt_ref[pl.ds(k * channels + start + at, rows), :width]
+                filt_im = filt_ref[pl.ds(k * channels + start + at, rows), width:]
                 put_split(
                     pair_ref, row, rows,
                     filt_re * sig_re + filt_im * sig_im, filt_re * sig_im - filt_im * sig_re,
@@ -234,7 +235,7 @@
         for at in range(0, step, rows):
             re_lines, im_lines = [], []
             for k in range(blocks + 1):
-                turn_cos, turn_sin = twist_ref[0, k : k + 1, :], twist_ref[1, k : k + 1, :]
+                turn_cos, turn_sin = twist_ref[k : k + 1, :width], twist_ref[k : k + 1, width:]
                 row = k * step + at
                 re, im = spec_ref[row : row + rows, :width], spec_ref[row : row + rows, width:]
                 re_lines.append(re * turn_cos - im * turn_sin)
@@ -247,18 +248,16 @@
 
 def correlate(signal, spectrum, step):
     blocks, channels, width = signal.shape
-    twist, forward, backward = dft_constants(blocks, width)
-    in_hbm = pl.BlockSpec(memory_space=pltpu.HBM)
     in_vmem = pl.BlockSpec(memory_space=pltpu.VMEM)
     return pl.pallas_call(
         functools.partial(correlate_kernel, blocks, step, min(16, step)),
-        in_specs=[in_vmem, in_vmem, in_hbm, in_hbm],
+        in_specs=[in_vmem, in_vmem],
         out_specs=in_vmem,
         out_shape=jax.ShapeDtypeStruct((blocks, channels, width), jnp.bfloat16),
-        scratch_shapes=transform_scratch(blocks, width, step, 4),
+        scratch_shapes=transform_scratch(blocks, width, step, 2),
         compiler_params=pltpu.CompilerParams(vmem_limit_bytes=VMEM_BYTES),
         name="correlate",
-    )(signal, spectrum, twist, np.concatenate(forward + backward))
+    )(signal, spectrum)
 
 
 def dft_tables(count_outer, count_inner):
@@ -536,7 +535,7 @@
     near, far = 2, 4
     hop = lambda values, mask: swap(values, "seq", seq_count, mask)
 
-    spectrum = filter_spectrum(long_filter, seq_count, min(32, group_width))
+    spectrum = filter_spectrum(long_filter, seq_count, min(128, group_width))
 
     shard = lax.axis_index("chan")
     home = shard == side
@@ -570,7 +569,7 @@
     regrouped = lax.all_to_all(
         gated.reshape(seq_count, group_width, token_count), "seq", split_axis=0, concat_axis=0, tiled=True
     )
-    inner = correlate(regrouped, spectrum, min(32, group_width))
+    inner = correlate(regrouped, spectrum, min(128, group_width))
     returned = lax.all_to_all(inner, "seq", split_axis=0, concat_axis=0, tiled=True)
     grad_key, grad_value = output_products(returned.reshape(chan_width, token_count), value_stream, key_stream)
     return (grad_gate, grad_key, grad_value)

time: 131 us -> 128 us (0.977)
  no operation moved by 1% of the time
where the time goes in v4:
time: 128 us
  waiting for transfers between devices  73.6 us (57%)
  blocking collectives  18.3 us (14%)
  starting transfers between devices  14.5 us (11%)
  Pallas kernels  14.3 us (11%)
  local copies, waits for them, and re-layouts  6.15 us (5%)
    ppermute x9, waiting for transfers between devices, swap(): return lax.ppermute(values, axis, [(i, i ^ mask) for i in range(count)])  57.5 us
    all_to_all x1, blocking collectives, per_device(): lax.all_to_all(inner, 'seq', split_axis=0, concat_axis=0, tiled=True)  18.3 us
    all_to_all x1, waiting for transfers between devices, per_device(): lax.all_to_all(gated.reshape(seq_count, group_width, token_count), 'seq',...  10.1 us
    ppermute x1, waiting for transfers between devices, per_device(): lax.ppermute(grad_out[:part], both, [(at(s, y), at(s ^ group, y)) for s,...  5.92 us
    ppermute x9, starting transfers between devices, swap(): return lax.ppermute(values, axis, [(i, i ^ mask) for i in range(count)])  5.4 us
    pallas_call x1, Pallas kernels, correlate(): pl.pallas_call(functools.partial(correlate_kernel, blocks, step, min(16,...  5.06 us
    pallas_call x1, Pallas kernels, partial_mix(): pl.pallas_call(functools.partial(mix_kernel, rows, step), in_specs=[pl.Bl...  4.02 us
    all_to_all x1, starting transfers between devices, per_device(): lax.all_to_all(gated.reshape(seq_count, group_width, token_count), 'seq',...  3.57 us
  transfers between devices with their start and end apart: 14, of which 8 were waited for; matrix products, arithmetic and copies ran while one was open for 3% of the time, Pallas kernels for 2%

profile of v4, /device:TPU:0, one launch (start us, length us, event | category | flops | bytes accessed | tf_op | source)
XLA Modules:
  0.0 127.9 jit_solution(10658454416403675396)
XLA Ops:
  0.7 3.0 %collective-permute-start.6 = (bf16[256,2048]{1,0:T(8,128)(2,1)}, bf16[256,2048]{1,0:T(8,128)(2,1)}, u32[]{:S(2)}, u32[]{:S(2)}) collective-permute-start(bf16[256,2048]{1,0:T(8,128)(2,1)} %refs_0_.1), channel_id=1, source_target_pairs={{0,4},{2,6},{4,0},{6,2},{8,12},{10,14},{12,8},{14,10},{16,20},{18,... | collective-permute-start | bytes 3145736 | tf_op jit(solution)/shard_map/ppermute | solution.py:521
  3.7 1.2 slice.25
  4.8 1.6 %collective-permute-start.9 = (bf16[256,1280]{1,0:T(8,128)(2,1)S(1)}, bf16[256,1280]{1,0:T(8,128)(2,1)S(1)}, u32[]{:S(2)}, u32[]{:S(2)}) collective-permute-start(bf16[256,1280]{1,0:T(8,128)(2,1)S(1)} %slice.25), channel_id=1, source_target_pairs={{0,8},{2,10},{4,12},{6,14},{8,0},{10,2},{12,4},{14,6},{16,24},{18,... | collective-permute-start | bytes 1966088 | tf_op jit(solution)/shard_map/ppermute | solution.py:521
  6.5 3.4 %collective-permute-start = (bf16[128,2048]{1,0:T(8,128)(2,1)}, bf16[128,2048]{1,0:T(8,128)(2,1)S(1)}, u32[]{:S(2)}, u32[]{:S(2)}) collective-permute-start(bf16[128,2048]{1,0:T(8,128)(2,1)} %own_ref.1), channel_id=1, source_target_pairs={{0,1},{2,3},{4,5},{6,7},{8,9},{10,11},{12,13},{14,15},{17,16},{19,... | collective-permute-start | bytes 1572872 | tf_op jit(solution)/shard_map/ppermute | solution.py:549
  9.9 1.1 fusion
  11.7 1.3 %collective-permute-start.1 = (bf16[64,2048]{1,0:T(8,128)(2,1)S(1)}, bf16[64,2048]{1,0:T(8,128)(2,1)S(1)}, u32[]{:S(2)}, u32[]{:S(2)}) collective-permute-start(bf16[64,2048]{1,0:T(8,128)(2,1)S(1)} %get-tuple-element.24), channel_id=1, source_target_pairs={{1,17},{3,19},{5,21},{7,23},{9,25},{11,27},{13,29},{15,31},{16,0},... | collective-permute-start | bytes 786440 | tf_op jit(solution)/shard_map/ppermute | solution.py:547
  13.0 16.8 %collective-permute-done.9.refs_4_ = bf16[256,1280]{1,0:T(8,128)(2,1)S(1)} collective-permute-done((bf16[256,1280]{1,0:T(8,128)(2,1)S(1)}, bf16[256,1280]{1,0:T(8,128)(2,1)S(1)}, u32[]{:S(2)}, u32[]{:S(2)}) %collective-permute-start.9) | collective-permute-done | bytes 655392 | tf_op jit(solution)/shard_map/ppermute | solution.py:521
  31.1 5.9 %collective-permute-done.1.first_ref = bf16[64,2048]{1,0:T(8,128)(2,1)S(1)} collective-permute-done((bf16[64,2048]{1,0:T(8,128)(2,1)S(1)}, bf16[64,2048]{1,0:T(8,128)(2,1)S(1)}, u32[]{:S(2)}, u32[]{:S(2)}) %collective-permute-start.1) | collective-permute-done | bytes 262176 | tf_op jit(solution)/shard_map/ppermute | solution.py:547
  37.8 1.0 slice.28
  39.0 6.0 %collective-permute-done.7.refs_2_ = bf16[256,768]{1,0:T(8,128)(2,1)} collective-permute-done((bf16[256,768]{1,0:T(8,128)(2,1)}, bf16[256,768]{1,0:T(8,128)(2,1)}, u32[]{:S(2)}, u32[]{:S(2)}) %collective-permute-start.7) | collective-permute-done | bytes 393248 | tf_op jit(solution)/shard_map/ppermute | solution.py:521
  45.0 5.0 %collective-permute-done.3.beside_ref = bf16[64,1024]{1,0:T(8,128)(2,1)S(1)} collective-permute-done((bf16[64,1024]{1,0:T(8,128)(2,1)S(1)}, bf16[64,1024]{1,0:T(8,128)(2,1)S(1)}, u32[]{:S(2)}, u32[]{:S(2)}) %collective-permute-start.3) | collective-permute-done | bytes 131104 | tf_op jit(solution)/shard_map/ppermute | solution.py:521
  50.0 2.0 %collective-permute-done.8.refs_3_ = bf16[256,768]{1,0:T(8,128)(2,1)S(1)} collective-permute-done((bf16[256,768]{1,0:T(8,128)(2,1)S(1)}, bf16[256,768]{1,0:T(8,128)(2,1)S(1)}, u32[]{:S(2)}, u32[]{:S(2)}) %collective-permute-start.8) | collective-permute-done | bytes 393248 | tf_op jit(solution)/shard_map/ppermute | solution.py:521
  52.0 4.0 %partial_mix.1 = (f32[256,2048]{1,0:T(8,128)S(1)}, bf16[256,2048]{1,0:T(8,128)(2,1)S(1)}) custom-call(s32[3]{0:T(128)S(1)} %pad_add_fusion.flags_ref, bf16[128,1024]{1,0:T(8,128)(2,1)S(1)} %get-tuple-element.13.mine_ref, bf16[64,1024]{1,0:T(8,128)(2,1)S(1)} %get-tuple-element.14.mine_far_ref, bf16[64,1024]{1,0:T(8,128)(2,1)S(1)} %collective-permute-done.3.beside_ref, ...), custom_call_target="tpu_custom_call" | custom-call | flops 2147483648 | bytes 4456448 | tf_op jit(solution)/shard_map/partial_mix/pallas_call | solution.py:455
  56.1 2.6 %collective-permute-done.11.near_ref = bf16[256,2048]{1,0:T(8,128)(2,1)S(1)} collective-permute-done((bf16[256,2048]{1,0:T(8,128)(2,1)S(1)}, bf16[256,2048]{1,0:T(8,128)(2,1)S(1)}, u32[]{:S(2)}, u32[]{:S(2)}) %collective-permute-start.11) | collective-permute-done | bytes 1048608 | tf_op jit(solution)/shard_map/ppermute | solution.py:521
  59.0 25.1 %collective-permute-done.12.far_ref = bf16[128,2048]{1,0:T(8,128)(2,1)S(1)} collective-permute-done((bf16[128,2048]{1,0:T(8,128)(2,1)S(1)}, bf16[128,2048]{1,0:T(8,128)(2,1)S(1)}, u32[]{:S(2)}, u32[]{:S(2)}) %collective-permute-start.12) | collective-permute-done | bytes 524320 | tf_op jit(solution)/shard_map/ppermute | solution.py:521
  84.1 1.4 %gate_mix.1 = (bf16[2048,128]{1,0:T(8,128)(2,1)}, bf16[2048,128]{1,0:T(8,128)(2,1)}) custom-call(f32[256,2048]{1,0:T(8,128)S(1)} %get-tuple-element.17.keep_ref, bf16[256,2048]{1,0:T(8,128)(2,1)S(1)} %collective-permute-done.11.near_ref, bf16[128,2048]{1,0:T(8,128)(2,1)S(1)} %collective-permute-done.12.far_ref, bf16[2048,128]{1,0:T(8,128)(2,1)S(1)} %copy-done.3, ...), custom_call_target="tpu_custom_call" | custom-call | bytes 4194304 | tf_op jit(solution)/shard_map/gate_mix/pallas_call | solution.py:487
  85.4 3.6 %all-to-all-start = ((bf16[16,128,128]{2,1,0:T(8,128)(2,1)}), bf16[16,128,128]{2,1,0:T(8,128)(2,1)S(1)}, u32[]{:S(2)}, u32[]{:S(2)}) async-start(bf16[16,128,128]{2,1,0:T(8,128)(2,1)} %bitcast.3), calls=%async_computation | async-start | bytes 1048576 | tf_op jit(solution)/shard_map/all_to_all | solution.py:569
  89.0 1.0 copy-done.2
  90.1 1.0 copy-done.7
  91.1 2.2 %filter_spectrum.1.filt_ref = f32[2712,256]{1,0:T(8,128)S(1)} custom-call(bf16[128,2048]{1,0:T(8,128)(2,1)S(1)} %copy-done.7, f32[536,256]{1,0:T(8,128)S(1)} %copy-done.2), custom_call_target="tpu_custom_call" | custom-call | tf_op jit(solution)/shard_map/filter_spectrum/pallas_call | solution.py:197
  93.3 10.1 %all-to-all-done.sig_ref = bf16[16,128,128]{2,1,0:T(8,128)(2,1)S(1)} async-done(((bf16[16,128,128]{2,1,0:T(8,128)(2,1)}), bf16[16,128,128]{2,1,0:T(8,128)(2,1)S(1)}, u32[]{:S(2)}, u32[]{:S(2)}) %all-to-all-start) | async-done | bytes 524320 | tf_op jit(solution)/shard_map/all_to_all | solution.py:569
  103.4 5.1 %correlate.1 = bf16[16,128,128]{2,1,0:T(8,128)(2,1)S(1)} custom-call(bf16[16,128,128]{2,1,0:T(8,128)(2,1)S(1)} %all-to-all-done.sig_ref, f32[2712,256]{1,0:T(8,128)S(1)} %filter_spectrum.1.filt_ref), custom_call_target="tpu_custom_call" | custom-call | tf_op jit(solution)/shard_map/correlate/pallas_call | solution.py:252
  108.5 18.3 %all_to_all.10 = bf16[16,128,128]{2,1,0:T(8,128)(2,1)S(1)} all-to-all(bf16[16,128,128]{2,1,0:T(8,128)(2,1)S(1)} %correlate.1), channel_id=1, replica_groups=mesh['seq'=16,'chan'=2] {'seq'}, dimensions={0} | all-to-all | bytes 1048576 | tf_op jit(solution)/shard_map/all_to_all | solution.py:573
  126.8 1.0 output_products.1
  (33 shorter events, 3.2 us)
Async XLA Ops:
  0.6 29.6 %copy-start.1 = (bf16[256,2048]{1,0:T(8,128)(2,1)S(1)}, bf16[256,2048]{1,0:T(8,128)(2,1)}, u32[]{:S(2)}) copy-start(bf16[256,2048]{1,0:T(8,128)(2,1)} %refs_0_.1) | copy-start | bytes 3145732
  0.6 36.4 %copy-start = (bf16[128,2048]{1,0:T(8,128)(2,1)S(1)}, bf16[128,2048]{1,0:T(8,128)(2,1)}, u32[]{:S(2)}) copy-start(bf16[128,2048]{1,0:T(8,128)(2,1)} %own_ref.1) | copy-start | bytes 1572868
  0.7 37.2 %collective-permute-start.6 = (bf16[256,2048]{1,0:T(8,128)(2,1)}, bf16[256,2048]{1,0:T(8,128)(2,1)}, u32[]{:S(2)}, u32[]{:S(2)}) collective-permute-start(bf16[256,2048]{1,0:T(8,128)(2,1)} %refs_0_.1), channel_id=1, source_target_pairs={{0,4},{2,6},{4,0},{6,2},{8,12},{10,14},{12,8},{14,10},{16,20},{18,... | collective-permute-start | bytes 3145736 | tf_op jit(solution)/shard_map/ppermute | solution.py:521
  4.8 25.0 %collective-permute-start.9 = (bf16[256,1280]{1,0:T(8,128)(2,1)S(1)}, bf16[256,1280]{1,0:T(8,128)(2,1)S(1)}, u32[]{:S(2)}, u32[]{:S(2)}) collective-permute-start(bf16[256,1280]{1,0:T(8,128)(2,1)S(1)} %slice.25), channel_id=1, source_target_pairs={{0,8},{2,10},{4,12},{6,14},{8,0},{10,2},{12,4},{14,6},{16,24},{18,... | collective-permute-start | bytes 1966088 | tf_op jit(solution)/shard_map/ppermute | solution.py:521
  6.5 30.6 %collective-permute-start = (bf16[128,2048]{1,0:T(8,128)(2,1)}, bf16[128,2048]{1,0:T(8,128)(2,1)S(1)}, u32[]{:S(2)}, u32[]{:S(2)}) collective-permute-start(bf16[128,2048]{1,0:T(8,128)(2,1)} %own_ref.1), channel_id=1, source_target_pairs={{0,1},{2,3},{4,5},{6,7},{8,9},{10,11},{12,13},{14,15},{17,16},{19,... | collective-permute-start | bytes 1572872 | tf_op jit(solution)/shard_map/ppermute | solution.py:549
  11.0 20.1 %collective-permute-start.2 = (bf16[64,2048]{1,0:T(8,128)(2,1)S(1)}, bf16[64,2048]{1,0:T(8,128)(2,1)S(1)}, u32[]{:S(2)}, u32[]{:S(2)}) collective-permute-start(bf16[64,2048]{1,0:T(8,128)(2,1)S(1)} %get-tuple-element.23), channel_id=1, source_target_pairs={{1,16},{3,18},{5,20},{7,22},{9,24},{11,26},{13,28},{15,30},{16,1},... | collective-permute-start | bytes 786440 | tf_op jit(solution)/shard_map/ppermute | solution.py:548
  11.7 25.4 %collective-permute-start.1 = (bf16[64,2048]{1,0:T(8,128)(2,1)S(1)}, bf16[64,2048]{1,0:T(8,128)(2,1)S(1)}, u32[]{:S(2)}, u32[]{:S(2)}) collective-permute-start(bf16[64,2048]{1,0:T(8,128)(2,1)S(1)} %get-tuple-element.24), channel_id=1, source_target_pairs={{1,17},{3,19},{5,21},{7,23},{9,25},{11,27},{13,29},{15,31},{16,0},... | collective-permute-start | bytes 786440 | tf_op jit(solution)/shard_map/ppermute | solution.py:547
  29.8 20.2 %collective-permute-start.10 = (bf16[256,1280]{1,0:T(8,128)(2,1)S(1)}, bf16[256,1280]{1,0:T(8,128)(2,1)}, u32[]{:S(2)}, u32[]{:S(2)}) collective-permute-start(bf16[256,1280]{1,0:T(8,128)(2,1)S(1)} %collective-permute-done.9.refs_4_), channel_id=1, source_target_pairs={{0,4},{2,6},{4,0},{6,2},{8,12},{10,14},{12,8},{14,10},{16,20},{18,... | collective-permute-start | bytes 1966088 | tf_op jit(solution)/shard_map/ppermute | solution.py:521
  31.1 14.0 %collective-permute-start.7 = (bf16[256,768]{1,0:T(8,128)(2,1)}, bf16[256,768]{1,0:T(8,128)(2,1)}, u32[]{:S(2)}, u32[]{:S(2)}) collective-permute-start(bf16[256,768]{1,0:T(8,128)(2,1)} %slice.23), channel_id=1, source_target_pairs={{0,8},{2,10},{4,12},{6,14},{8,0},{10,2},{12,4},{14,6},{16,24},{18,... | collective-permute-start | bytes 1179656 | tf_op jit(solution)/shard_map/ppermute | solution.py:521
  37.7 12.3 %collective-permute-start.4 = (bf16[192,1024]{1,0:T(8,128)(2,1)S(1)}, bf16[192,1024]{1,0:T(8,128)(2,1)S(1)}, u32[]{:S(2)}, u32[]{:S(2)}) collective-permute-start(bf16[192,1024]{1,0:T(8,128)(2,1)S(1)} %get-tuple-element.15), channel_id=1, source_target_pairs={{0,2},{2,0},{4,6},{6,4},{8,10},{10,8},{12,14},{14,12},{16,18},{18,... | collective-permute-start | bytes 1179656 | tf_op jit(solution)/shard_map/ppermute | solution.py:521
  38.9 13.2 %collective-permute-start.8 = (bf16[256,768]{1,0:T(8,128)(2,1)S(1)}, bf16[256,768]{1,0:T(8,128)(2,1)S(1)}, u32[]{:S(2)}, u32[]{:S(2)}) collective-permute-start(bf16[256,768]{1,0:T(8,128)(2,1)S(1)} %slice.28), channel_id=1, source_target_pairs={{0,8},{2,10},{4,12},{6,14},{8,0},{10,2},{12,4},{14,6},{16,24},{18,... | collective-permute-start | bytes 1179656 | tf_op jit(solution)/shard_map/ppermute | solution.py:521
  38.9 6.1 %collective-permute-start.5 = (bf16[64,1024]{1,0:T(8,128)(2,1)S(1)}, bf16[64,1024]{1,0:T(8,128)(2,1)S(1)}, u32[]{:S(2)}, u32[]{:S(2)}) collective-permute-start(bf16[64,1024]{1,0:T(8,128)(2,1)S(1)} %get-tuple-element.16), channel_id=1, source_target_pairs={{0,3},{1,2},{2,1},{3,0},{4,7},{5,6},{6,5},{7,4},{8,11},{9,10},{10,... | collective-permute-start | bytes 393224 | tf_op jit(solution)/shard_map/ppermute | solution.py:559
  45.0 5.0 %collective-permute-start.3 = (bf16[64,1024]{1,0:T(8,128)(2,1)S(1)}, bf16[64,1024]{1,0:T(8,128)(2,1)S(1)}, u32[]{:S(2)}, u32[]{:S(2)}) collective-permute-start(bf16[64,1024]{1,0:T(8,128)(2,1)S(1)} %get-tuple-element.14.mine_far_ref), channel_id=1, source_target_pairs={{0,1},{1,0},{2,3},{3,2},{4,5},{5,4},{6,7},{7,6},{8,9},{9,8},{10,11... | collective-permute-start | bytes 393224 | tf_op jit(solution)/shard_map/ppermute | solution.py:521
  56.0 28.0 %copy-start.3 = (bf16[2048,128]{1,0:T(8,128)(2,1)S(1)}, bf16[2048,128]{1,0:T(8,128)(2,1)}, u32[]{:S(2)}) copy-start(bf16[2048,128]{1,0:T(8,128)(2,1)} %gate_ref.1) | copy-start | bytes 1572868
  56.1 28.0 %copy-start.4 = (bf16[2048,128]{1,0:T(8,128)(2,1)S(1)}, bf16[2048,128]{1,0:T(8,128)(2,1)}, u32[]{:S(2)}) copy-start(bf16[2048,128]{1,0:T(8,128)(2,1)} %conv_ref.1) | copy-start | bytes 1572868
  56.1 2.7 %collective-permute-start.11 = (bf16[256,2048]{1,0:T(8,128)(2,1)S(1)}, bf16[256,2048]{1,0:T(8,128)(2,1)S(1)}, u32[]{:S(2)}, u32[]{:S(2)}) collective-permute-start(bf16[256,2048]{1,0:T(8,128)(2,1)S(1)} %get-tuple-element.18), channel_id=1, source_target_pairs={{0,2},{2,0},{4,6},{6,4},{8,10},{10,8},{12,14},{14,12},{16,18},{18,... | collective-permute-start | bytes 3145736 | tf_op jit(solution)/shard_map/ppermute | solution.py:521
  58.9 25.1 %collective-permute-start.12 = (bf16[128,2048]{1,0:T(8,128)(2,1)S(1)}, bf16[128,2048]{1,0:T(8,128)(2,1)S(1)}, u32[]{:S(2)}, u32[]{:S(2)}) collective-permute-start(bf16[128,2048]{1,0:T(8,128)(2,1)S(1)} %add_convert_fusion), channel_id=1, source_target_pairs={{0,16},{2,18},{4,20},{6,22},{8,24},{10,26},{12,28},{14,30},{16,0},... | collective-permute-start | bytes 1572872 | tf_op jit(solution)/shard_map/ppermute | solution.py:521
  85.4 18.0 %all-to-all-start = ((bf16[16,128,128]{2,1,0:T(8,128)(2,1)}), bf16[16,128,128]{2,1,0:T(8,128)(2,1)S(1)}, u32[]{:S(2)}, u32[]{:S(2)}) async-start(bf16[16,128,128]{2,1,0:T(8,128)(2,1)} %bitcast.3), calls=%async_computation | async-start | bytes 1048576 | tf_op jit(solution)/shard_map/all_to_all | solution.py:569
  89.0 1.1 copy-start.2
  90.1 1.0 copy-start.7
  103.4 23.4 %copy-start.5 = (bf16[2048,128]{1,0:T(8,128)(2,1)S(1)}, bf16[2048,128]{1,0:T(8,128)(2,1)}, u32[]{:S(2)}) copy-start(bf16[2048,128]{1,0:T(8,128)(2,1)} %value_ref.1) | copy-start | bytes 1572868
  103.4 23.4 %copy-start.6 = (bf16[2048,128]{1,0:T(8,128)(2,1)S(1)}, bf16[2048,128]{1,0:T(8,128)(2,1)}, u32[]{:S(2)}) copy-start(bf16[2048,128]{1,0:T(8,128)(2,1)} %key_ref.1) | copy-start | bytes 1572868

commit v5 on v4

--- a/solution.py
+++ b/solution.py
@@ -545,8 +545,8 @@
     at = lambda s, y: s * 2 + y
     away = [(s, 1 - s // group) for s in range(seq_count)]
     first = lax.ppermute(grad_out[:part], both, [(at(s, y), at(s ^ group, y)) for s, y in away])
-    second = lax.ppermute(grad_out[part:], both, [(at(s, y), at(s ^ group, 1 - y)) for s, y in away])
-    local = lax.ppermute(grad_out, both, [(at(s, 1 - y), at(s, y)) for s, y in away])
+    local = swap(grad_out, "chan", 2, 1)
+    second = lax.ppermute(local[part:], both, [(at(s, 1 - y), at(s ^ group, 1 - y)) for s, y in away])
 
     lead = chan_width // 8 * 3
     edge, rest = out_weight[:, :lead], out_weight[:, lead:]

time: 128 us -> 127 us (level)
  waiting for transfers between devices: 73.6 us -> 58.1 us
  starting transfers between devices: 14.5 us -> 27.9 us
    ppermute x9 -> x10, waiting for transfers between devices: 57.5 us -> 41.3 us  [swap(): return lax.ppermute(values, axis, [(i, i ^ mask) for i in range(count)])]
    ppermute x9 -> x10, starting transfers between devices: 5.4 us -> 15.1 us  [swap(): return lax.ppermute(values, axis, [(i, i ^ mask) for i in range(count)])]
    ppermute x1, waiting for transfers between devices: 5.92 us -> 0.01 us  [per_device(): lax.ppermute(grad_out[:part], both, [(at(s, y), at(s ^ group, y)) for s,...]
    ppermute x2 -> x1, waiting for transfers between devices: 0.01 us -> 3.41 us  [per_device(): lax.ppermute(local[part:], both, [(at(s, 1 - y), at(s ^ group, 1 - y)) fo...]
    ppermute x1, waiting for transfers between devices: 0.01 us -> 3.11 us  [per_device(): lax.ppermute(theirs_far, both, [(at(s, y), at(s ^ 1, 1 - y)) for s in ran...]
    ppermute x1, starting transfers between devices: 0.07 us -> 1.88 us  [per_device(): lax.ppermute(theirs_far, both, [(at(s, y), at(s ^ 1, 1 - y)) for s in ran...]
    all_to_all x1, starting transfers between devices: 3.57 us -> 5.09 us  [per_device(): lax.all_to_all(gated.reshape(seq_count, group_width, token_count), 'seq',...]
    ppermute x2 -> x1, starting transfers between devices: 4.12 us -> 4.5 us  [per_device(): lax.ppermute(local[part:], both, [(at(s, 1 - y), at(s ^ group, 1 - y)) fo...]
  transfers between devices with their start and end apart: 14 -> 14, of which waited for: 8 -> 9; matrix products, arithmetic and copies ran while one was open for 3% -> 4% of each run, Pallas kernels for 2% -> 2%
where the time goes in v5:
time: 127 us; the launch traced here: 126 us
  waiting for transfers between devices  58.1 us (46%)
  starting transfers between devices  27.9 us (22%)
  blocking collectives  18.4 us (14%)
  Pallas kernels  14.3 us (11%)
  local copies, waits for them, and re-layouts  6.81 us (5%)
    ppermute x10, waiting for transfers between devices, swap(): return lax.ppermute(values, axis, [(i, i ^ mask) for i in range(count)])  41.3 us
    all_to_all x1, blocking collectives, per_device(): lax.all_to_all(inner, 'seq', split_axis=0, concat_axis=0, tiled=True)  18.4 us
    ppermute x10, starting transfers between devices, swap(): return lax.ppermute(values, axis, [(i, i ^ mask) for i in range(count)])  15.1 us
    all_to_all x1, waiting for transfers between devices, per_device(): lax.all_to_all(gated.reshape(seq_count, group_width, token_count), 'seq',...  10.2 us
    all_to_all x1, starting transfers between devices, per_device(): lax.all_to_all(gated.reshape(seq_count, group_width, token_count), 'seq',...  5.09 us
    pallas_call x1, Pallas kernels, correlate(): pl.pallas_call(functools.partial(correlate_kernel, blocks, step, min(16,...  5.06 us
    ppermute x1, starting transfers between devices, per_device(): lax.ppermute(local[part:], both, [(at(s, 1 - y), at(s ^ group, 1 - y)) fo...  4.5 us
    pallas_call x1, Pallas kernels, partial_mix(): pl.pallas_call(functools.partial(mix_kernel, rows, step), in_specs=[pl.Bl...  4.02 us
  transfers between devices with their start and end apart: 14, of which 9 were waited for; matrix products, arithmetic and copies ran while one was open for 4% of the time, Pallas kernels for 2%

profile of v5, /device:TPU:0, one launch (start us, length us, event | category | flops | bytes accessed | tf_op | source)
XLA Modules:
  0.0 126.4 jit_solution(15275244713464548601)
XLA Ops:
  0.7 3.0 %collective-permute-start.6 = (bf16[256,2048]{1,0:T(8,128)(2,1)}, bf16[256,2048]{1,0:T(8,128)(2,1)}, u32[]{:S(2)}, u32[]{:S(2)}) collective-permute-start(bf16[256,2048]{1,0:T(8,128)(2,1)} %refs_0_.1), channel_id=1, source_target_pairs={{0,4},{2,6},{4,0},{6,2},{8,12},{10,14},{12,8},{14,10},{16,20},{18,... | collective-permute-start | bytes 3145736 | tf_op jit(solution)/shard_map/ppermute | solution.py:521
  3.7 1.2 slice.25
  4.8 1.6 %collective-permute-start.9 = (bf16[256,1280]{1,0:T(8,128)(2,1)S(1)}, bf16[256,1280]{1,0:T(8,128)(2,1)S(1)}, u32[]{:S(2)}, u32[]{:S(2)}) collective-permute-start(bf16[256,1280]{1,0:T(8,128)(2,1)S(1)} %slice.25), channel_id=1, source_target_pairs={{0,8},{2,10},{4,12},{6,14},{8,0},{10,2},{12,4},{14,6},{16,24},{18,... | collective-permute-start | bytes 1966088 | tf_op jit(solution)/shard_map/ppermute | solution.py:521
  6.5 1.5 %collective-permute-start = (bf16[128,2048]{1,0:T(8,128)(2,1)}, bf16[128,2048]{1,0:T(8,128)(2,1)S(1)}, u32[]{:S(2)}, u32[]{:S(2)}) collective-permute-start(bf16[128,2048]{1,0:T(8,128)(2,1)} %own_ref.1), channel_id=1, source_target_pairs={{0,1},{1,0},{2,3},{3,2},{4,5},{5,4},{6,7},{7,6},{8,9},{9,8},{10,11... | collective-permute-start | bytes 1572872 | tf_op jit(solution)/shard_map/ppermute | solution.py:521
  9.0 1.3 %collective-permute-start.1 = (bf16[64,2048]{1,0:T(8,128)(2,1)S(1)}, bf16[64,2048]{1,0:T(8,128)(2,1)S(1)}, u32[]{:S(2)}, u32[]{:S(2)}) collective-permute-start(bf16[64,2048]{1,0:T(8,128)(2,1)S(1)} %slice.21), channel_id=1, source_target_pairs={{1,17},{3,19},{5,21},{7,23},{9,25},{11,27},{13,29},{15,31},{16,0},... | collective-permute-start | bytes 786440 | tf_op jit(solution)/shard_map/ppermute | solution.py:547
  10.3 9.5 %collective-permute-done.local_ref = bf16[128,2048]{1,0:T(8,128)(2,1)S(1)} collective-permute-done((bf16[128,2048]{1,0:T(8,128)(2,1)}, bf16[128,2048]{1,0:T(8,128)(2,1)S(1)}, u32[]{:S(2)}, u32[]{:S(2)}) %collective-permute-start) | collective-permute-done | bytes 524320 | tf_op jit(solution)/shard_map/ppermute | solution.py:521
  20.5 4.5 %collective-permute-start.2 = (bf16[64,2048]{1,0:T(8,128)(2,1)}, bf16[64,2048]{1,0:T(8,128)(2,1)S(1)}, u32[]{:S(2)}, u32[]{:S(2)}) collective-permute-start(bf16[64,2048]{1,0:T(8,128)(2,1)} %slice.28), channel_id=1, source_target_pairs={{0,16},{2,18},{4,20},{6,22},{8,24},{10,26},{12,28},{14,30},{17,1},... | collective-permute-start | bytes 786440 | tf_op jit(solution)/shard_map/ppermute | solution.py:549
  25.0 1.7 %collective-permute-done.9.refs_4_ = bf16[256,1280]{1,0:T(8,128)(2,1)S(1)} collective-permute-done((bf16[256,1280]{1,0:T(8,128)(2,1)S(1)}, bf16[256,1280]{1,0:T(8,128)(2,1)S(1)}, u32[]{:S(2)}, u32[]{:S(2)}) %collective-permute-start.9) | collective-permute-done | bytes 655392 | tf_op jit(solution)/shard_map/ppermute | solution.py:521
  28.0 3.4 %collective-permute-done.2.second_ref = bf16[64,2048]{1,0:T(8,128)(2,1)S(1)} collective-permute-done((bf16[64,2048]{1,0:T(8,128)(2,1)}, bf16[64,2048]{1,0:T(8,128)(2,1)S(1)}, u32[]{:S(2)}, u32[]{:S(2)}) %collective-permute-start.2) | collective-permute-done | bytes 262176 | tf_op jit(solution)/shard_map/ppermute | solution.py:549
  33.2 4.2 %collective-permute-start.8 = (bf16[256,768]{1,0:T(8,128)(2,1)S(1)}, bf16[256,768]{1,0:T(8,128)(2,1)S(1)}, u32[]{:S(2)}, u32[]{:S(2)}) collective-permute-start(bf16[256,768]{1,0:T(8,128)(2,1)S(1)} %slice.29), channel_id=1, source_target_pairs={{0,8},{2,10},{4,12},{6,14},{8,0},{10,2},{12,4},{14,6},{16,24},{18,... | collective-permute-start | bytes 1179656 | tf_op jit(solution)/shard_map/ppermute | solution.py:521
  37.4 1.9 %collective-permute-start.5 = (bf16[64,1024]{1,0:T(8,128)(2,1)S(1)}, bf16[64,1024]{1,0:T(8,128)(2,1)S(1)}, u32[]{:S(2)}, u32[]{:S(2)}) collective-permute-start(bf16[64,1024]{1,0:T(8,128)(2,1)S(1)} %get-tuple-element.16), channel_id=1, source_target_pairs={{0,3},{1,2},{2,1},{3,0},{4,7},{5,6},{6,5},{7,4},{8,11},{9,10},{10,... | collective-permute-start | bytes 393224 | tf_op jit(solution)/shard_map/ppermute | solution.py:559
  40.0 3.1 %collective-permute-done.5.slant_ref = bf16[64,1024]{1,0:T(8,128)(2,1)S(1)} collective-permute-done((bf16[64,1024]{1,0:T(8,128)(2,1)S(1)}, bf16[64,1024]{1,0:T(8,128)(2,1)S(1)}, u32[]{:S(2)}, u32[]{:S(2)}) %collective-permute-start.5) | collective-permute-done | bytes 131104 | tf_op jit(solution)/shard_map/ppermute | solution.py:559
  43.1 3.0 %collective-permute-done.3.beside_ref = bf16[64,1024]{1,0:T(8,128)(2,1)S(1)} collective-permute-done((bf16[64,1024]{1,0:T(8,128)(2,1)S(1)}, bf16[64,1024]{1,0:T(8,128)(2,1)S(1)}, u32[]{:S(2)}, u32[]{:S(2)}) %collective-permute-start.3) | collective-permute-done | bytes 131104 | tf_op jit(solution)/shard_map/ppermute | solution.py:521
  47.2 4.0 %partial_mix.1 = (f32[256,2048]{1,0:T(8,128)S(1)}, bf16[256,2048]{1,0:T(8,128)(2,1)S(1)}) custom-call(s32[3]{0:T(128)S(1)} %pad_add_fusion.flags_ref, bf16[128,1024]{1,0:T(8,128)(2,1)S(1)} %get-tuple-element.13.mine_ref, bf16[64,1024]{1,0:T(8,128)(2,1)S(1)} %get-tuple-element.14.mine_far_ref, bf16[64,1024]{1,0:T(8,128)(2,1)S(1)} %collective-permute-done.3.beside_ref, ...), custom_call_target="tpu_custom_call" | custom-call | flops 2147483648 | bytes 4456448 | tf_op jit(solution)/shard_map/partial_mix/pallas_call | solution.py:455
  51.3 2.6 %collective-permute-done.11.near_ref = bf16[256,2048]{1,0:T(8,128)(2,1)S(1)} collective-permute-done((bf16[256,2048]{1,0:T(8,128)(2,1)S(1)}, bf16[256,2048]{1,0:T(8,128)(2,1)S(1)}, u32[]{:S(2)}, u32[]{:S(2)}) %collective-permute-start.11) | collective-permute-done | bytes 1048608 | tf_op jit(solution)/shard_map/ppermute | solution.py:521
  54.1 3.4 %collective-permute-start.12 = (bf16[128,2048]{1,0:T(8,128)(2,1)S(1)}, bf16[128,2048]{1,0:T(8,128)(2,1)S(1)}, u32[]{:S(2)}, u32[]{:S(2)}) collective-permute-start(bf16[128,2048]{1,0:T(8,128)(2,1)S(1)} %add_convert_fusion), channel_id=1, source_target_pairs={{0,16},{2,18},{4,20},{6,22},{8,24},{10,26},{12,28},{14,30},{16,0},... | collective-permute-start | bytes 1572872 | tf_op jit(solution)/shard_map/ppermute | solution.py:521
  57.5 23.5 %collective-permute-done.12.far_ref = bf16[128,2048]{1,0:T(8,128)(2,1)S(1)} collective-permute-done((bf16[128,2048]{1,0:T(8,128)(2,1)S(1)}, bf16[128,2048]{1,0:T(8,128)(2,1)S(1)}, u32[]{:S(2)}, u32[]{:S(2)}) %collective-permute-start.12) | collective-permute-done | bytes 524320 | tf_op jit(solution)/shard_map/ppermute | solution.py:521
  81.0 1.4 %gate_mix.1 = (bf16[2048,128]{1,0:T(8,128)(2,1)}, bf16[2048,128]{1,0:T(8,128)(2,1)}) custom-call(f32[256,2048]{1,0:T(8,128)S(1)} %get-tuple-element.17.keep_ref, bf16[256,2048]{1,0:T(8,128)(2,1)S(1)} %collective-permute-done.11.near_ref, bf16[128,2048]{1,0:T(8,128)(2,1)S(1)} %collective-permute-done.12.far_ref, bf16[2048,128]{1,0:T(8,128)(2,1)S(1)} %copy-done.3, ...), custom_call_target="tpu_custom_call" | custom-call | bytes 4194304 | tf_op jit(solution)/shard_map/gate_mix/pallas_call | solution.py:487
  82.3 5.1 %all-to-all-start = ((bf16[16,128,128]{2,1,0:T(8,128)(2,1)}), bf16[16,128,128]{2,1,0:T(8,128)(2,1)S(1)}, u32[]{:S(2)}, u32[]{:S(2)}) async-start(bf16[16,128,128]{2,1,0:T(8,128)(2,1)} %bitcast.3), calls=%async_computation | async-start | bytes 1048576 | tf_op jit(solution)/shard_map/all_to_all | solution.py:569
  89.5 2.2 %filter_spectrum.1.filt_ref = f32[2712,256]{1,0:T(8,128)S(1)} custom-call(bf16[128,2048]{1,0:T(8,128)(2,1)S(1)} %copy-done.7, f32[536,256]{1,0:T(8,128)S(1)} %copy-done.2), custom_call_target="tpu_custom_call" | custom-call | tf_op jit(solution)/shard_map/filter_spectrum/pallas_call | solution.py:197
  91.7 10.2 %all-to-all-done.sig_ref = bf16[16,128,128]{2,1,0:T(8,128)(2,1)S(1)} async-done(((bf16[16,128,128]{2,1,0:T(8,128)(2,1)}), bf16[16,128,128]{2,1,0:T(8,128)(2,1)S(1)}, u32[]{:S(2)}, u32[]{:S(2)}) %all-to-all-start) | async-done | bytes 524320 | tf_op jit(solution)/shard_map/all_to_all | solution.py:569
  101.9 5.1 %correlate.1 = bf16[16,128,128]{2,1,0:T(8,128)(2,1)S(1)} custom-call(bf16[16,128,128]{2,1,0:T(8,128)(2,1)S(1)} %all-to-all-done.sig_ref, f32[2712,256]{1,0:T(8,128)S(1)} %filter_spectrum.1.filt_ref), custom_call_target="tpu_custom_call" | custom-call | tf_op jit(solution)/shard_map/correlate/pallas_call | solution.py:252
  107.0 18.4 %all_to_all.10 = bf16[16,128,128]{2,1,0:T(8,128)(2,1)S(1)} all-to-all(bf16[16,128,128]{2,1,0:T(8,128)(2,1)S(1)} %correlate.1), channel_id=1, replica_groups=mesh['seq'=16,'chan'=2] {'seq'}, dimensions={0} | all-to-all | bytes 1048576 | tf_op jit(solution)/shard_map/all_to_all | solution.py:573
  125.3 1.0 output_products.1
  (34 shorter events, 8.9 us)
Async XLA Ops:
  0.6 26.5 %copy-start.1 = (bf16[256,2048]{1,0:T(8,128)(2,1)S(1)}, bf16[256,2048]{1,0:T(8,128)(2,1)}, u32[]{:S(2)}) copy-start(bf16[256,2048]{1,0:T(8,128)(2,1)} %refs_0_.1) | copy-start | bytes 3145732
  0.6 30.8 %copy-start = (bf16[128,2048]{1,0:T(8,128)(2,1)S(1)}, bf16[128,2048]{1,0:T(8,128)(2,1)}, u32[]{:S(2)}) copy-start(bf16[128,2048]{1,0:T(8,128)(2,1)} %own_ref.1) | copy-start | bytes 1572868
  0.7 31.5 %collective-permute-start.6 = (bf16[256,2048]{1,0:T(8,128)(2,1)}, bf16[256,2048]{1,0:T(8,128)(2,1)}, u32[]{:S(2)}, u32[]{:S(2)}) collective-permute-start(bf16[256,2048]{1,0:T(8,128)(2,1)} %refs_0_.1), channel_id=1, source_target_pairs={{0,4},{2,6},{4,0},{6,2},{8,12},{10,14},{12,8},{14,10},{16,20},{18,... | collective-permute-start | bytes 3145736 | tf_op jit(solution)/shard_map/ppermute | solution.py:521
  4.8 21.9 %collective-permute-start.9 = (bf16[256,1280]{1,0:T(8,128)(2,1)S(1)}, bf16[256,1280]{1,0:T(8,128)(2,1)S(1)}, u32[]{:S(2)}, u32[]{:S(2)}) collective-permute-start(bf16[256,1280]{1,0:T(8,128)(2,1)S(1)} %slice.25), channel_id=1, source_target_pairs={{0,8},{2,10},{4,12},{6,14},{8,0},{10,2},{12,4},{14,6},{16,24},{18,... | collective-permute-start | bytes 1966088 | tf_op jit(solution)/shard_map/ppermute | solution.py:521
  6.5 13.3 %collective-permute-start = (bf16[128,2048]{1,0:T(8,128)(2,1)}, bf16[128,2048]{1,0:T(8,128)(2,1)S(1)}, u32[]{:S(2)}, u32[]{:S(2)}) collective-permute-start(bf16[128,2048]{1,0:T(8,128)(2,1)} %own_ref.1), channel_id=1, source_target_pairs={{0,1},{1,0},{2,3},{3,2},{4,5},{5,4},{6,7},{7,6},{8,9},{9,8},{10,11... | collective-permute-start | bytes 1572872 | tf_op jit(solution)/shard_map/ppermute | solution.py:521
  9.0 19.0 %collective-permute-start.1 = (bf16[64,2048]{1,0:T(8,128)(2,1)S(1)}, bf16[64,2048]{1,0:T(8,128)(2,1)S(1)}, u32[]{:S(2)}, u32[]{:S(2)}) collective-permute-start(bf16[64,2048]{1,0:T(8,128)(2,1)S(1)} %slice.21), channel_id=1, source_target_pairs={{1,17},{3,19},{5,21},{7,23},{9,25},{11,27},{13,29},{15,31},{16,0},... | collective-permute-start | bytes 786440 | tf_op jit(solution)/shard_map/ppermute | solution.py:547
  20.5 10.9 %collective-permute-start.2 = (bf16[64,2048]{1,0:T(8,128)(2,1)}, bf16[64,2048]{1,0:T(8,128)(2,1)S(1)}, u32[]{:S(2)}, u32[]{:S(2)}) collective-permute-start(bf16[64,2048]{1,0:T(8,128)(2,1)} %slice.28), channel_id=1, source_target_pairs={{0,16},{2,18},{4,20},{6,22},{8,24},{10,26},{12,28},{14,30},{17,1},... | collective-permute-start | bytes 786440 | tf_op jit(solution)/shard_map/ppermute | solution.py:549
  26.7 19.5 %collective-permute-start.10 = (bf16[256,1280]{1,0:T(8,128)(2,1)S(1)}, bf16[256,1280]{1,0:T(8,128)(2,1)}, u32[]{:S(2)}, u32[]{:S(2)}) collective-permute-start(bf16[256,1280]{1,0:T(8,128)(2,1)S(1)} %collective-permute-done.9.refs_4_), channel_id=1, source_target_pairs={{0,4},{2,6},{4,0},{6,2},{8,12},{10,14},{12,8},{14,10},{16,20},{18,... | collective-permute-start | bytes 1966088 | tf_op jit(solution)/shard_map/ppermute | solution.py:521
  28.0 11.4 %collective-permute-start.7 = (bf16[256,768]{1,0:T(8,128)(2,1)}, bf16[256,768]{1,0:T(8,128)(2,1)}, u32[]{:S(2)}, u32[]{:S(2)}) collective-permute-start(bf16[256,768]{1,0:T(8,128)(2,1)} %slice.23), channel_id=1, source_target_pairs={{0,8},{2,10},{4,12},{6,14},{8,0},{10,2},{12,4},{14,6},{16,24},{18,... | collective-permute-start | bytes 1179656 | tf_op jit(solution)/shard_map/ppermute | solution.py:521
  32.1 14.1 %collective-permute-start.4 = (bf16[192,1024]{1,0:T(8,128)(2,1)S(1)}, bf16[192,1024]{1,0:T(8,128)(2,1)S(1)}, u32[]{:S(2)}, u32[]{:S(2)}) collective-permute-start(bf16[192,1024]{1,0:T(8,128)(2,1)S(1)} %get-tuple-element.15), channel_id=1, source_target_pairs={{0,2},{2,0},{4,6},{6,4},{8,10},{10,8},{12,14},{14,12},{16,18},{18,... | collective-permute-start | bytes 1179656 | tf_op jit(solution)/shard_map/ppermute | solution.py:521
  33.2 14.0 %collective-permute-start.8 = (bf16[256,768]{1,0:T(8,128)(2,1)S(1)}, bf16[256,768]{1,0:T(8,128)(2,1)S(1)}, u32[]{:S(2)}, u32[]{:S(2)}) collective-permute-start(bf16[256,768]{1,0:T(8,128)(2,1)S(1)} %slice.29), channel_id=1, source_target_pairs={{0,8},{2,10},{4,12},{6,14},{8,0},{10,2},{12,4},{14,6},{16,24},{18,... | collective-permute-start | bytes 1179656 | tf_op jit(solution)/shard_map/ppermute | solution.py:521
  37.4 5.7 %collective-permute-start.5 = (bf16[64,1024]{1,0:T(8,128)(2,1)S(1)}, bf16[64,1024]{1,0:T(8,128)(2,1)S(1)}, u32[]{:S(2)}, u32[]{:S(2)}) collective-permute-start(bf16[64,1024]{1,0:T(8,128)(2,1)S(1)} %get-tuple-element.16), channel_id=1, source_target_pairs={{0,3},{1,2},{2,1},{3,0},{4,7},{5,6},{6,5},{7,4},{8,11},{9,10},{10,... | collective-permute-start | bytes 393224 | tf_op jit(solution)/shard_map/ppermute | solution.py:559
  39.3 6.9 %collective-permute-start.3 = (bf16[64,1024]{1,0:T(8,128)(2,1)S(1)}, bf16[64,1024]{1,0:T(8,128)(2,1)S(1)}, u32[]{:S(2)}, u32[]{:S(2)}) collective-permute-start(bf16[64,1024]{1,0:T(8,128)(2,1)S(1)} %get-tuple-element.14.mine_far_ref), channel_id=1, source_target_pairs={{0,1},{1,0},{2,3},{3,2},{4,5},{5,4},{6,7},{7,6},{8,9},{9,8},{10,11... | collective-permute-start | bytes 393224 | tf_op jit(solution)/shard_map/ppermute | solution.py:521
  51.2 29.7 %copy-start.3 = (bf16[2048,128]{1,0:T(8,128)(2,1)S(1)}, bf16[2048,128]{1,0:T(8,128)(2,1)}, u32[]{:S(2)}) copy-start(bf16[2048,128]{1,0:T(8,128)(2,1)} %gate_ref.1) | copy-start | bytes 1572868
  51.2 29.7 %copy-start.4 = (bf16[2048,128]{1,0:T(8,128)(2,1)S(1)}, bf16[2048,128]{1,0:T(8,128)(2,1)}, u32[]{:S(2)}) copy-start(bf16[2048,128]{1,0:T(8,128)(2,1)} %conv_ref.1) | copy-start | bytes 1572868
  51.2 2.7 %collective-permute-start.11 = (bf16[256,2048]{1,0:T(8,128)(2,1)S(1)}, bf16[256,2048]{1,0:T(8,128)(2,1)S(1)}, u32[]{:S(2)}, u32[]{:S(2)}) collective-permute-start(bf16[256,2048]{1,0:T(8,128)(2,1)S(1)} %get-tuple-element.18), channel_id=1, source_target_pairs={{0,2},{2,0},{4,6},{6,4},{8,10},{10,8},{12,14},{14,12},{16,18},{18,... | collective-permute-start | bytes 3145736 | tf_op jit(solution)/shard_map/ppermute | solution.py:521
  54.1 26.9 %collective-permute-start.12 = (bf16[128,2048]{1,0:T(8,128)(2,1)S(1)}, bf16[128,2048]{1,0:T(8,128)(2,1)S(1)}, u32[]{:S(2)}, u32[]{:S(2)}) collective-permute-start(bf16[128,2048]{1,0:T(8,128)(2,1)S(1)} %add_convert_fusion), channel_id=1, source_target_pairs={{0,16},{2,18},{4,20},{6,22},{8,24},{10,26},{12,28},{14,30},{16,0},... | collective-permute-start | bytes 1572872 | tf_op jit(solution)/shard_map/ppermute | solution.py:521
  82.3 19.6 %all-to-all-start = ((bf16[16,128,128]{2,1,0:T(8,128)(2,1)}), bf16[16,128,128]{2,1,0:T(8,128)(2,1)S(1)}, u32[]{:S(2)}, u32[]{:S(2)}) async-start(bf16[16,128,128]{2,1,0:T(8,128)(2,1)} %bitcast.3), calls=%async_computation | async-start | bytes 1048576 | tf_op jit(solution)/shard_map/all_to_all | solution.py:569
  87.4 1.1 copy-start.2
  88.5 1.0 copy-start.7
  101.9 23.4 %copy-start.5 = (bf16[2048,128]{1,0:T(8,128)(2,1)S(1)}, bf16[2048,128]{1,0:T(8,128)(2,1)}, u32[]{:S(2)}) copy-start(bf16[2048,128]{1,0:T(8,128)(2,1)} %value_ref.1) | copy-start | bytes 1572868
  101.9 23.4 %copy-start.6 = (bf16[2048,128]{1,0:T(8,128)(2,1)S(1)}, bf16[2048,128]{1,0:T(8,128)(2,1)}, u32[]{:S(2)}) copy-start(bf16[2048,128]{1,0:T(8,128)(2,1)} %key_ref.1) | copy-start | bytes 1572868

commit v6 on v5

--- a/solution.py
+++ b/solution.py
@@ -551,7 +551,9 @@
     lead = chan_width // 8 * 3
     edge, rest = out_weight[:, :lead], out_weight[:, lead:]
     near_all, far_rest = hop(out_weight, near), hop(rest, far)
-    far_edge, corner_edge, corner_rest = hop(edge, far), hop(near_all[:, :lead], far), hop(far_rest, near)
+    near_edge = near_all[:, :lead]
+    first, second, local, near_edge = lax.optimization_barrier((first, second, local, near_edge))
+    far_edge, corner_edge, corner_rest = hop(edge, far), hop(near_edge, far), hop(far_rest, near)
 
     mine, mine_far, theirs, theirs_far = share_blocks(flags, weight_rows, grad_out, local, first, second)
     beside = swap(mine_far, "chan", 2, 1)

time: 127 us -> 126 us (level)
  transfers between devices with their start and end apart: 14 -> 14, of which waited for: 9 -> 10; matrix products, arithmetic and copies ran while one was open for 4% -> 4% of each run, Pallas kernels for 2% -> 2%
where the time goes in v6:
time: 126 us; the launch traced here: 125 us
  waiting for transfers between devices  56.9 us (45%)
  starting transfers between devices  27.9 us (22%)
  blocking collectives  18.4 us (15%)
  Pallas kernels  14.3 us (11%)
  local copies, waits for them, and re-layouts  6.81 us (5%)
    ppermute x10, waiting for transfers between devices, swap(): return lax.ppermute(values, axis, [(i, i ^ mask) for i in range(count)])  42.5 us
    all_to_all x1, blocking collectives, per_device(): lax.all_to_all(inner, 'seq', split_axis=0, concat_axis=0, tiled=True)  18.4 us
    ppermute x10, starting transfers between devices, swap(): return lax.ppermute(values, axis, [(i, i ^ mask) for i in range(count)])  15.2 us
    all_to_all x1, waiting for transfers between devices, per_device(): lax.all_to_all(gated.reshape(seq_count, group_width, token_count), 'seq',...  10.2 us
    all_to_all x1, starting transfers between devices, per_device(): lax.all_to_all(gated.reshape(seq_count, group_width, token_count), 'seq',...  5.09 us
    pallas_call x1, Pallas kernels, correlate(): pl.pallas_call(functools.partial(correlate_kernel, blocks, step, min(16,...  5.06 us
    ppermute x1, starting transfers between devices, per_device(): lax.ppermute(local[part:], both, [(at(s, 1 - y), at(s ^ group, 1 - y)) fo...  4.5 us
    pallas_call x1, Pallas kernels, partial_mix(): pl.pallas_call(functools.partial(mix_kernel, rows, step), in_specs=[pl.Bl...  4.02 us
  transfers between devices with their start and end apart: 14, of which 10 were waited for; matrix products, arithmetic and copies ran while one was open for 4% of the time, Pallas kernels for 2%

profile of v6, /device:TPU:0, one launch (start us, length us, event | category | flops | bytes accessed | tf_op | source)
XLA Modules:
  0.0 125.3 jit_solution(12481364128711396818)
XLA Ops:
  0.7 3.0 %collective-permute-start.3 = (bf16[256,2048]{1,0:T(8,128)(2,1)}, bf16[256,2048]{1,0:T(8,128)(2,1)}, u32[]{:S(2)}, u32[]{:S(2)}) collective-permute-start(bf16[256,2048]{1,0:T(8,128)(2,1)} %refs_0_.1), channel_id=1, source_target_pairs={{0,4},{2,6},{4,0},{6,2},{8,12},{10,14},{12,8},{14,10},{16,20},{18,... | collective-permute-start | bytes 3145736 | tf_op jit(solution)/shard_map/ppermute | solution.py:521
  4.8 1.6 %collective-permute-start.9 = (bf16[256,1280]{1,0:T(8,128)(2,1)S(1)}, bf16[256,1280]{1,0:T(8,128)(2,1)S(1)}, u32[]{:S(2)}, u32[]{:S(2)}) collective-permute-start(bf16[256,1280]{1,0:T(8,128)(2,1)S(1)} %slice.25), channel_id=1, source_target_pairs={{0,8},{2,10},{4,12},{6,14},{8,0},{10,2},{12,4},{14,6},{16,24},{18,... | collective-permute-start | bytes 1966088 | tf_op jit(solution)/shard_map/ppermute | solution.py:521
  6.5 1.5 %collective-permute-start.1 = (bf16[128,2048]{1,0:T(8,128)(2,1)}, bf16[128,2048]{1,0:T(8,128)(2,1)S(1)}, u32[]{:S(2)}, u32[]{:S(2)}) collective-permute-start(bf16[128,2048]{1,0:T(8,128)(2,1)} %own_ref.1), channel_id=1, source_target_pairs={{0,1},{1,0},{2,3},{3,2},{4,5},{5,4},{6,7},{7,6},{8,9},{9,8},{10,11... | collective-permute-start | bytes 1572872 | tf_op jit(solution)/shard_map/ppermute | solution.py:521
  9.0 1.3 %collective-permute-start = (bf16[64,2048]{1,0:T(8,128)(2,1)S(1)}, bf16[64,2048]{1,0:T(8,128)(2,1)S(1)}, u32[]{:S(2)}, u32[]{:S(2)}) collective-permute-start(bf16[64,2048]{1,0:T(8,128)(2,1)S(1)} %slice.21), channel_id=1, source_target_pairs={{1,17},{3,19},{5,21},{7,23},{9,25},{11,27},{13,29},{15,31},{16,0},... | collective-permute-start | bytes 786440 | tf_op jit(solution)/shard_map/ppermute | solution.py:547
  10.3 9.5 %collective-permute-done.1.local_ref = bf16[128,2048]{1,0:T(8,128)(2,1)S(1)} collective-permute-done((bf16[128,2048]{1,0:T(8,128)(2,1)}, bf16[128,2048]{1,0:T(8,128)(2,1)S(1)}, u32[]{:S(2)}, u32[]{:S(2)}) %collective-permute-start.1) | collective-permute-done | bytes 524320 | tf_op jit(solution)/shard_map/ppermute | solution.py:521
  20.5 4.5 %collective-permute-start.2 = (bf16[64,2048]{1,0:T(8,128)(2,1)}, bf16[64,2048]{1,0:T(8,128)(2,1)S(1)}, u32[]{:S(2)}, u32[]{:S(2)}) collective-permute-start(bf16[64,2048]{1,0:T(8,128)(2,1)} %slice.28), channel_id=1, source_target_pairs={{0,16},{2,18},{4,20},{6,22},{8,24},{10,26},{12,28},{14,30},{17,1},... | collective-permute-start | bytes 786440 | tf_op jit(solution)/shard_map/ppermute | solution.py:549
  25.0 1.7 %collective-permute-done.9.refs_4_ = bf16[256,1280]{1,0:T(8,128)(2,1)S(1)} collective-permute-done((bf16[256,1280]{1,0:T(8,128)(2,1)S(1)}, bf16[256,1280]{1,0:T(8,128)(2,1)S(1)}, u32[]{:S(2)}, u32[]{:S(2)}) %collective-permute-start.9) | collective-permute-done | bytes 655392 | tf_op jit(solution)/shard_map/ppermute | solution.py:521
  29.1 2.4 %collective-permute-done.2.second_ref = bf16[64,2048]{1,0:T(8,128)(2,1)S(1)} collective-permute-done((bf16[64,2048]{1,0:T(8,128)(2,1)}, bf16[64,2048]{1,0:T(8,128)(2,1)S(1)}, u32[]{:S(2)}, u32[]{:S(2)}) %collective-permute-start.2) | collective-permute-done | bytes 262176 | tf_op jit(solution)/shard_map/ppermute | solution.py:549
  32.2 4.2 %collective-permute-start.8 = (bf16[256,768]{1,0:T(8,128)(2,1)S(1)}, bf16[256,768]{1,0:T(8,128)(2,1)S(1)}, u32[]{:S(2)}, u32[]{:S(2)}) collective-permute-start(bf16[256,768]{1,0:T(8,128)(2,1)S(1)} %slice.29), channel_id=1, source_target_pairs={{0,8},{2,10},{4,12},{6,14},{8,0},{10,2},{12,4},{14,6},{16,24},{18,... | collective-permute-start | bytes 1179656 | tf_op jit(solution)/shard_map/ppermute | solution.py:521
  36.4 1.7 %collective-permute-start.6 = (bf16[64,1024]{1,0:T(8,128)(2,1)S(1)}, bf16[64,1024]{1,0:T(8,128)(2,1)S(1)}, u32[]{:S(2)}, u32[]{:S(2)}) collective-permute-start(bf16[64,1024]{1,0:T(8,128)(2,1)S(1)} %get-tuple-element.23), channel_id=1, source_target_pairs={{0,3},{1,2},{2,1},{3,0},{4,7},{5,6},{6,5},{7,4},{8,11},{9,10},{10,... | collective-permute-start | bytes 393224 | tf_op jit(solution)/shard_map/ppermute | solution.py:561
  38.8 1.3 %collective-permute-start.4 = (bf16[64,1024]{1,0:T(8,128)(2,1)S(1)}, bf16[64,1024]{1,0:T(8,128)(2,1)S(1)}, u32[]{:S(2)}, u32[]{:S(2)}) collective-permute-start(bf16[64,1024]{1,0:T(8,128)(2,1)S(1)} %get-tuple-element.21.mine_far_ref), channel_id=1, source_target_pairs={{0,1},{1,0},{2,3},{3,2},{4,5},{5,4},{6,7},{7,6},{8,9},{9,8},{10,11... | collective-permute-start | bytes 393224 | tf_op jit(solution)/shard_map/ppermute | solution.py:521
  40.0 1.9 %collective-permute-done.6.slant_ref = bf16[64,1024]{1,0:T(8,128)(2,1)S(1)} collective-permute-done((bf16[64,1024]{1,0:T(8,128)(2,1)S(1)}, bf16[64,1024]{1,0:T(8,128)(2,1)S(1)}, u32[]{:S(2)}, u32[]{:S(2)}) %collective-permute-start.6) | collective-permute-done | bytes 131104 | tf_op jit(solution)/shard_map/ppermute | solution.py:561
  42.0 3.0 %collective-permute-done.4.beside_ref = bf16[64,1024]{1,0:T(8,128)(2,1)S(1)} collective-permute-done((bf16[64,1024]{1,0:T(8,128)(2,1)S(1)}, bf16[64,1024]{1,0:T(8,128)(2,1)S(1)}, u32[]{:S(2)}, u32[]{:S(2)}) %collective-permute-start.4) | collective-permute-done | bytes 131104 | tf_op jit(solution)/shard_map/ppermute | solution.py:521
  45.0 1.5 %collective-permute-done.8.refs_3_ = bf16[256,768]{1,0:T(8,128)(2,1)S(1)} collective-permute-done((bf16[256,768]{1,0:T(8,128)(2,1)S(1)}, bf16[256,768]{1,0:T(8,128)(2,1)S(1)}, u32[]{:S(2)}, u32[]{:S(2)}) %collective-permute-start.8) | collective-permute-done | bytes 393248 | tf_op jit(solution)/shard_map/ppermute | solution.py:521
  46.5 4.0 %partial_mix.1 = (f32[256,2048]{1,0:T(8,128)S(1)}, bf16[256,2048]{1,0:T(8,128)(2,1)S(1)}) custom-call(s32[3]{0:T(128)S(1)} %pad_add_fusion.flags_ref, bf16[128,1024]{1,0:T(8,128)(2,1)S(1)} %get-tuple-element.20.mine_ref, bf16[64,1024]{1,0:T(8,128)(2,1)S(1)} %get-tuple-element.21.mine_far_ref, bf16[64,1024]{1,0:T(8,128)(2,1)S(1)} %collective-permute-done.4.beside_ref, ...), custom_call_target="tpu_custom_call" | custom-call | flops 2147483648 | bytes 4456448 | tf_op jit(solution)/shard_map/partial_mix/pallas_call | solution.py:455
  50.6 2.6 %collective-permute-done.11.near_ref = bf16[256,2048]{1,0:T(8,128)(2,1)S(1)} collective-permute-done((bf16[256,2048]{1,0:T(8,128)(2,1)S(1)}, bf16[256,2048]{1,0:T(8,128)(2,1)S(1)}, u32[]{:S(2)}, u32[]{:S(2)}) %collective-permute-start.11) | collective-permute-done | bytes 1048608 | tf_op jit(solution)/shard_map/ppermute | solution.py:521
  53.4 3.0 %collective-permute-start.12 = (bf16[128,2048]{1,0:T(8,128)(2,1)S(1)}, bf16[128,2048]{1,0:T(8,128)(2,1)S(1)}, u32[]{:S(2)}, u32[]{:S(2)}) collective-permute-start(bf16[128,2048]{1,0:T(8,128)(2,1)S(1)} %add_convert_fusion), channel_id=1, source_target_pairs={{0,16},{2,18},{4,20},{6,22},{8,24},{10,26},{12,28},{14,30},{16,0},... | collective-permute-start | bytes 1572872 | tf_op jit(solution)/shard_map/ppermute | solution.py:521
  56.4 23.5 %collective-permute-done.12.far_ref = bf16[128,2048]{1,0:T(8,128)(2,1)S(1)} collective-permute-done((bf16[128,2048]{1,0:T(8,128)(2,1)S(1)}, bf16[128,2048]{1,0:T(8,128)(2,1)S(1)}, u32[]{:S(2)}, u32[]{:S(2)}) %collective-permute-start.12) | collective-permute-done | bytes 524320 | tf_op jit(solution)/shard_map/ppermute | solution.py:521
  79.9 1.4 %gate_mix.1 = (bf16[2048,128]{1,0:T(8,128)(2,1)}, bf16[2048,128]{1,0:T(8,128)(2,1)}) custom-call(f32[256,2048]{1,0:T(8,128)S(1)} %get-tuple-element.25.keep_ref, bf16[256,2048]{1,0:T(8,128)(2,1)S(1)} %collective-permute-done.11.near_ref, bf16[128,2048]{1,0:T(8,128)(2,1)S(1)} %collective-permute-done.12.far_ref, bf16[2048,128]{1,0:T(8,128)(2,1)S(1)} %copy-done.3, ...), custom_call_target="tpu_custom_call" | custom-call | bytes 4194304 | tf_op jit(solution)/shard_map/gate_mix/pallas_call | solution.py:487
  81.2 5.1 %all-to-all-start = ((bf16[16,128,128]{2,1,0:T(8,128)(2,1)}), bf16[16,128,128]{2,1,0:T(8,128)(2,1)S(1)}, u32[]{:S(2)}, u32[]{:S(2)}) async-start(bf16[16,128,128]{2,1,0:T(8,128)(2,1)} %bitcast.3), calls=%async_computation | async-start | bytes 1048576 | tf_op jit(solution)/shard_map/all_to_all | solution.py:571
  88.4 2.2 %filter_spectrum.1.filt_ref = f32[2712,256]{1,0:T(8,128)S(1)} custom-call(bf16[128,2048]{1,0:T(8,128)(2,1)S(1)} %copy-done.7, f32[536,256]{1,0:T(8,128)S(1)} %copy-done.2), custom_call_target="tpu_custom_call" | custom-call | tf_op jit(solution)/shard_map/filter_spectrum/pallas_call | solution.py:197
  90.6 10.2 %all-to-all-done.sig_ref = bf16[16,128,128]{2,1,0:T(8,128)(2,1)S(1)} async-done(((bf16[16,128,128]{2,1,0:T(8,128)(2,1)}), bf16[16,128,128]{2,1,0:T(8,128)(2,1)S(1)}, u32[]{:S(2)}, u32[]{:S(2)}) %all-to-all-start) | async-done | bytes 524320 | tf_op jit(solution)/shard_map/all_to_all | solution.py:571
  100.8 5.1 %correlate.1 = bf16[16,128,128]{2,1,0:T(8,128)(2,1)S(1)} custom-call(bf16[16,128,128]{2,1,0:T(8,128)(2,1)S(1)} %all-to-all-done.sig_ref, f32[2712,256]{1,0:T(8,128)S(1)} %filter_spectrum.1.filt_ref), custom_call_target="tpu_custom_call" | custom-call | tf_op jit(solution)/shard_map/correlate/pallas_call | solution.py:252
  105.9 18.4 %all_to_all.10 = bf16[16,128,128]{2,1,0:T(8,128)(2,1)S(1)} all-to-all(bf16[16,128,128]{2,1,0:T(8,128)(2,1)S(1)} %correlate.1), channel_id=1, replica_groups=mesh['seq'=16,'chan'=2] {'seq'}, dimensions={0} | all-to-all | bytes 1048576 | tf_op jit(solution)/shard_map/all_to_all | solution.py:575
  (34 shorter events, 10.0 us)
Async XLA Ops:
  0.6 26.5 %copy-start.1 = (bf16[256,2048]{1,0:T(8,128)(2,1)S(1)}, bf16[256,2048]{1,0:T(8,128)(2,1)}, u32[]{:S(2)}) copy-start(bf16[256,2048]{1,0:T(8,128)(2,1)} %refs_0_.1) | copy-start | bytes 3145732
  0.6 30.8 %copy-start = (bf16[128,2048]{1,0:T(8,128)(2,1)S(1)}, bf16[128,2048]{1,0:T(8,128)(2,1)}, u32[]{:S(2)}) copy-start(bf16[128,2048]{1,0:T(8,128)(2,1)} %own_ref.1) | copy-start | bytes 1572868
  0.7 27.4 %collective-permute-start.3 = (bf16[256,2048]{1,0:T(8,128)(2,1)}, bf16[256,2048]{1,0:T(8,128)(2,1)}, u32[]{:S(2)}, u32[]{:S(2)}) collective-permute-start(bf16[256,2048]{1,0:T(8,128)(2,1)} %refs_0_.1), channel_id=1, source_target_pairs={{0,4},{2,6},{4,0},{6,2},{8,12},{10,14},{12,8},{14,10},{16,20},{18,... | collective-permute-start | bytes 3145736 | tf_op jit(solution)/shard_map/ppermute | solution.py:521
  4.8 21.9 %collective-permute-start.9 = (bf16[256,1280]{1,0:T(8,128)(2,1)S(1)}, bf16[256,1280]{1,0:T(8,128)(2,1)S(1)}, u32[]{:S(2)}, u32[]{:S(2)}) collective-permute-start(bf16[256,1280]{1,0:T(8,128)(2,1)S(1)} %slice.25), channel_id=1, source_target_pairs={{0,8},{2,10},{4,12},{6,14},{8,0},{10,2},{12,4},{14,6},{16,24},{18,... | collective-permute-start | bytes 1966088 | tf_op jit(solution)/shard_map/ppermute | solution.py:521
  6.5 13.3 %collective-permute-start.1 = (bf16[128,2048]{1,0:T(8,128)(2,1)}, bf16[128,2048]{1,0:T(8,128)(2,1)S(1)}, u32[]{:S(2)}, u32[]{:S(2)}) collective-permute-start(bf16[128,2048]{1,0:T(8,128)(2,1)} %own_ref.1), channel_id=1, source_target_pairs={{0,1},{1,0},{2,3},{3,2},{4,5},{5,4},{6,7},{7,6},{8,9},{9,8},{10,11... | collective-permute-start | bytes 1572872 | tf_op jit(solution)/shard_map/ppermute | solution.py:521
  9.0 20.1 %collective-permute-start = (bf16[64,2048]{1,0:T(8,128)(2,1)S(1)}, bf16[64,2048]{1,0:T(8,128)(2,1)S(1)}, u32[]{:S(2)}, u32[]{:S(2)}) collective-permute-start(bf16[64,2048]{1,0:T(8,128)(2,1)S(1)} %slice.21), channel_id=1, source_target_pairs={{1,17},{3,19},{5,21},{7,23},{9,25},{11,27},{13,29},{15,31},{16,0},... | collective-permute-start | bytes 786440 | tf_op jit(solution)/shard_map/ppermute | solution.py:547
  20.5 10.9 %collective-permute-start.2 = (bf16[64,2048]{1,0:T(8,128)(2,1)}, bf16[64,2048]{1,0:T(8,128)(2,1)S(1)}, u32[]{:S(2)}, u32[]{:S(2)}) collective-permute-start(bf16[64,2048]{1,0:T(8,128)(2,1)} %slice.28), channel_id=1, source_target_pairs={{0,16},{2,18},{4,20},{6,22},{8,24},{10,26},{12,28},{14,30},{17,1},... | collective-permute-start | bytes 786440 | tf_op jit(solution)/shard_map/ppermute | solution.py:549
  26.7 18.3 %collective-permute-start.10 = (bf16[256,1280]{1,0:T(8,128)(2,1)S(1)}, bf16[256,1280]{1,0:T(8,128)(2,1)}, u32[]{:S(2)}, u32[]{:S(2)}) collective-permute-start(bf16[256,1280]{1,0:T(8,128)(2,1)S(1)} %collective-permute-done.9.refs_4_), channel_id=1, source_target_pairs={{0,4},{2,6},{4,0},{6,2},{8,12},{10,14},{12,8},{14,10},{16,20},{18,... | collective-permute-start | bytes 1966088 | tf_op jit(solution)/shard_map/ppermute | solution.py:521
  28.0 10.8 %collective-permute-start.7 = (bf16[256,768]{1,0:T(8,128)(2,1)}, bf16[256,768]{1,0:T(8,128)(2,1)}, u32[]{:S(2)}, u32[]{:S(2)}) collective-permute-start(bf16[256,768]{1,0:T(8,128)(2,1)} %slice.24), channel_id=1, source_target_pairs={{0,8},{2,10},{4,12},{6,14},{8,0},{10,2},{12,4},{14,6},{16,24},{18,... | collective-permute-start | bytes 1179656 | tf_op jit(solution)/shard_map/ppermute | solution.py:521
  32.1 12.9 %collective-permute-start.5 = (bf16[192,1024]{1,0:T(8,128)(2,1)S(1)}, bf16[192,1024]{1,0:T(8,128)(2,1)S(1)}, u32[]{:S(2)}, u32[]{:S(2)}) collective-permute-start(bf16[192,1024]{1,0:T(8,128)(2,1)S(1)} %get-tuple-element.22), channel_id=1, source_target_pairs={{0,2},{2,0},{4,6},{6,4},{8,10},{10,8},{12,14},{14,12},{16,18},{18,... | collective-permute-start | bytes 1179656 | tf_op jit(solution)/shard_map/ppermute | solution.py:521
  32.2 14.3 %collective-permute-start.8 = (bf16[256,768]{1,0:T(8,128)(2,1)S(1)}, bf16[256,768]{1,0:T(8,128)(2,1)S(1)}, u32[]{:S(2)}, u32[]{:S(2)}) collective-permute-start(bf16[256,768]{1,0:T(8,128)(2,1)S(1)} %slice.29), channel_id=1, source_target_pairs={{0,8},{2,10},{4,12},{6,14},{8,0},{10,2},{12,4},{14,6},{16,24},{18,... | collective-permute-start | bytes 1179656 | tf_op jit(solution)/shard_map/ppermute | solution.py:521
  36.4 5.6 %collective-permute-start.6 = (bf16[64,1024]{1,0:T(8,128)(2,1)S(1)}, bf16[64,1024]{1,0:T(8,128)(2,1)S(1)}, u32[]{:S(2)}, u32[]{:S(2)}) collective-permute-start(bf16[64,1024]{1,0:T(8,128)(2,1)S(1)} %get-tuple-element.23), channel_id=1, source_target_pairs={{0,3},{1,2},{2,1},{3,0},{4,7},{5,6},{6,5},{7,4},{8,11},{9,10},{10,... | collective-permute-start | bytes 393224 | tf_op jit(solution)/shard_map/ppermute | solution.py:561
  38.8 6.2 %collective-permute-start.4 = (bf16[64,1024]{1,0:T(8,128)(2,1)S(1)}, bf16[64,1024]{1,0:T(8,128)(2,1)S(1)}, u32[]{:S(2)}, u32[]{:S(2)}) collective-permute-start(bf16[64,1024]{1,0:T(8,128)(2,1)S(1)} %get-tuple-element.21.mine_far_ref), channel_id=1, source_target_pairs={{0,1},{1,0},{2,3},{3,2},{4,5},{5,4},{6,7},{7,6},{8,9},{9,8},{10,11... | collective-permute-start | bytes 393224 | tf_op jit(solution)/shard_map/ppermute | solution.py:521
  50.5 29.3 %copy-start.3 = (bf16[2048,128]{1,0:T(8,128)(2,1)S(1)}, bf16[2048,128]{1,0:T(8,128)(2,1)}, u32[]{:S(2)}) copy-start(bf16[2048,128]{1,0:T(8,128)(2,1)} %gate_ref.1) | copy-start | bytes 1572868
  50.5 29.3 %copy-start.4 = (bf16[2048,128]{1,0:T(8,128)(2,1)S(1)}, bf16[2048,128]{1,0:T(8,128)(2,1)}, u32[]{:S(2)}) copy-start(bf16[2048,128]{1,0:T(8,128)(2,1)} %conv_ref.1) | copy-start | bytes 1572868
  50.6 2.7 %collective-permute-start.11 = (bf16[256,2048]{1,0:T(8,128)(2,1)S(1)}, bf16[256,2048]{1,0:T(8,128)(2,1)S(1)}, u32[]{:S(2)}, u32[]{:S(2)}) collective-permute-start(bf16[256,2048]{1,0:T(8,128)(2,1)S(1)} %get-tuple-element.26), channel_id=1, source_target_pairs={{0,2},{2,0},{4,6},{6,4},{8,10},{10,8},{12,14},{14,12},{16,18},{18,... | collective-permute-start | bytes 3145736 | tf_op jit(solution)/shard_map/ppermute | solution.py:521
  53.4 26.5 %collective-permute-start.12 = (bf16[128,2048]{1,0:T(8,128)(2,1)S(1)}, bf16[128,2048]{1,0:T(8,128)(2,1)S(1)}, u32[]{:S(2)}, u32[]{:S(2)}) collective-permute-start(bf16[128,2048]{1,0:T(8,128)(2,1)S(1)} %add_convert_fusion), channel_id=1, source_target_pairs={{0,16},{2,18},{4,20},{6,22},{8,24},{10,26},{12,28},{14,30},{16,0},... | collective-permute-start | bytes 1572872 | tf_op jit(solution)/shard_map/ppermute | solution.py:521
  81.2 19.6 %all-to-all-start = ((bf16[16,128,128]{2,1,0:T(8,128)(2,1)}), bf16[16,128,128]{2,1,0:T(8,128)(2,1)S(1)}, u32[]{:S(2)}, u32[]{:S(2)}) async-start(bf16[16,128,128]{2,1,0:T(8,128)(2,1)} %bitcast.3), calls=%async_computation | async-start | bytes 1048576 | tf_op jit(solution)/shard_map/all_to_all | solution.py:571
  86.3 1.1 copy-start.2
  87.4 1.0 copy-start.7
  100.8 23.4 %copy-start.5 = (bf16[2048,128]{1,0:T(8,128)(2,1)S(1)}, bf16[2048,128]{1,0:T(8,128)(2,1)}, u32[]{:S(2)}) copy-start(bf16[2048,128]{1,0:T(8,128)(2,1)} %value_ref.1) | copy-start | bytes 1572868
  100.8 23.4 %copy-start.6 = (bf16[2048,128]{1,0:T(8,128)(2,1)S(1)}, bf16[2048,128]{1,0:T(8,128)(2,1)}, u32[]{:S(2)}) copy-start(bf16[2048,128]{1,0:T(8,128)(2,1)} %key_ref.1) | copy-start | bytes 1572868

commit v7 on v6

--- a/solution.py
+++ b/solution.py
@@ -119,10 +119,10 @@
 
 def wide_dot(pair, high, low):
     depth = high.shape[0]
-    return (
-        jnp.dot(pair[:, :depth], high, preferred_element_type=jnp.float32)
-        + jnp.dot(pair[:, depth:], high, preferred_element_type=jnp.float32)
-        + jnp.dot(pair[:, :depth], low, preferred_element_type=jnp.float32)
+    return jnp.dot(
+        jnp.concatenate([pair, pair[:, :depth]], axis=1),
+        jnp.concatenate([high, high, low], axis=0),
+        preferred_element_type=jnp.float32,
     )
 
 
@@ -382,26 +382,27 @@
     return (grad_gate, grad_key, grad_value)
 
 
-def share_kernel(rows, flags_ref, own_ref, local_ref, first_ref, second_ref, mine_ref, mine_far_ref, theirs_ref, theirs_far_ref):
+def share_kernel(rows, flags_ref, own_ref, low_ref, high_ref, first_ref, second_ref, mine_ref, mine_far_ref, theirs_ref, theirs_far_ref):
     home, core = flags_ref[0] == 1, flags_ref[1]
-    tokens = own_ref.shape[0]
-
-    def place(near, far):
+    tokens, part = own_ref.shape[0], low_ref.shape[0]
+
+    def place(nears, far):
         for block in range(own_ref.shape[1] // (2 * rows)):
             lanes = pl.ds(block * rows, rows)
             mine = pl.ds(pl.multiple_of((2 * block + core) * rows, rows), rows)
             theirs = pl.ds(pl.multiple_of((2 * block + 1 - core) * rows, rows), rows)
-            mine_ref[:, lanes] = near[:, mine]
+            for start, near in nears:
+                mine_ref[start : start + near.shape[0], lanes] = near[:, mine]
+                theirs_ref[start : start + near.shape[0], lanes] = near[:, theirs]
             mine_far_ref[:, lanes] = far[:, mine]
-            theirs_ref[:tokens, lanes] = near[:, theirs]
             theirs_ref[tokens:, lanes] = far[:, theirs]
             theirs_far_ref[:, lanes] = far[:, theirs]
 
-    pl.when(home)(lambda: place(own_ref, first_ref))
-    pl.when(jnp.logical_not(home))(lambda: place(local_ref, second_ref))
-
-
-def share_blocks(flags, rows, own, local, first, second):
+    pl.when(home)(lambda: place([(0, own_ref)], first_ref))
+    pl.when(jnp.logical_not(home))(lambda: place([(0, low_ref), (part, high_ref)], second_ref))
+
+
+def share_blocks(flags, rows, own, low, high, first, second):
     tokens, features = own.shape
     part = first.shape[0]
     whole = lambda a: pl.BlockSpec(a.shape, lambda: (0, 0))
@@ -410,11 +411,11 @@
     ]
     return pl.pallas_call(
         functools.partial(share_kernel, rows),
-        in_specs=[pl.BlockSpec(memory_space=pltpu.SMEM)] + [whole(a) for a in (own, local, first, second)],
+        in_specs=[pl.BlockSpec(memory_space=pltpu.SMEM)] + [whole(a) for a in (own, low, high, first, second)],
         out_shape=shapes,
         compiler_params=pltpu.CompilerParams(vmem_limit_bytes=VMEM_BYTES),
         name="share_blocks",
-    )(flags, own, local, first, second)
+    )(flags, own, low, high, first, second)
 
 
 def mix_kernel(rows, step, flags_ref, mine_ref, mine_far_ref, beside_ref, across_ref, slant_ref, *refs):
@@ -435,13 +436,14 @@
     pl.when(flags_ref[0] == 1)(lambda: place(0, part))
     pl.when(flags_ref[0] != 1)(lambda: place(part, 0))
 
-    edge = far_edge_ref.shape[1]
-    for start in range(0, own_ref.shape[1], step):
-        lanes = slice(start, start + step)
+    edge, channels = far_edge_ref.shape[1], own_ref.shape[1]
+    for start in [*range(0, edge, step), *range(edge, channels, step)]:
+        stop = min(start + step, edge if start < edge else channels)
+        lanes = slice(start, stop)
         if start < edge:
             others = (far_edge_ref[:, lanes], corner_edge_ref[:, lanes])
         else:
-            others = (far_ref[:, start - edge : start - edge + step], corner_ref[:, start - edge : start - edge + step])
+            others = (far_ref[:, start - edge : stop - edge], corner_ref[:, start - edge : stop - edge])
         weight = jnp.concatenate([own_ref[:, lanes], near_ref[:, lanes], *others], axis=0)
         total = jnp.dot(grad_ref[...], weight, preferred_element_type=jnp.float32)
         keep_ref[:, lanes] = total[: 2 * tokens]
@@ -545,17 +547,18 @@
     at = lambda s, y: s * 2 + y
     away = [(s, 1 - s // group) for s in range(seq_count)]
     first = lax.ppermute(grad_out[:part], both, [(at(s, y), at(s ^ group, y)) for s, y in away])
-    local = swap(grad_out, "chan", 2, 1)
-    second = lax.ppermute(local[part:], both, [(at(s, 1 - y), at(s ^ group, 1 - y)) for s, y in away])
-
-    lead = chan_width // 8 * 3
+    high = swap(grad_out[part:], "chan", 2, 1)
+    low = swap(grad_out[:part], "chan", 2, 1)
+    second = lax.ppermute(high, both, [(at(s, 1 - y), at(s ^ group, 1 - y)) for s, y in away])
+
+    lead = chan_width // 16 * 7
     edge, rest = out_weight[:, :lead], out_weight[:, lead:]
     near_all, far_rest = hop(out_weight, near), hop(rest, far)
     near_edge = near_all[:, :lead]
-    first, second, local, near_edge = lax.optimization_barrier((first, second, local, near_edge))
+    first, second, low, near_edge = lax.optimization_barrier((first, second, low, near_edge))
     far_edge, corner_edge, corner_rest = hop(edge, far), hop(near_edge, far), hop(far_rest, near)
 
-    mine, mine_far, theirs, theirs_far = share_blocks(flags, weight_rows, grad_out, local, first, second)
+    mine, mine_far, theirs, theirs_far = share_blocks(flags, weight_rows, grad_out, low, high, first, second)
     beside = swap(mine_far, "chan", 2, 1)
     across = hop(theirs, 1)
     slant = lax.ppermute(

time: 126 us -> 124 us (0.984)
  starting transfers between devices: 27.9 us -> 23.4 us
  waiting for transfers between devices: 56.9 us -> 60.3 us
    ppermute x10 -> x11, waiting for transfers between devices: 42.5 us -> 50 us  [swap(): return lax.ppermute(values, axis, [(i, i ^ mask) for i in range(count)])]
    ppermute x10 -> x11, starting transfers between devices: 15.2 us -> 12.4 us  [swap(): return lax.ppermute(values, axis, [(i, i ^ mask) for i in range(count)])]
    ppermute x1, waiting for transfers between devices: 2.37 us -> 0.01 us  [per_device(): lax.ppermute(high, both, [(at(s, 1 - y), at(s ^ group, 1 - y)) for s, y i...]
    ppermute x1, waiting for transfers between devices: 1.93 us -> 0.01 us  [per_device(): lax.ppermute(theirs_far, both, [(at(s, y), at(s ^ 1, 1 - y)) for s in ran...]
    all_to_all x1, starting transfers between devices: 5.09 us -> 3.57 us  [per_device(): lax.all_to_all(gated.reshape(seq_count, group_width, token_count), 'seq',...]
  transfers between devices with their start and end apart: 14 -> 15, of which waited for: 10 -> 9; matrix products, arithmetic and copies ran while one was open for 4% -> 3% of each run, Pallas kernels for 2% -> 2%
where the time goes in v7:
time: 124 us
  waiting for transfers between devices  60.3 us (49%)
  starting transfers between devices  23.4 us (19%)
  blocking collectives  18.4 us (15%)
  Pallas kernels  14.3 us (12%)
  local copies, waits for them, and re-layouts  6.18 us (5%)
    ppermute x11, waiting for transfers between devices, swap(): return lax.ppermute(values, axis, [(i, i ^ mask) for i in range(count)])  50 us
    all_to_all x1, blocking collectives, per_device(): lax.all_to_all(inner, 'seq', split_axis=0, concat_axis=0, tiled=True)  18.4 us
    ppermute x11, starting transfers between devices, swap(): return lax.ppermute(values, axis, [(i, i ^ mask) for i in range(count)])  12.4 us
    all_to_all x1, waiting for transfers between devices, per_device(): lax.all_to_all(gated.reshape(seq_count, group_width, token_count), 'seq',...  10.3 us
    pallas_call x1, Pallas kernels, correlate(): pl.pallas_call(functools.partial(correlate_kernel, blocks, step, min(16,...  4.9 us
    ppermute x1, starting transfers between devices, per_device(): lax.ppermute(high, both, [(at(s, 1 - y), at(s ^ group, 1 - y)) for s, y i...  4.5 us
    pallas_call x1, Pallas kernels, partial_mix(): pl.pallas_call(functools.partial(mix_kernel, rows, step), in_specs=[pl.Bl...  4.29 us
    all_to_all x1, starting transfers between devices, per_device(): lax.all_to_all(gated.reshape(seq_count, group_width, token_count), 'seq',...  3.57 us
  transfers between devices with their start and end apart: 15, of which 9 were waited for; matrix products, arithmetic and copies ran while one was open for 3% of the time, Pallas kernels for 2%

profile of v7, /device:TPU:0, one launch (start us, length us, event | category | flops | bytes accessed | tf_op | source)
XLA Modules:
  0.0 123.5 jit_solution(1346564431679583659)
XLA Ops:
  0.7 3.0 %collective-permute-start.4 = (bf16[256,2048]{1,0:T(8,128)(2,1)}, bf16[256,2048]{1,0:T(8,128)(2,1)}, u32[]{:S(2)}, u32[]{:S(2)}) collective-permute-start(bf16[256,2048]{1,0:T(8,128)(2,1)} %refs_0_.1), channel_id=1, source_target_pairs={{0,4},{2,6},{4,0},{6,2},{8,12},{10,14},{12,8},{14,10},{16,20},{18,... | collective-permute-start | bytes 3145736 | tf_op jit(solution)/shard_map/ppermute | solution.py:523
  4.8 1.6 %collective-permute-start.10 = (bf16[256,1152]{1,0:T(8,128)(2,1)S(1)}, bf16[256,1152]{1,0:T(8,128)(2,1)S(1)}, u32[]{:S(2)}, u32[]{:S(2)}) collective-permute-start(bf16[256,1152]{1,0:T(8,128)(2,1)S(1)} %slice.26), channel_id=1, source_target_pairs={{0,8},{2,10},{4,12},{6,14},{8,0},{10,2},{12,4},{14,6},{16,24},{18,... | collective-permute-start | bytes 1769480 | tf_op jit(solution)/shard_map/ppermute | solution.py:523
  7.5 1.6 %collective-permute-start.1 = (bf16[64,2048]{1,0:T(8,128)(2,1)S(1)}, bf16[64,2048]{1,0:T(8,128)(2,1)S(1)}, u32[]{:S(2)}, u32[]{:S(2)}) collective-permute-start(bf16[64,2048]{1,0:T(8,128)(2,1)S(1)} %get-tuple-element.31), channel_id=1, source_target_pairs={{0,1},{1,0},{2,3},{3,2},{4,5},{5,4},{6,7},{7,6},{8,9},{9,8},{10,11... | collective-permute-start | bytes 786440 | tf_op jit(solution)/shard_map/ppermute | solution.py:523
  9.6 1.3 %collective-permute-start = (bf16[64,2048]{1,0:T(8,128)(2,1)S(1)}, bf16[64,2048]{1,0:T(8,128)(2,1)S(1)}, u32[]{:S(2)}, u32[]{:S(2)}) collective-permute-start(bf16[64,2048]{1,0:T(8,128)(2,1)S(1)} %get-tuple-element.32), channel_id=1, source_target_pairs={{1,17},{3,19},{5,21},{7,23},{9,25},{11,27},{13,29},{15,31},{16,0},... | collective-permute-start | bytes 786440 | tf_op jit(solution)/shard_map/ppermute | solution.py:549
  10.9 5.9 %collective-permute-done.1.high_ref = bf16[64,2048]{1,0:T(8,128)(2,1)S(1)} collective-permute-done((bf16[64,2048]{1,0:T(8,128)(2,1)S(1)}, bf16[64,2048]{1,0:T(8,128)(2,1)S(1)}, u32[]{:S(2)}, u32[]{:S(2)}) %collective-permute-start.1) | collective-permute-done | bytes 262176 | tf_op jit(solution)/shard_map/ppermute | solution.py:523
  16.8 4.5 %collective-permute-start.2 = (bf16[64,2048]{1,0:T(8,128)(2,1)S(1)}, bf16[64,2048]{1,0:T(8,128)(2,1)S(1)}, u32[]{:S(2)}, u32[]{:S(2)}) collective-permute-start(bf16[64,2048]{1,0:T(8,128)(2,1)S(1)} %collective-permute-done.1.high_ref), channel_id=1, source_target_pairs={{0,16},{2,18},{4,20},{6,22},{8,24},{10,26},{12,28},{14,30},{17,1},... | collective-permute-start | bytes 786440 | tf_op jit(solution)/shard_map/ppermute | solution.py:552
  22.1 3.1 %collective-permute-done.10.refs_4_ = bf16[256,1152]{1,0:T(8,128)(2,1)S(1)} collective-permute-done((bf16[256,1152]{1,0:T(8,128)(2,1)S(1)}, bf16[256,1152]{1,0:T(8,128)(2,1)S(1)}, u32[]{:S(2)}, u32[]{:S(2)}) %collective-permute-start.10) | collective-permute-done | bytes 589856 | tf_op jit(solution)/shard_map/ppermute | solution.py:523
  25.3 1.9 %collective-permute-done.4.refs_1_ = bf16[256,2048]{1,0:T(8,128)(2,1)} collective-permute-done((bf16[256,2048]{1,0:T(8,128)(2,1)}, bf16[256,2048]{1,0:T(8,128)(2,1)}, u32[]{:S(2)}, u32[]{:S(2)}) %collective-permute-start.4) | collective-permute-done | bytes 1048608 | tf_op jit(solution)/shard_map/ppermute | solution.py:523
  27.1 1.7 %collective-permute-start.11 = (bf16[256,1152]{1,0:T(8,128)(2,1)S(1)}, bf16[256,1152]{1,0:T(8,128)(2,1)}, u32[]{:S(2)}, u32[]{:S(2)}) collective-permute-start(bf16[256,1152]{1,0:T(8,128)(2,1)S(1)} %collective-permute-done.10.refs_4_), channel_id=1, source_target_pairs={{0,4},{2,6},{4,0},{6,2},{8,12},{10,14},{12,8},{14,10},{16,20},{18,... | collective-permute-start | bytes 1769480 | tf_op jit(solution)/shard_map/ppermute | solution.py:523
  30.0 1.6 %collective-permute-start.9 = (bf16[256,896]{1,0:T(8,128)(2,1)S(1)}, bf16[256,896]{1,0:T(8,128)(2,1)S(1)}, u32[]{:S(2)}, u32[]{:S(2)}) collective-permute-start(bf16[256,896]{1,0:T(8,128)(2,1)S(1)} %slice.29), channel_id=1, source_target_pairs={{0,8},{2,10},{4,12},{6,14},{8,0},{10,2},{12,4},{14,6},{16,24},{18,... | collective-permute-start | bytes 1376264 | tf_op jit(solution)/shard_map/ppermute | solution.py:523
  32.4 1.6 %collective-permute-start.7 = (bf16[64,1024]{1,0:T(8,128)(2,1)S(1)}, bf16[64,1024]{1,0:T(8,128)(2,1)S(1)}, u32[]{:S(2)}, u32[]{:S(2)}) collective-permute-start(bf16[64,1024]{1,0:T(8,128)(2,1)S(1)} %get-tuple-element.23), channel_id=1, source_target_pairs={{0,3},{1,2},{2,1},{3,0},{4,7},{5,6},{6,5},{7,4},{8,11},{9,10},{10,... | collective-permute-start | bytes 393224 | tf_op jit(solution)/shard_map/ppermute | solution.py:564
  34.1 5.0 %collective-permute-done.8.refs_2_ = bf16[256,896]{1,0:T(8,128)(2,1)} collective-permute-done((bf16[256,896]{1,0:T(8,128)(2,1)}, bf16[256,896]{1,0:T(8,128)(2,1)}, u32[]{:S(2)}, u32[]{:S(2)}) %collective-permute-start.8) | collective-permute-done | bytes 458784 | tf_op jit(solution)/shard_map/ppermute | solution.py:523
  40.0 4.0 %collective-permute-done.5.beside_ref = bf16[64,1024]{1,0:T(8,128)(2,1)S(1)} collective-permute-done((bf16[64,1024]{1,0:T(8,128)(2,1)S(1)}, bf16[64,1024]{1,0:T(8,128)(2,1)S(1)}, u32[]{:S(2)}, u32[]{:S(2)}) %collective-permute-start.5) | collective-permute-done | bytes 131104 | tf_op jit(solution)/shard_map/ppermute | solution.py:523
  44.0 2.5 %collective-permute-done.9.refs_3_ = bf16[256,896]{1,0:T(8,128)(2,1)S(1)} collective-permute-done((bf16[256,896]{1,0:T(8,128)(2,1)S(1)}, bf16[256,896]{1,0:T(8,128)(2,1)S(1)}, u32[]{:S(2)}, u32[]{:S(2)}) %collective-permute-start.9) | collective-permute-done | bytes 458784 | tf_op jit(solution)/shard_map/ppermute | solution.py:523
  46.5 4.3 %partial_mix.1 = (f32[256,2048]{1,0:T(8,128)S(1)}, bf16[256,2048]{1,0:T(8,128)(2,1)S(1)}) custom-call(s32[3]{0:T(128)S(1)} %pad_add_fusion.flags_ref, bf16[128,1024]{1,0:T(8,128)(2,1)S(1)} %get-tuple-element.20.mine_ref, bf16[64,1024]{1,0:T(8,128)(2,1)S(1)} %get-tuple-element.21.mine_far_ref, bf16[64,1024]{1,0:T(8,128)(2,1)S(1)} %collective-permute-done.5.beside_ref, ...), custom_call_target="tpu_custom_call" | custom-call | flops 2147483648 | bytes 4456448 | tf_op jit(solution)/shard_map/partial_mix/pallas_call | solution.py:457
  50.9 2.6 %collective-permute-done.12.near_ref = bf16[256,2048]{1,0:T(8,128)(2,1)S(1)} collective-permute-done((bf16[256,2048]{1,0:T(8,128)(2,1)S(1)}, bf16[256,2048]{1,0:T(8,128)(2,1)S(1)}, u32[]{:S(2)}, u32[]{:S(2)}) %collective-permute-start.12) | collective-permute-done | bytes 1048608 | tf_op jit(solution)/shard_map/ppermute | solution.py:523
  53.7 1.2 collective-permute-start.13
  54.8 25.0 %collective-permute-done.13.far_ref = bf16[128,2048]{1,0:T(8,128)(2,1)S(1)} collective-permute-done((bf16[128,2048]{1,0:T(8,128)(2,1)S(1)}, bf16[128,2048]{1,0:T(8,128)(2,1)S(1)}, u32[]{:S(2)}, u32[]{:S(2)}) %collective-permute-start.13) | collective-permute-done | bytes 524320 | tf_op jit(solution)/shard_map/ppermute | solution.py:523
  79.8 1.4 %gate_mix.1 = (bf16[2048,128]{1,0:T(8,128)(2,1)}, bf16[2048,128]{1,0:T(8,128)(2,1)}) custom-call(f32[256,2048]{1,0:T(8,128)S(1)} %get-tuple-element.25.keep_ref, bf16[256,2048]{1,0:T(8,128)(2,1)S(1)} %collective-permute-done.12.near_ref, bf16[128,2048]{1,0:T(8,128)(2,1)S(1)} %collective-permute-done.13.far_ref, bf16[2048,128]{1,0:T(8,128)(2,1)S(1)} %copy-done.3, ...), custom_call_target="tpu_custom_call" | custom-call | bytes 4194304 | tf_op jit(solution)/shard_map/gate_mix/pallas_call | solution.py:489
  81.2 3.6 %all-to-all-start = ((bf16[16,128,128]{2,1,0:T(8,128)(2,1)}), bf16[16,128,128]{2,1,0:T(8,128)(2,1)S(1)}, u32[]{:S(2)}, u32[]{:S(2)}) async-start(bf16[16,128,128]{2,1,0:T(8,128)(2,1)} %bitcast.3), calls=%async_computation | async-start | bytes 1048576 | tf_op jit(solution)/shard_map/all_to_all | solution.py:574
  86.9 2.0 %filter_spectrum.1.filt_ref = f32[2712,256]{1,0:T(8,128)S(1)} custom-call(bf16[128,2048]{1,0:T(8,128)(2,1)S(1)} %copy-done.7, f32[536,256]{1,0:T(8,128)S(1)} %copy-done.2), custom_call_target="tpu_custom_call" | custom-call | tf_op jit(solution)/shard_map/filter_spectrum/pallas_call | solution.py:197
  88.9 10.3 %all-to-all-done.sig_ref = bf16[16,128,128]{2,1,0:T(8,128)(2,1)S(1)} async-done(((bf16[16,128,128]{2,1,0:T(8,128)(2,1)}), bf16[16,128,128]{2,1,0:T(8,128)(2,1)S(1)}, u32[]{:S(2)}, u32[]{:S(2)}) %all-to-all-start) | async-done | bytes 524320 | tf_op jit(solution)/shard_map/all_to_all | solution.py:574
  99.2 4.9 %correlate.1 = bf16[16,128,128]{2,1,0:T(8,128)(2,1)S(1)} custom-call(bf16[16,128,128]{2,1,0:T(8,128)(2,1)S(1)} %all-to-all-done.sig_ref, f32[2712,256]{1,0:T(8,128)S(1)} %filter_spectrum.1.filt_ref), custom_call_target="tpu_custom_call" | custom-call | tf_op jit(solution)/shard_map/correlate/pallas_call | solution.py:252
  104.1 18.4 %all_to_all.10 = bf16[16,128,128]{2,1,0:T(8,128)(2,1)S(1)} all-to-all(bf16[16,128,128]{2,1,0:T(8,128)(2,1)S(1)} %correlate.1), channel_id=1, replica_groups=mesh['seq'=16,'chan'=2] {'seq'}, dimensions={0} | all-to-all | bytes 1048576 | tf_op jit(solution)/shard_map/all_to_all | solution.py:578
  (35 shorter events, 9.7 us)
Async XLA Ops:
  0.6 20.7 %copy-start.1 = (bf16[256,2048]{1,0:T(8,128)(2,1)S(1)}, bf16[256,2048]{1,0:T(8,128)(2,1)}, u32[]{:S(2)}) copy-start(bf16[256,2048]{1,0:T(8,128)(2,1)} %refs_0_.1) | copy-start | bytes 3145732
  0.6 31.0 %copy-start = (bf16[128,2048]{1,0:T(8,128)(2,1)S(1)}, bf16[128,2048]{1,0:T(8,128)(2,1)}, u32[]{:S(2)}) copy-start(bf16[128,2048]{1,0:T(8,128)(2,1)} %own_ref.1) | copy-start | bytes 1572868
  0.7 26.5 %collective-permute-start.4 = (bf16[256,2048]{1,0:T(8,128)(2,1)}, bf16[256,2048]{1,0:T(8,128)(2,1)}, u32[]{:S(2)}, u32[]{:S(2)}) collective-permute-start(bf16[256,2048]{1,0:T(8,128)(2,1)} %refs_0_.1), channel_id=1, source_target_pairs={{0,4},{2,6},{4,0},{6,2},{8,12},{10,14},{12,8},{14,10},{16,20},{18,... | collective-permute-start | bytes 3145736 | tf_op jit(solution)/shard_map/ppermute | solution.py:523
  4.8 20.5 %collective-permute-start.10 = (bf16[256,1152]{1,0:T(8,128)(2,1)S(1)}, bf16[256,1152]{1,0:T(8,128)(2,1)S(1)}, u32[]{:S(2)}, u32[]{:S(2)}) collective-permute-start(bf16[256,1152]{1,0:T(8,128)(2,1)S(1)} %slice.26), channel_id=1, source_target_pairs={{0,8},{2,10},{4,12},{6,14},{8,0},{10,2},{12,4},{14,6},{16,24},{18,... | collective-permute-start | bytes 1769480 | tf_op jit(solution)/shard_map/ppermute | solution.py:523
  7.5 9.3 %collective-permute-start.1 = (bf16[64,2048]{1,0:T(8,128)(2,1)S(1)}, bf16[64,2048]{1,0:T(8,128)(2,1)S(1)}, u32[]{:S(2)}, u32[]{:S(2)}) collective-permute-start(bf16[64,2048]{1,0:T(8,128)(2,1)S(1)} %get-tuple-element.31), channel_id=1, source_target_pairs={{0,1},{1,0},{2,3},{3,2},{4,5},{5,4},{6,7},{7,6},{8,9},{9,8},{10,11... | collective-permute-start | bytes 786440 | tf_op jit(solution)/shard_map/ppermute | solution.py:523
  9.1 20.8 %collective-permute-start.3 = (bf16[64,2048]{1,0:T(8,128)(2,1)S(1)}, bf16[64,2048]{1,0:T(8,128)(2,1)S(1)}, u32[]{:S(2)}, u32[]{:S(2)}) collective-permute-start(bf16[64,2048]{1,0:T(8,128)(2,1)S(1)} %get-tuple-element.32), channel_id=1, source_target_pairs={{0,1},{1,0},{2,3},{3,2},{4,5},{5,4},{6,7},{7,6},{8,9},{9,8},{10,11... | collective-permute-start | bytes 786440 | tf_op jit(solution)/shard_map/ppermute | solution.py:523
  9.6 20.3 %collective-permute-start = (bf16[64,2048]{1,0:T(8,128)(2,1)S(1)}, bf16[64,2048]{1,0:T(8,128)(2,1)S(1)}, u32[]{:S(2)}, u32[]{:S(2)}) collective-permute-start(bf16[64,2048]{1,0:T(8,128)(2,1)S(1)} %get-tuple-element.32), channel_id=1, source_target_pairs={{1,17},{3,19},{5,21},{7,23},{9,25},{11,27},{13,29},{15,31},{16,0},... | collective-permute-start | bytes 786440 | tf_op jit(solution)/shard_map/ppermute | solution.py:549
  16.8 13.1 %collective-permute-start.2 = (bf16[64,2048]{1,0:T(8,128)(2,1)S(1)}, bf16[64,2048]{1,0:T(8,128)(2,1)S(1)}, u32[]{:S(2)}, u32[]{:S(2)}) collective-permute-start(bf16[64,2048]{1,0:T(8,128)(2,1)S(1)} %collective-permute-done.1.high_ref), channel_id=1, source_target_pairs={{0,16},{2,18},{4,20},{6,22},{8,24},{10,26},{12,28},{14,30},{17,1},... | collective-permute-start | bytes 786440 | tf_op jit(solution)/shard_map/ppermute | solution.py:552
  25.3 13.8 %collective-permute-start.8 = (bf16[256,896]{1,0:T(8,128)(2,1)}, bf16[256,896]{1,0:T(8,128)(2,1)}, u32[]{:S(2)}, u32[]{:S(2)}) collective-permute-start(bf16[256,896]{1,0:T(8,128)(2,1)} %slice.25), channel_id=1, source_target_pairs={{0,8},{2,10},{4,12},{6,14},{8,0},{10,2},{12,4},{14,6},{16,24},{18,... | collective-permute-start | bytes 1376264 | tf_op jit(solution)/shard_map/ppermute | solution.py:523
  27.1 16.9 %collective-permute-start.11 = (bf16[256,1152]{1,0:T(8,128)(2,1)S(1)}, bf16[256,1152]{1,0:T(8,128)(2,1)}, u32[]{:S(2)}, u32[]{:S(2)}) collective-permute-start(bf16[256,1152]{1,0:T(8,128)(2,1)S(1)} %collective-permute-done.10.refs_4_), channel_id=1, source_target_pairs={{0,4},{2,6},{4,0},{6,2},{8,12},{10,14},{12,8},{14,10},{16,20},{18,... | collective-permute-start | bytes 1769480 | tf_op jit(solution)/shard_map/ppermute | solution.py:523
  30.0 16.5 %collective-permute-start.9 = (bf16[256,896]{1,0:T(8,128)(2,1)S(1)}, bf16[256,896]{1,0:T(8,128)(2,1)S(1)}, u32[]{:S(2)}, u32[]{:S(2)}) collective-permute-start(bf16[256,896]{1,0:T(8,128)(2,1)S(1)} %slice.29), channel_id=1, source_target_pairs={{0,8},{2,10},{4,12},{6,14},{8,0},{10,2},{12,4},{14,6},{16,24},{18,... | collective-permute-start | bytes 1376264 | tf_op jit(solution)/shard_map/ppermute | solution.py:523
  32.3 11.7 %collective-permute-start.6 = (bf16[192,1024]{1,0:T(8,128)(2,1)S(1)}, bf16[192,1024]{1,0:T(8,128)(2,1)S(1)}, u32[]{:S(2)}, u32[]{:S(2)}) collective-permute-start(bf16[192,1024]{1,0:T(8,128)(2,1)S(1)} %get-tuple-element.22), channel_id=1, source_target_pairs={{0,2},{2,0},{4,6},{6,4},{8,10},{10,8},{12,14},{14,12},{16,18},{18,... | collective-permute-start | bytes 1179656 | tf_op jit(solution)/shard_map/ppermute | solution.py:523
  32.4 7.6 %collective-permute-start.7 = (bf16[64,1024]{1,0:T(8,128)(2,1)S(1)}, bf16[64,1024]{1,0:T(8,128)(2,1)S(1)}, u32[]{:S(2)}, u32[]{:S(2)}) collective-permute-start(bf16[64,1024]{1,0:T(8,128)(2,1)S(1)} %get-tuple-element.23), channel_id=1, source_target_pairs={{0,3},{1,2},{2,1},{3,0},{4,7},{5,6},{6,5},{7,4},{8,11},{9,10},{10,... | collective-permute-start | bytes 393224 | tf_op jit(solution)/shard_map/ppermute | solution.py:564
  39.0 5.0 %collective-permute-start.5 = (bf16[64,1024]{1,0:T(8,128)(2,1)S(1)}, bf16[64,1024]{1,0:T(8,128)(2,1)S(1)}, u32[]{:S(2)}, u32[]{:S(2)}) collective-permute-start(bf16[64,1024]{1,0:T(8,128)(2,1)S(1)} %get-tuple-element.21.mine_far_ref), channel_id=1, source_target_pairs={{0,1},{1,0},{2,3},{3,2},{4,5},{5,4},{6,7},{7,6},{8,9},{9,8},{10,11... | collective-permute-start | bytes 393224 | tf_op jit(solution)/shard_map/ppermute | solution.py:523
  50.8 29.0 %copy-start.3 = (bf16[2048,128]{1,0:T(8,128)(2,1)S(1)}, bf16[2048,128]{1,0:T(8,128)(2,1)}, u32[]{:S(2)}) copy-start(bf16[2048,128]{1,0:T(8,128)(2,1)} %gate_ref.1) | copy-start | bytes 1572868
  50.8 29.0 %copy-start.4 = (bf16[2048,128]{1,0:T(8,128)(2,1)S(1)}, bf16[2048,128]{1,0:T(8,128)(2,1)}, u32[]{:S(2)}) copy-start(bf16[2048,128]{1,0:T(8,128)(2,1)} %conv_ref.1) | copy-start | bytes 1572868
  50.8 2.7 %collective-permute-start.12 = (bf16[256,2048]{1,0:T(8,128)(2,1)S(1)}, bf16[256,2048]{1,0:T(8,128)(2,1)S(1)}, u32[]{:S(2)}, u32[]{:S(2)}) collective-permute-start(bf16[256,2048]{1,0:T(8,128)(2,1)S(1)} %get-tuple-element.26), channel_id=1, source_target_pairs={{0,2},{2,0},{4,6},{6,4},{8,10},{10,8},{12,14},{14,12},{16,18},{18,... | collective-permute-start | bytes 3145736 | tf_op jit(solution)/shard_map/ppermute | solution.py:523
  53.7 26.2 %collective-permute-start.13 = (bf16[128,2048]{1,0:T(8,128)(2,1)S(1)}, bf16[128,2048]{1,0:T(8,128)(2,1)S(1)}, u32[]{:S(2)}, u32[]{:S(2)}) collective-permute-start(bf16[128,2048]{1,0:T(8,128)(2,1)S(1)} %add_convert_fusion), channel_id=1, source_target_pairs={{0,16},{2,18},{4,20},{6,22},{8,24},{10,26},{12,28},{14,30},{16,0},... | collective-permute-start | bytes 1572872 | tf_op jit(solution)/shard_map/ppermute | solution.py:523
  81.2 18.0 %all-to-all-start = ((bf16[16,128,128]{2,1,0:T(8,128)(2,1)}), bf16[16,128,128]{2,1,0:T(8,128)(2,1)S(1)}, u32[]{:S(2)}, u32[]{:S(2)}) async-start(bf16[16,128,128]{2,1,0:T(8,128)(2,1)} %bitcast.3), calls=%async_computation | async-start | bytes 1048576 | tf_op jit(solution)/shard_map/all_to_all | solution.py:574
  84.8 1.1 copy-start.2
  85.8 1.0 copy-start.7
  99.2 23.3 %copy-start.5 = (bf16[2048,128]{1,0:T(8,128)(2,1)S(1)}, bf16[2048,128]{1,0:T(8,128)(2,1)}, u32[]{:S(2)}) copy-start(bf16[2048,128]{1,0:T(8,128)(2,1)} %value_ref.1) | copy-start | bytes 1572868
  99.2 23.3 %copy-start.6 = (bf16[2048,128]{1,0:T(8,128)(2,1)S(1)}, bf16[2048,128]{1,0:T(8,128)(2,1)}, u32[]{:S(2)}) copy-start(bf16[2048,128]{1,0:T(8,128)(2,1)} %key_ref.1) | copy-start | bytes 1572868

commit v8 on v7

--- a/solution.py
+++ b/solution.py
@@ -566,7 +566,7 @@
     )
     keep, send = partial_mix(
         flags, (mine, mine_far, beside, across, slant),
-        out_weight, near_all, (far_edge, far_rest), (corner_edge, corner_rest), chan_width // 8,
+        out_weight, near_all, (far_edge, far_rest), (corner_edge, corner_rest), chan_width // 4,
     )
     given = hop(send, 1)
     over = hop((keep[token_count:] + given[token_count:].astype(jnp.float32)).astype(jnp.bfloat16), group)

time: 124 us -> 124 us (level)
  no operation moved by 1% of the time
where the time goes in v8:
time: 124 us
  waiting for transfers between devices  60.3 us (49%)
  starting transfers between devices  23.4 us (19%)
  blocking collectives  18.4 us (15%)
  Pallas kernels  14.3 us (12%)
  local copies, waits for them, and re-layouts  6.18 us (5%)
    ppermute x11, waiting for transfers between devices, swap(): return lax.ppermute(values, axis, [(i, i ^ mask) for i in range(count)])  50 us
    all_to_all x1, blocking collectives, per_device(): lax.all_to_all(inner, 'seq', split_axis=0, concat_axis=0, tiled=True)  18.4 us
    ppermute x11, starting transfers between devices, swap(): return lax.ppermute(values, axis, [(i, i ^ mask) for i in range(count)])  12.4 us
    all_to_all x1, waiting for transfers between devices, per_device(): lax.all_to_all(gated.reshape(seq_count, group_width, token_count), 'seq',...  10.3 us
    pallas_call x1, Pallas kernels, correlate(): pl.pallas_call(functools.partial(correlate_kernel, blocks, step, min(16,...  4.9 us
    ppermute x1, starting transfers between devices, per_device(): lax.ppermute(high, both, [(at(s, 1 - y), at(s ^ group, 1 - y)) for s, y i...  4.5 us
    pallas_call x1, Pallas kernels, partial_mix(): pl.pallas_call(functools.partial(mix_kernel, rows, step), in_specs=[pl.Bl...  4.29 us
    all_to_all x1, starting transfers between devices, per_device(): lax.all_to_all(gated.reshape(seq_count, group_width, token_count), 'seq',...  3.57 us
  transfers between devices with their start and end apart: 15, of which 9 were waited for; matrix products, arithmetic and copies ran while one was open for 3% of the time, Pallas kernels for 2%

profile of v8, /device:TPU:0, one launch (start us, length us, event | category | flops | bytes accessed | tf_op | source)
XLA Modules:
  0.0 123.5 jit_solution(14595962615925426000)
XLA Ops:
  0.7 3.0 %collective-permute-start.4 = (bf16[256,2048]{1,0:T(8,128)(2,1)}, bf16[256,2048]{1,0:T(8,128)(2,1)}, u32[]{:S(2)}, u32[]{:S(2)}) collective-permute-start(bf16[256,2048]{1,0:T(8,128)(2,1)} %refs_0_.1), channel_id=1, source_target_pairs={{0,4},{2,6},{4,0},{6,2},{8,12},{10,14},{12,8},{14,10},{16,20},{18,... | collective-permute-start | bytes 3145736 | tf_op jit(solution)/shard_map/ppermute | solution.py:523
  4.8 1.6 %collective-permute-start.10 = (bf16[256,1152]{1,0:T(8,128)(2,1)S(1)}, bf16[256,1152]{1,0:T(8,128)(2,1)S(1)}, u32[]{:S(2)}, u32[]{:S(2)}) collective-permute-start(bf16[256,1152]{1,0:T(8,128)(2,1)S(1)} %slice.26), channel_id=1, source_target_pairs={{0,8},{2,10},{4,12},{6,14},{8,0},{10,2},{12,4},{14,6},{16,24},{18,... | collective-permute-start | bytes 1769480 | tf_op jit(solution)/shard_map/ppermute | solution.py:523
  7.5 1.6 %collective-permute-start.1 = (bf16[64,2048]{1,0:T(8,128)(2,1)S(1)}, bf16[64,2048]{1,0:T(8,128)(2,1)S(1)}, u32[]{:S(2)}, u32[]{:S(2)}) collective-permute-start(bf16[64,2048]{1,0:T(8,128)(2,1)S(1)} %get-tuple-element.31), channel_id=1, source_target_pairs={{0,1},{1,0},{2,3},{3,2},{4,5},{5,4},{6,7},{7,6},{8,9},{9,8},{10,11... | collective-permute-start | bytes 786440 | tf_op jit(solution)/shard_map/ppermute | solution.py:523
  9.6 1.3 %collective-permute-start = (bf16[64,2048]{1,0:T(8,128)(2,1)S(1)}, bf16[64,2048]{1,0:T(8,128)(2,1)S(1)}, u32[]{:S(2)}, u32[]{:S(2)}) collective-permute-start(bf16[64,2048]{1,0:T(8,128)(2,1)S(1)} %get-tuple-element.32), channel_id=1, source_target_pairs={{1,17},{3,19},{5,21},{7,23},{9,25},{11,27},{13,29},{15,31},{16,0},... | collective-permute-start | bytes 786440 | tf_op jit(solution)/shard_map/ppermute | solution.py:549
  10.9 5.9 %collective-permute-done.1.high_ref = bf16[64,2048]{1,0:T(8,128)(2,1)S(1)} collective-permute-done((bf16[64,2048]{1,0:T(8,128)(2,1)S(1)}, bf16[64,2048]{1,0:T(8,128)(2,1)S(1)}, u32[]{:S(2)}, u32[]{:S(2)}) %collective-permute-start.1) | collective-permute-done | bytes 262176 | tf_op jit(solution)/shard_map/ppermute | solution.py:523
  16.8 4.5 %collective-permute-start.2 = (bf16[64,2048]{1,0:T(8,128)(2,1)S(1)}, bf16[64,2048]{1,0:T(8,128)(2,1)S(1)}, u32[]{:S(2)}, u32[]{:S(2)}) collective-permute-start(bf16[64,2048]{1,0:T(8,128)(2,1)S(1)} %collective-permute-done.1.high_ref), channel_id=1, source_target_pairs={{0,16},{2,18},{4,20},{6,22},{8,24},{10,26},{12,28},{14,30},{17,1},... | collective-permute-start | bytes 786440 | tf_op jit(solution)/shard_map/ppermute | solution.py:552
  22.1 3.1 %collective-permute-done.10.refs_4_ = bf16[256,1152]{1,0:T(8,128)(2,1)S(1)} collective-permute-done((bf16[256,1152]{1,0:T(8,128)(2,1)S(1)}, bf16[256,1152]{1,0:T(8,128)(2,1)S(1)}, u32[]{:S(2)}, u32[]{:S(2)}) %collective-permute-start.10) | collective-permute-done | bytes 589856 | tf_op jit(solution)/shard_map/ppermute | solution.py:523
  25.3 1.9 %collective-permute-done.4.refs_1_ = bf16[256,2048]{1,0:T(8,128)(2,1)} collective-permute-done((bf16[256,2048]{1,0:T(8,128)(2,1)}, bf16[256,2048]{1,0:T(8,128)(2,1)}, u32[]{:S(2)}, u32[]{:S(2)}) %collective-permute-start.4) | collective-permute-done | bytes 1048608 | tf_op jit(solution)/shard_map/ppermute | solution.py:523
  27.1 1.7 %collective-permute-start.11 = (bf16[256,1152]{1,0:T(8,128)(2,1)S(1)}, bf16[256,1152]{1,0:T(8,128)(2,1)}, u32[]{:S(2)}, u32[]{:S(2)}) collective-permute-start(bf16[256,1152]{1,0:T(8,128)(2,1)S(1)} %collective-permute-done.10.refs_4_), channel_id=1, source_target_pairs={{0,4},{2,6},{4,0},{6,2},{8,12},{10,14},{12,8},{14,10},{16,20},{18,... | collective-permute-start | bytes 1769480 | tf_op jit(solution)/shard_map/ppermute | solution.py:523
  30.0 1.6 %collective-permute-start.9 = (bf16[256,896]{1,0:T(8,128)(2,1)S(1)}, bf16[256,896]{1,0:T(8,128)(2,1)S(1)}, u32[]{:S(2)}, u32[]{:S(2)}) collective-permute-start(bf16[256,896]{1,0:T(8,128)(2,1)S(1)} %slice.29), channel_id=1, source_target_pairs={{0,8},{2,10},{4,12},{6,14},{8,0},{10,2},{12,4},{14,6},{16,24},{18,... | collective-permute-start | bytes 1376264 | tf_op jit(solution)/shard_map/ppermute | solution.py:523
  32.4 1.6 %collective-permute-start.7 = (bf16[64,1024]{1,0:T(8,128)(2,1)S(1)}, bf16[64,1024]{1,0:T(8,128)(2,1)S(1)}, u32[]{:S(2)}, u32[]{:S(2)}) collective-permute-start(bf16[64,1024]{1,0:T(8,128)(2,1)S(1)} %get-tuple-element.23), channel_id=1, source_target_pairs={{0,3},{1,2},{2,1},{3,0},{4,7},{5,6},{6,5},{7,4},{8,11},{9,10},{10,... | collective-permute-start | bytes 393224 | tf_op jit(solution)/shard_map/ppermute | solution.py:564
  34.1 5.0 %collective-permute-done.8.refs_2_ = bf16[256,896]{1,0:T(8,128)(2,1)} collective-permute-done((bf16[256,896]{1,0:T(8,128)(2,1)}, bf16[256,896]{1,0:T(8,128)(2,1)}, u32[]{:S(2)}, u32[]{:S(2)}) %collective-permute-start.8) | collective-permute-done | bytes 458784 | tf_op jit(solution)/shard_map/ppermute | solution.py:523
  40.0 4.0 %collective-permute-done.5.beside_ref = bf16[64,1024]{1,0:T(8,128)(2,1)S(1)} collective-permute-done((bf16[64,1024]{1,0:T(8,128)(2,1)S(1)}, bf16[64,1024]{1,0:T(8,128)(2,1)S(1)}, u32[]{:S(2)}, u32[]{:S(2)}) %collective-permute-start.5) | collective-permute-done | bytes 131104 | tf_op jit(solution)/shard_map/ppermute | solution.py:523
  44.0 2.5 %collective-permute-done.9.refs_3_ = bf16[256,896]{1,0:T(8,128)(2,1)S(1)} collective-permute-done((bf16[256,896]{1,0:T(8,128)(2,1)S(1)}, bf16[256,896]{1,0:T(8,128)(2,1)S(1)}, u32[]{:S(2)}, u32[]{:S(2)}) %collective-permute-start.9) | collective-permute-done | bytes 458784 | tf_op jit(solution)/shard_map/ppermute | solution.py:523
  46.5 4.3 %partial_mix.1 = (f32[256,2048]{1,0:T(8,128)S(1)}, bf16[256,2048]{1,0:T(8,128)(2,1)S(1)}) custom-call(s32[3]{0:T(128)S(1)} %pad_add_fusion.flags_ref, bf16[128,1024]{1,0:T(8,128)(2,1)S(1)} %get-tuple-element.20.mine_ref, bf16[64,1024]{1,0:T(8,128)(2,1)S(1)} %get-tuple-element.21.mine_far_ref, bf16[64,1024]{1,0:T(8,128)(2,1)S(1)} %collective-permute-done.5.beside_ref, ...), custom_call_target="tpu_custom_call" | custom-call | flops 2147483648 | bytes 4456448 | tf_op jit(solution)/shard_map/partial_mix/pallas_call | solution.py:457
  50.9 2.6 %collective-permute-done.12.near_ref = bf16[256,2048]{1,0:T(8,128)(2,1)S(1)} collective-permute-done((bf16[256,2048]{1,0:T(8,128)(2,1)S(1)}, bf16[256,2048]{1,0:T(8,128)(2,1)S(1)}, u32[]{:S(2)}, u32[]{:S(2)}) %collective-permute-start.12) | collective-permute-done | bytes 1048608 | tf_op jit(solution)/shard_map/ppermute | solution.py:523
  53.7 1.2 collective-permute-start.13
  54.8 25.0 %collective-permute-done.13.far_ref = bf16[128,2048]{1,0:T(8,128)(2,1)S(1)} collective-permute-done((bf16[128,2048]{1,0:T(8,128)(2,1)S(1)}, bf16[128,2048]{1,0:T(8,128)(2,1)S(1)}, u32[]{:S(2)}, u32[]{:S(2)}) %collective-permute-start.13) | collective-permute-done | bytes 524320 | tf_op jit(solution)/shard_map/ppermute | solution.py:523
  79.8 1.4 %gate_mix.1 = (bf16[2048,128]{1,0:T(8,128)(2,1)}, bf16[2048,128]{1,0:T(8,128)(2,1)}) custom-call(f32[256,2048]{1,0:T(8,128)S(1)} %get-tuple-element.25.keep_ref, bf16[256,2048]{1,0:T(8,128)(2,1)S(1)} %collective-permute-done.12.near_ref, bf16[128,2048]{1,0:T(8,128)(2,1)S(1)} %collective-permute-done.13.far_ref, bf16[2048,128]{1,0:T(8,128)(2,1)S(1)} %copy-done.3, ...), custom_call_target="tpu_custom_call" | custom-call | bytes 4194304 | tf_op jit(solution)/shard_map/gate_mix/pallas_call | solution.py:489
  81.2 3.6 %all-to-all-start = ((bf16[16,128,128]{2,1,0:T(8,128)(2,1)}), bf16[16,128,128]{2,1,0:T(8,128)(2,1)S(1)}, u32[]{:S(2)}, u32[]{:S(2)}) async-start(bf16[16,128,128]{2,1,0:T(8,128)(2,1)} %bitcast.3), calls=%async_computation | async-start | bytes 1048576 | tf_op jit(solution)/shard_map/all_to_all | solution.py:574
  86.9 2.0 %filter_spectrum.1.filt_ref = f32[2712,256]{1,0:T(8,128)S(1)} custom-call(bf16[128,2048]{1,0:T(8,128)(2,1)S(1)} %copy-done.7, f32[536,256]{1,0:T(8,128)S(1)} %copy-done.2), custom_call_target="tpu_custom_call" | custom-call | tf_op jit(solution)/shard_map/filter_spectrum/pallas_call | solution.py:197
  88.9 10.3 %all-to-all-done.sig_ref = bf16[16,128,128]{2,1,0:T(8,128)(2,1)S(1)} async-done(((bf16[16,128,128]{2,1,0:T(8,128)(2,1)}), bf16[16,128,128]{2,1,0:T(8,128)(2,1)S(1)}, u32[]{:S(2)}, u32[]{:S(2)}) %all-to-all-start) | async-done | bytes 524320 | tf_op jit(solution)/shard_map/all_to_all | solution.py:574
  99.2 4.9 %correlate.1 = bf16[16,128,128]{2,1,0:T(8,128)(2,1)S(1)} custom-call(bf16[16,128,128]{2,1,0:T(8,128)(2,1)S(1)} %all-to-all-done.sig_ref, f32[2712,256]{1,0:T(8,128)S(1)} %filter_spectrum.1.filt_ref), custom_call_target="tpu_custom_call" | custom-call | tf_op jit(solution)/shard_map/correlate/pallas_call | solution.py:252
  104.1 18.4 %all_to_all.10 = bf16[16,128,128]{2,1,0:T(8,128)(2,1)S(1)} all-to-all(bf16[16,128,128]{2,1,0:T(8,128)(2,1)S(1)} %correlate.1), channel_id=1, replica_groups=mesh['seq'=16,'chan'=2] {'seq'}, dimensions={0} | all-to-all | bytes 1048576 | tf_op jit(solution)/shard_map/all_to_all | solution.py:578
  (35 shorter events, 9.7 us)
Async XLA Ops:
  0.6 20.7 %copy-start.1 = (bf16[256,2048]{1,0:T(8,128)(2,1)S(1)}, bf16[256,2048]{1,0:T(8,128)(2,1)}, u32[]{:S(2)}) copy-start(bf16[256,2048]{1,0:T(8,128)(2,1)} %refs_0_.1) | copy-start | bytes 3145732
  0.6 31.0 %copy-start = (bf16[128,2048]{1,0:T(8,128)(2,1)S(1)}, bf16[128,2048]{1,0:T(8,128)(2,1)}, u32[]{:S(2)}) copy-start(bf16[128,2048]{1,0:T(8,128)(2,1)} %own_ref.1) | copy-start | bytes 1572868
  0.7 26.5 %collective-permute-start.4 = (bf16[256,2048]{1,0:T(8,128)(2,1)}, bf16[256,2048]{1,0:T(8,128)(2,1)}, u32[]{:S(2)}, u32[]{:S(2)}) collective-permute-start(bf16[256,2048]{1,0:T(8,128)(2,1)} %refs_0_.1), channel_id=1, source_target_pairs={{0,4},{2,6},{4,0},{6,2},{8,12},{10,14},{12,8},{14,10},{16,20},{18,... | collective-permute-start | bytes 3145736 | tf_op jit(solution)/shard_map/ppermute | solution.py:523
  4.8 20.5 %collective-permute-start.10 = (bf16[256,1152]{1,0:T(8,128)(2,1)S(1)}, bf16[256,1152]{1,0:T(8,128)(2,1)S(1)}, u32[]{:S(2)}, u32[]{:S(2)}) collective-permute-start(bf16[256,1152]{1,0:T(8,128)(2,1)S(1)} %slice.26), channel_id=1, source_target_pairs={{0,8},{2,10},{4,12},{6,14},{8,0},{10,2},{12,4},{14,6},{16,24},{18,... | collective-permute-start | bytes 1769480 | tf_op jit(solution)/shard_map/ppermute | solution.py:523
  7.5 9.3 %collective-permute-start.1 = (bf16[64,2048]{1,0:T(8,128)(2,1)S(1)}, bf16[64,2048]{1,0:T(8,128)(2,1)S(1)}, u32[]{:S(2)}, u32[]{:S(2)}) collective-permute-start(bf16[64,2048]{1,0:T(8,128)(2,1)S(1)} %get-tuple-element.31), channel_id=1, source_target_pairs={{0,1},{1,0},{2,3},{3,2},{4,5},{5,4},{6,7},{7,6},{8,9},{9,8},{10,11... | collective-permute-start | bytes 786440 | tf_op jit(solution)/shard_map/ppermute | solution.py:523
  9.1 20.8 %collective-permute-start.3 = (bf16[64,2048]{1,0:T(8,128)(2,1)S(1)}, bf16[64,2048]{1,0:T(8,128)(2,1)S(1)}, u32[]{:S(2)}, u32[]{:S(2)}) collective-permute-start(bf16[64,2048]{1,0:T(8,128)(2,1)S(1)} %get-tuple-element.32), channel_id=1, source_target_pairs={{0,1},{1,0},{2,3},{3,2},{4,5},{5,4},{6,7},{7,6},{8,9},{9,8},{10,11... | collective-permute-start | bytes 786440 | tf_op jit(solution)/shard_map/ppermute | solution.py:523
  9.6 20.3 %collective-permute-start = (bf16[64,2048]{1,0:T(8,128)(2,1)S(1)}, bf16[64,2048]{1,0:T(8,128)(2,1)S(1)}, u32[]{:S(2)}, u32[]{:S(2)}) collective-permute-start(bf16[64,2048]{1,0:T(8,128)(2,1)S(1)} %get-tuple-element.32), channel_id=1, source_target_pairs={{1,17},{3,19},{5,21},{7,23},{9,25},{11,27},{13,29},{15,31},{16,0},... | collective-permute-start | bytes 786440 | tf_op jit(solution)/shard_map/ppermute | solution.py:549
  16.8 13.1 %collective-permute-start.2 = (bf16[64,2048]{1,0:T(8,128)(2,1)S(1)}, bf16[64,2048]{1,0:T(8,128)(2,1)S(1)}, u32[]{:S(2)}, u32[]{:S(2)}) collective-permute-start(bf16[64,2048]{1,0:T(8,128)(2,1)S(1)} %collective-permute-done.1.high_ref), channel_id=1, source_target_pairs={{0,16},{2,18},{4,20},{6,22},{8,24},{10,26},{12,28},{14,30},{17,1},... | collective-permute-start | bytes 786440 | tf_op jit(solution)/shard_map/ppermute | solution.py:552
  25.3 13.8 %collective-permute-start.8 = (bf16[256,896]{1,0:T(8,128)(2,1)}, bf16[256,896]{1,0:T(8,128)(2,1)}, u32[]{:S(2)}, u32[]{:S(2)}) collective-permute-start(bf16[256,896]{1,0:T(8,128)(2,1)} %slice.25), channel_id=1, source_target_pairs={{0,8},{2,10},{4,12},{6,14},{8,0},{10,2},{12,4},{14,6},{16,24},{18,... | collective-permute-start | bytes 1376264 | tf_op jit(solution)/shard_map/ppermute | solution.py:523
  27.1 16.9 %collective-permute-start.11 = (bf16[256,1152]{1,0:T(8,128)(2,1)S(1)}, bf16[256,1152]{1,0:T(8,128)(2,1)}, u32[]{:S(2)}, u32[]{:S(2)}) collective-permute-start(bf16[256,1152]{1,0:T(8,128)(2,1)S(1)} %collective-permute-done.10.refs_4_), channel_id=1, source_target_pairs={{0,4},{2,6},{4,0},{6,2},{8,12},{10,14},{12,8},{14,10},{16,20},{18,... | collective-permute-start | bytes 1769480 | tf_op jit(solution)/shard_map/ppermute | solution.py:523
  30.0 16.5 %collective-permute-start.9 = (bf16[256,896]{1,0:T(8,128)(2,1)S(1)}, bf16[256,896]{1,0:T(8,128)(2,1)S(1)}, u32[]{:S(2)}, u32[]{:S(2)}) collective-permute-start(bf16[256,896]{1,0:T(8,128)(2,1)S(1)} %slice.29), channel_id=1, source_target_pairs={{0,8},{2,10},{4,12},{6,14},{8,0},{10,2},{12,4},{14,6},{16,24},{18,... | collective-permute-start | bytes 1376264 | tf_op jit(solution)/shard_map/ppermute | solution.py:523
  32.3 11.7 %collective-permute-start.6 = (bf16[192,1024]{1,0:T(8,128)(2,1)S(1)}, bf16[192,1024]{1,0:T(8,128)(2,1)S(1)}, u32[]{:S(2)}, u32[]{:S(2)}) collective-permute-start(bf16[192,1024]{1,0:T(8,128)(2,1)S(1)} %get-tuple-element.22), channel_id=1, source_target_pairs={{0,2},{2,0},{4,6},{6,4},{8,10},{10,8},{12,14},{14,12},{16,18},{18,... | collective-permute-start | bytes 1179656 | tf_op jit(solution)/shard_map/ppermute | solution.py:523
  32.4 7.6 %collective-permute-start.7 = (bf16[64,1024]{1,0:T(8,128)(2,1)S(1)}, bf16[64,1024]{1,0:T(8,128)(2,1)S(1)}, u32[]{:S(2)}, u32[]{:S(2)}) collective-permute-start(bf16[64,1024]{1,0:T(8,128)(2,1)S(1)} %get-tuple-element.23), channel_id=1, source_target_pairs={{0,3},{1,2},{2,1},{3,0},{4,7},{5,6},{6,5},{7,4},{8,11},{9,10},{10,... | collective-permute-start | bytes 393224 | tf_op jit(solution)/shard_map/ppermute | solution.py:564
  39.0 5.0 %collective-permute-start.5 = (bf16[64,1024]{1,0:T(8,128)(2,1)S(1)}, bf16[64,1024]{1,0:T(8,128)(2,1)S(1)}, u32[]{:S(2)}, u32[]{:S(2)}) collective-permute-start(bf16[64,1024]{1,0:T(8,128)(2,1)S(1)} %get-tuple-element.21.mine_far_ref), channel_id=1, source_target_pairs={{0,1},{1,0},{2,3},{3,2},{4,5},{5,4},{6,7},{7,6},{8,9},{9,8},{10,11... | collective-permute-start | bytes 393224 | tf_op jit(solution)/shard_map/ppermute | solution.py:523
  50.8 29.0 %copy-start.3 = (bf16[2048,128]{1,0:T(8,128)(2,1)S(1)}, bf16[2048,128]{1,0:T(8,128)(2,1)}, u32[]{:S(2)}) copy-start(bf16[2048,128]{1,0:T(8,128)(2,1)} %gate_ref.1) | copy-start | bytes 1572868
  50.8 29.0 %copy-start.4 = (bf16[2048,128]{1,0:T(8,128)(2,1)S(1)}, bf16[2048,128]{1,0:T(8,128)(2,1)}, u32[]{:S(2)}) copy-start(bf16[2048,128]{1,0:T(8,128)(2,1)} %conv_ref.1) | copy-start | bytes 1572868
  50.8 2.7 %collective-permute-start.12 = (bf16[256,2048]{1,0:T(8,128)(2,1)S(1)}, bf16[256,2048]{1,0:T(8,128)(2,1)S(1)}, u32[]{:S(2)}, u32[]{:S(2)}) collective-permute-start(bf16[256,2048]{1,0:T(8,128)(2,1)S(1)} %get-tuple-element.26), channel_id=1, source_target_pairs={{0,2},{2,0},{4,6},{6,4},{8,10},{10,8},{12,14},{14,12},{16,18},{18,... | collective-permute-start | bytes 3145736 | tf_op jit(solution)/shard_map/ppermute | solution.py:523
  53.7 26.2 %collective-permute-start.13 = (bf16[128,2048]{1,0:T(8,128)(2,1)S(1)}, bf16[128,2048]{1,0:T(8,128)(2,1)S(1)}, u32[]{:S(2)}, u32[]{:S(2)}) collective-permute-start(bf16[128,2048]{1,0:T(8,128)(2,1)S(1)} %add_convert_fusion), channel_id=1, source_target_pairs={{0,16},{2,18},{4,20},{6,22},{8,24},{10,26},{12,28},{14,30},{16,0},... | collective-permute-start | bytes 1572872 | tf_op jit(solution)/shard_map/ppermute | solution.py:523
  81.2 18.0 %all-to-all-start = ((bf16[16,128,128]{2,1,0:T(8,128)(2,1)}), bf16[16,128,128]{2,1,0:T(8,128)(2,1)S(1)}, u32[]{:S(2)}, u32[]{:S(2)}) async-start(bf16[16,128,128]{2,1,0:T(8,128)(2,1)} %bitcast.3), calls=%async_computation | async-start | bytes 1048576 | tf_op jit(solution)/shard_map/all_to_all | solution.py:574
  84.8 1.1 copy-start.2
  85.8 1.0 copy-start.7
  99.2 23.3 %copy-start.5 = (bf16[2048,128]{1,0:T(8,128)(2,1)S(1)}, bf16[2048,128]{1,0:T(8,128)(2,1)}, u32[]{:S(2)}) copy-start(bf16[2048,128]{1,0:T(8,128)(2,1)} %value_ref.1) | copy-start | bytes 1572868
  99.2 23.3 %copy-start.6 = (bf16[2048,128]{1,0:T(8,128)(2,1)S(1)}, bf16[2048,128]{1,0:T(8,128)(2,1)}, u32[]{:S(2)}) copy-start(bf16[2048,128]{1,0:T(8,128)(2,1)} %key_ref.1) | copy-start | bytes 1572868
